TPU v7x, 128 devices: a whole 4x4x4 slice. The times are simulated.
128 devices in a mesh: gx: 8 (over x_lo, y), gy: 16 (over x_hi, z, core).
Axes of the slice: x: 4 (x_hi: 2, x_lo: 2; x = x_hi * 2 + x_lo), y: 4, z: 4, core: 2. Of those that a mesh axis runs over, the one named last changes fastest.
Arguments:
- velocity: float32 [80, 160, 64], P('gy', None, 'gx'), may hold values from 1.5 to 4.5
- forward_now: float32 [320, 640, 256], P('gx', 'gy'), may hold values from -6 to 6
- forward_before: float32 [320, 640, 256], P('gx', 'gy'), may hold values from -6 to 6
- adjoint_now: float32 [320, 640, 256], P('gx', 'gy'), may hold values from -6 to 6
- adjoint_after: float32 [320, 640, 256], P('gx', 'gy'), may hold values from -6 to 6
- source_cells: int32 [3, 4], replicated, may hold values from 0 to 639, as said below
- receiver_cells: int32 [3, 1024], replicated, may hold values from 0 to 639, as said below
- wavelet: float32 [4, 4], replicated, may hold values from -24 to 24
- observed: float32 [4, 1024], replicated, may hold values from -24 to 24
Outputs:
- gradient: float32 [80, 160, 64], P('gy', None, 'gx')
Inputs may be any that keep to these rules, and one draw needn't show every extreme that they name: `source_cells`: row 0 holds x cells of 0 to 319, row 1 y cells of 0 to 639, row 2 z cells of 0 to 255; the first source sits at the cell (319, 639, 255) and the second at (0, 0, 0); cells may repeat. `receiver_cells`: row 0 holds x cells of 0 to 319, row 1 y cells of 0 to 639, row 2 z cells of 0 to 255; the first receiver sits at the cell (319, 639, 255) and the second at (0, 0, 0); cells may repeat.
All inputs are finite; a program needn't handle non-finite values.
Results may differ from a plain program's by a relative error of at most 0.0003.
Values sent between devices are 32-bit elements; how exact they have to be, the bound alone decides.
No kernel may reach another device: no remote copies, remote signals or barrier semaphores. Data moves between devices by JAX's collectives and lax.ppermute only.
A program may use at most 128 MiB of HBM per device.

v0:
```python
import jax
import jax.numpy as jnp
from jax import lax
from jax.sharding import PartitionSpec as P

ITERS = 4


COEFFS = (-205.0 / 72.0, 8.0 / 5.0, -1.0 / 5.0, 8.0 / 315.0, -1.0 / 560.0)


def padded_2(block, sides, width):
    for axis, dim in sides:
        count = lax.axis_size(axis)
        forward = [(i, i + 1) for i in range(count - 1)]
        backward = [(target, source) for source, target in forward]
        low = lax.ppermute(
            lax.slice_in_dim(block, block.shape[dim] - width, None, axis=dim), axis, forward
        )
        high = lax.ppermute(lax.slice_in_dim(block, 0, width, axis=dim), axis, backward)
        block = jnp.concatenate([low, block, high], axis=dim)
    return block


def weights(fine_count, coarse):
    position = jnp.arange(fine_count, dtype=jnp.int32)
    lower = position // 4
    higher = jnp.minimum(lower + 1, coarse - 1)
    fraction = (position % 4).astype(jnp.float32) * 0.25
    column = jnp.arange(coarse, dtype=jnp.int32)
    first = jnp.where(column[None, :] == lower[:, None], 1.0 - fraction[:, None], 0.0)
    second = jnp.where(column[None, :] == higher[:, None], fraction[:, None], 0.0)
    return first + second


def laplacian(padded):
    span_x = padded.shape[0] - 8
    span_y = padded.shape[1] - 8
    span_z = padded.shape[2] - 8

    def shifted(move_x, move_y, move_z):
        return padded[
            4 + move_x : 4 + move_x + span_x,
            4 + move_y : 4 + move_y + span_y,
            4 + move_z : 4 + move_z + span_z,
        ]

    result_sum = 3.0 * COEFFS[0] * shifted(0, 0, 0)
    for reach in range(1, 5):
        pairs = (
            shifted(reach, 0, 0)
            + shifted(-reach, 0, 0)
            + shifted(0, reach, 0)
            + shifted(0, -reach, 0)
        )
        pairs = pairs + shifted(0, 0, reach) + shifted(0, 0, -reach)
        result_sum = result_sum + COEFFS[reach] * pairs
    return result_sum


def stencil(field):
    padded = padded_2(field, (("gx", 0), ("gy", 1)), 4)
    padded = jnp.pad(padded, ((0, 0), (0, 0), (4, 4)))
    return laplacian(padded)


def locate(cells, base_x, base_y, cells_x, cells_y, cells_z):
    local_x = cells[0] - base_x
    local_y = cells[1] - base_y
    inside = (local_x >= 0) & (local_x < cells_x) & (local_y >= 0) & (local_y < cells_y)
    flat_index = (
        jnp.clip(local_x, 0, cells_x - 1) * cells_y + jnp.clip(local_y, 0, cells_y - 1)
    ) * cells_z + cells[2]
    return (flat_index, inside.astype(jnp.float32))


def per_device(
    velocity,
    forward_now,
    forward_before,
    adjoint_now,
    adjoint_after,
    source_cells,
    receiver_cells,
    wavelet,
    observed,
):
    exact = lax.Precision.HIGHEST
    count_y = lax.axis_size("gy")
    index_x = lax.axis_index("gx")
    index_y = lax.axis_index("gy")
    cells_x, cells_y, cells_z = forward_now.shape
    block_x = cells_x // 4
    block_y = cells_y // 4
    deep_model = lax.all_gather(velocity, "gx", axis=2, tiled=True)
    rows_x = deep_model.shape[0]
    coarse_y = deep_model.shape[1]
    coarse_z = deep_model.shape[2]
    coarse_x = rows_x * count_y
    offsets = jnp.arange(block_y + 1, dtype=jnp.int32)
    starts = jnp.arange(count_y, dtype=jnp.int32) * block_y
    take_all = jnp.minimum(starts[:, None] + offsets[None, :], coarse_y - 1).reshape(-1)
    whole_model = lax.all_gather(deep_model, "gy", axis=0, tiled=True)
    take_y = jnp.minimum(index_y * block_y + offsets, coarse_y - 1)
    near_model = jnp.take(whole_model, take_y, axis=1)
    take_x = jnp.minimum(index_x * block_x + jnp.arange(block_x + 1, dtype=jnp.int32), coarse_x - 1)
    local_model = jnp.take(near_model, take_x, axis=0)
    weight_x = weights(cells_x, block_x + 1)
    weight_y = weights(cells_y, block_y + 1)
    weight_z = weights(cells_z, coarse_z)
    fine_speed = jnp.einsum("abc,zc->abz", local_model, weight_z, precision=exact)
    fine_speed = jnp.einsum("abz,yb->ayz", fine_speed, weight_y, precision=exact)
    fine_speed = jnp.einsum("ayz,xa->xyz", fine_speed, weight_x, precision=exact)
    courant = fine_speed * fine_speed * 0.01
    base_x = index_x * cells_x
    base_y = index_y * cells_y
    source_flat, source_in = locate(source_cells, base_x, base_y, cells_x, cells_y, cells_z)
    receiver_flat, receiver_in = locate(receiver_cells, base_x, base_y, cells_x, cells_y, cells_z)
    image_sum = jnp.zeros_like(forward_now)
    before, field_now = (forward_before, forward_now)
    accel_list = []
    residual_list = []
    for section in range(ITERS):
        accel = courant * stencil(field_now)
        accel = (
            accel.reshape(-1)
            .at[source_flat]
            .add(wavelet[section] * source_in)
            .reshape(field_now.shape)
        )
        field_after = 2.0 * field_now - before + accel
        sampled = field_after.reshape(-1)[receiver_flat]
        residual_list.append((sampled - observed[section]) * receiver_in)
        accel_list.append(accel)
        before, field_now = (field_now, field_after)
    field_later, field_now = (adjoint_after, adjoint_now)
    for section in reversed(range(ITERS)):
        change = stencil(courant * field_now)
        change = (
            change.reshape(-1)
            .at[receiver_flat]
            .add(residual_list[section])
            .reshape(field_now.shape)
        )
        earlier = 2.0 * field_now - field_later + change
        image_sum = image_sum + earlier * accel_list[section]
        field_later, field_now = (field_now, earlier)
    image_sum = image_sum * 2.0 / fine_speed
    coarse_part = jnp.einsum("xyz,xa->ayz", image_sum, weight_x, precision=exact)
    coarse_part = jnp.einsum("ayz,yb->abz", coarse_part, weight_y, precision=exact)
    coarse_part = jnp.einsum("abz,zc->abc", coarse_part, weight_z, precision=exact) * 0.125
    spread_x = jnp.zeros((coarse_x, block_y + 1, coarse_z), jnp.float32).at[take_x].add(coarse_part)
    summed = lax.psum_scatter(spread_x, "gx", scatter_dimension=2, tiled=True)
    depth_share = summed.shape[2]
    returned = lax.all_to_all(
        summed.reshape(coarse_x, 1, block_y + 1, depth_share),
        "gy",
        split_axis=0,
        concat_axis=1,
        tiled=True,
    )
    gathered_rows = returned.reshape(rows_x, count_y * (block_y + 1), depth_share)
    result_grid = (
        jnp.zeros((rows_x, coarse_y, depth_share), jnp.float32).at[:, take_all].add(gathered_rows)
    )
    return result_grid


def solution(mesh):
    return jax.shard_map(
        per_device,
        mesh=mesh,
        in_specs=(
            P("gy", None, "gx"),
            P("gx", "gy", None),
            P("gx", "gy", None),
            P("gx", "gy", None),
            P("gx", "gy", None),
            P(),
            P(),
            P(),
            P(),
        ),
        out_specs=P("gy", None, "gx"),
        check_vma=False,
    )
```

profile of v0, /device:TPU:1, one launch (start us, length us, event | category | flops | bytes accessed | tf_op | source)
XLA Modules:
  0.0 810.3 jit_solution(2117044680546764999)
XLA Ops:
  6.5 25.7 %all_gather.6 = f32[5,160,64]{1,2,0:T(8,128)} all-gather(f32[5,160,8]{1,2,0:T(8,128)} %param.9), channel_id=1, replica_groups=mesh['gx'=8,'gy'=16] {'gx'}, dimensions={2}, use_global_device_ids=true | all-gather | bytes 230400 | tf_op jit(solution)/shard_map/all_gather | solution.py:95
  43.2 10.1 %collective-permute-start.6 = (f32[48,4,256]{2,0,1:T(8,128)S(1)}, f32[48,4,256]{2,0,1:T(8,128)S(1)}, u32[]{:S(2)}, u32[]{:S(2)}) collective-permute-start(f32[48,4,256]{2,0,1:T(8,128)S(1)} %get-tuple-element.36), channel_id=1, source_target_pairs={{1,0},{2,1},{3,2},{4,3},{5,4},{6,5},{7,6},{8,7},{9,8},{10,9},{11,1... | collective-permute-start | bytes 589832 | tf_op jit(solution)/shard_map/ppermute | solution.py:20
  67.7 35.2 %all-gather.2.cloned.1.call-done = f32[80,160,64]{1,2,0:T(8,128)} async-done(((f32[5,160,64]{1,2,0:T(8,128)}), f32[80,160,64]{1,2,0:T(8,128)}) %all-gather.2.cloned.1.call-update) | async-done | bytes 3276816 | tf_op jit(solution)/shard_map/all_gather | solution.py:103
  102.9 7.3 copy.110
  119.9 23.8 %fusion.181 = f32[40,40,256]{2,0,1:T(8,128)} fusion(f32[40,40,256]{2,0,1:T(8,128)S(1)} %get-tuple-element.54, f32[4,40,256]{2,0,1:T(4,128)S(1)} %collective-permute-done.5, f32[48,48,264]{2,0,1:T(8,128)} %select_maximum_fusion.24, f32[48,44,256]{2,0,1:T(8,128)} %get-tuple-element.34, f32[48,44,256]{2,0,1:T(8,128)} %get-tuple-element.33, ...), kind=kLoop, calls=%fused_computation.337 | loop fusion | flops 14745600 | bytes 37847040 | tf_op jit(solution)/shard_map/mul | solution.py:124
  170.6 5.4 collective-permute-start.1
  183.0 18.8 %fusion.152 = f32[40,40,256]{2,0,1:T(8,128)} fusion(f32[40,40,256]{2,0,1:T(8,128)S(1)} %fusion.246, f32[4,40,256]{2,0,1:T(4,128)} %copy-done.18, f32[4,40,256]{2,0,1:T(4,128)} %copy-done.17, f32[48,48,264]{2,0,1:T(8,128)} %select_maximum_fusion.20, f32[48,44,256]{2,0,1:T(8,128)} %get-tuple-element.30, f32[48,44,256]{2,0,1:T(8,128)} %get-tuple-element.29, ...), kind=kLoop, calls=%fused_computation.308 | loop fusion | flops 16384000 | bytes 31457280 | tf_op jit(solution)/shard_map/mul | solution.py:124
  227.9 37.3 %gather_fusion.5 = f32[1024]{0:T(1024)S(1)} fusion(f32[409600]{0:T(1024)} %bitcast.86, s32[1024]{0:T(1024)S(1)} %get-tuple-element.73), kind=kCustom, calls=%fused_computation.5 | custom fusion | bytes 12288 | tf_op jit(solution)/shard_map/gather | solution.py:132
  272.3 5.5 select_maximum_fusion.28
  281.5 5.4 select_maximum_fusion.16
  286.9 19.5 %fusion.123 = f32[40,40,256]{2,0,1:T(8,128)} fusion(f32[40,40,256]{2,0,1:T(8,128)S(1)} %subtract_add_fusion.2, f32[4,40,256]{2,0,1:T(4,128)} %collective-permute-done.13, f32[4,40,256]{2,0,1:T(4,128)} %collective-permute-done.12, f32[48,48,264]{2,0,1:T(8,128)} %select_maximum_fusion.16, f32[48,44,256]{2,0,1:T(8,128)} %get-tuple-element.26, ...), kind=kLoop, calls=%fused_computation.279 | loop fusion | flops 16384000 | bytes 31457280 | tf_op jit(solution)/shard_map/mul | solution.py:124
  335.1 24.1 %fusion.206 = f32[40,40,256]{2,0,1:T(8,128)} fusion(f32[40,40,256]{2,0,1:T(8,128)} %get-tuple-element.70, f32[4,40,256]{2,0,1:T(4,128)} %collective-permute-done.1, f32[4,40,256]{2,0,1:T(4,128)S(1)} %collective-permute-done, f32[48,48,264]{2,0,1:T(8,128)} %select_maximum_fusion.28, f32[48,44,256]{2,0,1:T(8,128)} %get-tuple-element.38, ...), kind=kLoop, calls=%fused_computation.362 | loop fusion | flops 15155200 | bytes 29818880 | tf_op jit(solution)/shard_map/add | solution.py:57
  361.8 37.1 %gather_fusion.4 = f32[1024]{0:T(1024)S(1)} fusion(f32[409600]{0:T(1024)} %bitcast.88, s32[1024]{0:T(1024)S(1)} %get-tuple-element.73), kind=kCustom, calls=%fused_computation.4 | custom fusion | bytes 12288 | tf_op jit(solution)/shard_map/gather | solution.py:132
  405.4 37.1 %gather_fusion.3 = f32[1024]{0:T(1024)S(1)} fusion(f32[409600]{0:T(1024)} %bitcast.89, s32[1024]{0:T(1024)S(1)} %get-tuple-element.73), kind=kCustom, calls=%fused_computation.3 | custom fusion | bytes 12288 | tf_op jit(solution)/shard_map/gather | solution.py:132
  447.5 5.3 select_maximum_fusion.12
  452.8 24.9 %fusion.94 = f32[40,40,256]{2,0,1:T(8,128)} fusion(f32[40,40,256]{2,0,1:T(8,128)} %copy-done.2, f32[4,40,256]{2,0,1:T(4,128)} %copy-done.15, f32[4,40,256]{2,0,1:T(4,128)S(1)} %copy-done.14, f32[48,48,264]{2,0,1:T(8,128)} %select_maximum_fusion.12, f32[48,44,256]{2,0,1:T(8,128)} %get-tuple-element.22, f32[48,44,256]{2,0,1:T(8,128)} %get-tuple-element.21, ...), kind=kLoop, calls=%fused_computation.250 | loop fusion | flops 16384000 | bytes 31457280 | tf_op jit(solution)/shard_map/mul | solution.py:124
  492.9 37.1 %gather_fusion.2 = f32[1024]{0:T(1024)S(1)} fusion(f32[409600]{0:T(1024)} %bitcast.87, s32[1024]{0:T(1024)S(1)} %get-tuple-element.73), kind=kCustom, calls=%fused_computation.2 | custom fusion | bytes 12288 | tf_op jit(solution)/shard_map/gather | solution.py:132
  530.0 7.0 scatter_fusion.4
  538.6 5.4 fusion.259
  551.6 9.1 %collective-permute-start.22 = (f32[48,4,256]{2,0,1:T(8,128)S(1)}, f32[48,4,256]{2,0,1:T(8,128)S(1)}, u32[]{:S(2)}, u32[]{:S(2)}) collective-permute-start(f32[48,4,256]{2,0,1:T(8,128)S(1)} %get-tuple-element.20), channel_id=1, source_target_pairs={{1,0},{2,1},{3,2},{4,3},{5,4},{6,5},{7,6},{8,7},{9,8},{10,9},{11,1... | collective-permute-start | bytes 589832 | tf_op jit(solution)/shard_map/ppermute | solution.py:20
  572.3 18.5 %fusion.65 = f32[40,40,256]{2,0,1:T(8,128)} fusion(f32[40,40,256]{2,0,1:T(8,128)S(1)} %get-tuple-element.5, f32[4,40,256]{2,0,1:T(4,128)} %copy-done.10, f32[4,40,256]{2,0,1:T(4,128)S(1)} %collective-permute-done.20, f32[48,48,264]{2,0,1:T(8,128)} %select_maximum_fusion.8, f32[48,44,256]{2,0,1:T(8,128)} %get-tuple-element.18, ...), kind=kLoop, calls=%fused_computation.221 | loop fusion | flops 15155200 | bytes 29818880 | tf_op jit(solution)/shard_map/add | solution.py:57
  593.7 7.0 scatter_fusion.5
  630.9 19.8 %fusion.37 = f32[40,40,256]{2,0,1:T(8,128)} fusion(f32[40,40,256]{2,0,1:T(8,128)S(1)} %fusion.258, f32[4,40,256]{2,0,1:T(4,128)} %copy-done.11, f32[4,40,256]{2,0,1:T(4,128)S(1)} %collective-permute-done.24, f32[48,48,264]{2,0,1:T(8,128)} %select_maximum_fusion.4, f32[48,44,256]{2,0,1:T(8,128)} %get-tuple-element.14, f32[48,44,256]{2,0,1:T(8,128)} %get-tuple-element.13), kind=kLoop, calls=%fused_computation.193 | loop fusion | flops 15155200 | bytes 29818880 | tf_op jit(solution)/shard_map/add | solution.py:57
  653.5 7.0 scatter_fusion.6
  676.8 5.4 collective-permute-start.31
  691.6 19.1 %fusion.9 = f32[40,40,256]{2,0,1:T(8,128)} fusion(f32[40,40,256]{2,0,1:T(8,128)S(1)} %fusion.254, f32[4,40,256]{2,0,1:T(4,128)} %copy-done.12, f32[4,40,256]{2,0,1:T(4,128)S(1)} %collective-permute-done.28, f32[48,48,264]{2,0,1:T(8,128)} %select_maximum_fusion, f32[48,44,256]{2,0,1:T(8,128)} %get-tuple-element.10, f32[48,44,256]{2,0,1:T(8,128)} %get-tuple-element.9), kind=kLoop, calls=%fused_computation.165 | loop fusion | flops 15155200 | bytes 29818880 | tf_op jit(solution)/shard_map/add | solution.py:57
  714.7 9.0 %scatter_fusion.7 = f32[409600]{0:T(1024)} fusion(f32[409600]{0:T(1024)} %bitcast.46, s32[1024]{0:T(1024)S(1)} %bitcast.113, f32[1024]{0:T(1024)S(1)} %get-tuple-element.66), kind=kCustom, calls=%fused_computation.13 | custom fusion | flops 1024 | bytes 16384 | tf_op jit(solution)/shard_map/scatter-add | solution.py:142
  726.7 8.3 %fusion.247 = f32[11,40,256]{2,0,1:T(8,128)S(1)} fusion(f32[40,40,256]{2,0,1:T(8,128)S(1)} %get-tuple-element.71, f32[40,40,256]{2,1,0:T(8,128)} %reshape.399, f32[40,40,256]{2,0,1:T(8,128)} %get-tuple-element.6, f32[40,40,256]{2,1,0:T(8,128)} %reshape.388, f32[40,40,256]{2,1,0:T(8,128)} %reshape.386, f32[40,40,256]{2,1,0:T(8,128)} %reshape.384, ...), kind=kOutput, calls=%fused_computation.460 | convolution fusion | flops 61442200 | bytes 16835200 | tf_op jit(solution)/shard_map/xyz,xa->ayz/dot_general | solution.py:149
  738.3 33.9 %reduce-scatter.2.cloned.1.call-done = f32[80,11,8]{0,1,2:T(8,128)} async-done(((f32[80,11,64]{0,1,2:T(8,128)}), f32[80,11,8]{0,1,2:T(8,128)}) %reduce-scatter.2.cloned.1.call-update) | async-done | bytes 28176 | tf_op jit(solution)/shard_map/reduce_scatter | solution.py:153
  774.2 12.3 %all-to-all-start = ((f32[16,1,440]{2,1,0:T(1,128)}), f32[16,1,440]{2,1,0:T(1,128)S(1)}, u32[]{:S(2)}, u32[]{:S(2)}) async-start(f32[16,1,440]{2,1,0:T(1,128)} %reshape.549), calls=%async_computation.1 | async-start | bytes 65536 | tf_op jit(solution)/shard_map/all_to_all | solution.py:155
  786.5 7.3 all-to-all-done
  795.8 6.6 scatter_fusion.9
  (262 shorter events, 260.1 us)
Async XLA Ops:
  6.5 96.4 %all-gather.2.cloned.1.call-start = ((), (), s32[]{:S(2)}) async-start(), calls=%async_computation.2 | async-start | bytes 5570560 | tf_op jit(solution)/shard_map/all_gather | solution.py:103
  32.3 739.9 %reduce-scatter.2.cloned.1.call-start = ((), (), s32[]{:S(2)}) async-start(), calls=%async_computation.3 | async-start | bytes 589824 | tf_op jit(solution)/shard_map/reduce_scatter | solution.py:153
  36.9 6.2 collective-permute-start.5
  43.2 15.4 %collective-permute-start.6 = (f32[48,4,256]{2,0,1:T(8,128)S(1)}, f32[48,4,256]{2,0,1:T(8,128)S(1)}, u32[]{:S(2)}, u32[]{:S(2)}) collective-permute-start(f32[48,4,256]{2,0,1:T(8,128)S(1)} %get-tuple-element.36), channel_id=1, source_target_pairs={{1,0},{2,1},{3,2},{4,3},{5,4},{6,5},{7,6},{8,7},{9,8},{10,9},{11,1... | collective-permute-start | bytes 589832 | tf_op jit(solution)/shard_map/ppermute | solution.py:20
  53.3 7.4 collective-permute-start.7
  153.5 7.4 collective-permute-start.8
  154.8 7.0 collective-permute-start.9
  161.9 14.1 %collective-permute-start.10 = (f32[48,4,256]{2,0,1:T(8,128)S(1)}, f32[48,4,256]{2,0,1:T(8,128)S(1)}, u32[]{:S(2)}, u32[]{:S(2)}) collective-permute-start(f32[48,4,256]{2,0,1:T(8,128)S(1)} %get-tuple-element.32), channel_id=1, source_target_pairs={{1,0},{2,1},{3,2},{4,3},{5,4},{6,5},{7,6},{8,7},{9,8},{10,9},{11,1... | collective-permute-start | bytes 589832 | tf_op jit(solution)/shard_map/ppermute | solution.py:20
  165.2 10.8 %collective-permute-start.11 = (f32[48,4,256]{2,0,1:T(8,128)S(1)}, f32[48,4,256]{2,0,1:T(8,128)S(1)}, u32[]{:S(2)}, u32[]{:S(2)}) collective-permute-start(f32[48,4,256]{2,0,1:T(8,128)S(1)} %get-tuple-element.31), channel_id=1, source_target_pairs={{0,1},{1,2},{2,3},{3,4},{4,5},{5,6},{6,7},{7,8},{8,9},{9,10},{10,1... | collective-permute-start | bytes 589832 | tf_op jit(solution)/shard_map/ppermute | solution.py:17
  169.3 48.6 %collective-permute-start = (f32[4,40,256]{2,0,1:T(4,128)}, f32[4,40,256]{2,0,1:T(4,128)S(1)}, u32[]{:S(2)}, u32[]{:S(2)}) collective-permute-start(f32[4,40,256]{2,0,1:T(4,128)} %get-tuple-element.57), channel_id=1, source_target_pairs={{16,0},{32,16},{48,32},{64,48},{80,64},{96,80},{112,96},{17,1},{33... | collective-permute-start | bytes 491528 | tf_op jit(solution)/shard_map/ppermute | solution.py:20
  170.6 47.3 %collective-permute-start.1 = (f32[4,40,256]{2,0,1:T(4,128)}, f32[4,40,256]{2,0,1:T(4,128)}, u32[]{:S(2)}, u32[]{:S(2)}) collective-permute-start(f32[4,40,256]{2,0,1:T(4,128)} %get-tuple-element.58), channel_id=1, source_target_pairs={{0,16},{16,32},{32,48},{48,64},{64,80},{80,96},{96,112},{1,17},{17... | collective-permute-start | bytes 491528 | tf_op jit(solution)/shard_map/ppermute | solution.py:17
  212.0 53.3 %collective-permute-start.12 = (f32[4,40,256]{2,0,1:T(4,128)}, f32[4,40,256]{2,0,1:T(4,128)}, u32[]{:S(2)}, u32[]{:S(2)}) collective-permute-start(f32[4,40,256]{2,0,1:T(4,128)} %get-tuple-element.49), channel_id=1, source_target_pairs={{16,0},{32,16},{48,32},{64,48},{80,64},{96,80},{112,96},{17,1},{33... | collective-permute-start | bytes 491528 | tf_op jit(solution)/shard_map/ppermute | solution.py:20
  213.2 52.0 %collective-permute-start.13 = (f32[4,40,256]{2,0,1:T(4,128)}, f32[4,40,256]{2,0,1:T(4,128)}, u32[]{:S(2)}, u32[]{:S(2)}) collective-permute-start(f32[4,40,256]{2,0,1:T(4,128)} %get-tuple-element.50), channel_id=1, source_target_pairs={{0,16},{16,32},{32,48},{48,64},{64,80},{80,96},{96,112},{1,17},{17... | collective-permute-start | bytes 491528 | tf_op jit(solution)/shard_map/ppermute | solution.py:17
  219.5 52.8 %collective-permute-start.2 = (f32[48,4,256]{2,0,1:T(8,128)}, f32[48,4,256]{2,0,1:T(8,128)}, u32[]{:S(2)}, u32[]{:S(2)}) collective-permute-start(f32[48,4,256]{2,0,1:T(8,128)} %get-tuple-element.40), channel_id=1, source_target_pairs={{1,0},{2,1},{3,2},{4,3},{5,4},{6,5},{7,6},{8,7},{9,8},{10,9},{11,1... | collective-permute-start | bytes 589832 | tf_op jit(solution)/shard_map/ppermute | solution.py:20
  222.4 49.9 %collective-permute-start.3 = (f32[48,4,256]{2,0,1:T(8,128)}, f32[48,4,256]{2,0,1:T(8,128)}, u32[]{:S(2)}, u32[]{:S(2)}) collective-permute-start(f32[48,4,256]{2,0,1:T(8,128)} %get-tuple-element.39), channel_id=1, source_target_pairs={{0,1},{1,2},{2,3},{3,4},{4,5},{5,6},{6,7},{7,8},{8,9},{9,10},{10,1... | collective-permute-start | bytes 589832 | tf_op jit(solution)/shard_map/ppermute | solution.py:17
  266.2 11.6 %collective-permute-start.14 = (f32[48,4,256]{2,0,1:T(8,128)S(1)}, f32[48,4,256]{2,0,1:T(8,128)S(1)}, u32[]{:S(2)}, u32[]{:S(2)}) collective-permute-start(f32[48,4,256]{2,0,1:T(8,128)S(1)} %get-tuple-element.28), channel_id=1, source_target_pairs={{1,0},{2,1},{3,2},{4,3},{5,4},{6,5},{7,6},{8,7},{9,8},{10,9},{11,1... | collective-permute-start | bytes 589832 | tf_op jit(solution)/shard_map/ppermute | solution.py:20
  270.4 7.4 collective-permute-start.15
  319.1 9.1 %collective-permute-start.16 = (f32[4,40,256]{2,0,1:T(4,128)S(1)}, f32[4,40,256]{2,0,1:T(4,128)S(1)}, u32[]{:S(2)}, u32[]{:S(2)}) collective-permute-start(f32[4,40,256]{2,0,1:T(4,128)S(1)} %get-tuple-element.47), channel_id=1, source_target_pairs={{16,0},{32,16},{48,32},{64,48},{80,64},{96,80},{112,96},{17,1},{33... | collective-permute-start | bytes 491528 | tf_op jit(solution)/shard_map/ppermute | solution.py:20
  320.4 7.8 collective-permute-start.17
  329.1 113.5 %collective-permute-start.18 = (f32[48,4,256]{2,0,1:T(8,128)}, f32[48,4,256]{2,0,1:T(8,128)}, u32[]{:S(2)}, u32[]{:S(2)}) collective-permute-start(f32[48,4,256]{2,0,1:T(8,128)} %get-tuple-element.24), channel_id=1, source_target_pairs={{1,0},{2,1},{3,2},{4,3},{5,4},{6,5},{7,6},{8,7},{9,8},{10,9},{11,1... | collective-permute-start | bytes 589832 | tf_op jit(solution)/shard_map/ppermute | solution.py:20
  332.0 110.6 %collective-permute-start.19 = (f32[48,4,256]{2,0,1:T(8,128)}, f32[48,4,256]{2,0,1:T(8,128)}, u32[]{:S(2)}, u32[]{:S(2)}) collective-permute-start(f32[48,4,256]{2,0,1:T(8,128)} %get-tuple-element.23), channel_id=1, source_target_pairs={{0,1},{1,2},{2,3},{3,4},{4,5},{5,6},{6,7},{7,8},{8,9},{9,10},{10,1... | collective-permute-start | bytes 589832 | tf_op jit(solution)/shard_map/ppermute | solution.py:17
  545.3 6.2 collective-permute-start.21
  551.6 11.1 %collective-permute-start.22 = (f32[48,4,256]{2,0,1:T(8,128)S(1)}, f32[48,4,256]{2,0,1:T(8,128)S(1)}, u32[]{:S(2)}, u32[]{:S(2)}) collective-permute-start(f32[48,4,256]{2,0,1:T(8,128)S(1)} %get-tuple-element.20), channel_id=1, source_target_pairs={{1,0},{2,1},{3,2},{4,3},{5,4},{6,5},{7,6},{8,7},{9,8},{10,9},{11,1... | collective-permute-start | bytes 589832 | tf_op jit(solution)/shard_map/ppermute | solution.py:20
  606.0 7.5 collective-permute-start.24
  607.3 8.0 collective-permute-start.25
  615.4 7.3 collective-permute-start.26
  617.3 6.6 collective-permute-start.27
  666.8 6.6 collective-permute-start.28
  668.1 6.8 collective-permute-start.29
  674.9 8.5 %collective-permute-start.30 = (f32[48,4,256]{2,0,1:T(8,128)S(1)}, f32[48,4,256]{2,0,1:T(8,128)S(1)}, u32[]{:S(2)}, u32[]{:S(2)}) collective-permute-start(f32[48,4,256]{2,0,1:T(8,128)S(1)} %get-tuple-element.12), channel_id=1, source_target_pairs={{1,0},{2,1},{3,2},{4,3},{5,4},{6,5},{7,6},{8,7},{9,8},{10,9},{11,1... | collective-permute-start | bytes 589832 | tf_op jit(solution)/shard_map/ppermute | solution.py:20
  676.8 7.8 collective-permute-start.31
  774.2 19.6 %all-to-all-start = ((f32[16,1,440]{2,1,0:T(1,128)}), f32[16,1,440]{2,1,0:T(1,128)S(1)}, u32[]{:S(2)}, u32[]{:S(2)}) async-start(f32[16,1,440]{2,1,0:T(1,128)} %reshape.549), calls=%async_computation.1 | async-start | bytes 65536 | tf_op jit(solution)/shard_map/all_to_all | solution.py:155
  (44 other events, 943.4 us)
Sparse Core Ops, SparseCore 0:
  32.4 70.4 all-gather.1
  738.3 33.8 reduce-scatter.1
where the time goes:
time: 824 us; the launch traced here: 810 us
  other arithmetic  310 us (38%)
  local copies, waits for them, and re-layouts  227 us (28%)
  starting transfers between devices  120 us (15%)
  waiting for transfers between devices  99.1 us (12%)
  blocking collectives  25.7 us (3%)
  between operations  14.9 us (2%)
  matrix products  14.6 us (2%)
    gather x4, local copies, waits for them, and re-layouts, per_device(): sampled = field_after.reshape(-1)[receiver_flat]  149 us
    mul x4, other arithmetic, per_device(): accel = courant * stencil(field_now)  87 us
    add x4, other arithmetic, laplacian(): result_sum = result_sum + COEFFS[reach] * pairs  81.6 us
    concatenate x24, other arithmetic, padded_2(): block = jnp.concatenate([low, block, high], axis=dim)  67.2 us
    ppermute x16, starting transfers between devices, padded_2(): lax.ppermute(lax.slice_in_dim(block, block.shape[dim] - width, None, axis...  60.5 us
    ppermute x16, starting transfers between devices, padded_2(): lax.ppermute(lax.slice_in_dim(block, 0, width, axis=dim), axis, backward)  46.7 us
    all_gather x1, waiting for transfers between devices, per_device(): whole_model = lax.all_gather(deep_model, 'gy', axis=0, tiled=True)  35.2 us
    reduce_scatter x1, waiting for transfers between devices, per_device(): summed = lax.psum_scatter(spread_x, 'gx', scatter_dimension=2, tiled=True)  33.9 us
  transfers between devices with their start and end apart: 35, of which 20 were waited for; matrix products, arithmetic and copies ran while one was open for 26% of the time, Pallas kernels for 0%

commit v1 on v0

v1 whole, which is shorter than its diff:
```python
import jax
import jax.numpy as jnp
from jax import lax
from jax.experimental import pallas as pl
from jax.experimental.pallas import tpu as pltpu
from jax.sharding import PartitionSpec as P

ITERS = 4
HALO = 16
OWN = 40
EXT = OWN + 2 * HALO
LANES = 128
ACC_ROWS = 48
ACC_PLANES = 44
CENTRE = -43050.0
RING = (8064.0, -1008.0, 128.0, -9.0)
SCALE = 5040.0
SMEM = pltpu.SMEM
VMEM = pltpu.VMEM
EXACT = lax.Precision.HIGHEST


def params(mib):
    return pltpu.CompilerParams(vmem_limit_bytes=mib * 1024 * 1024)


def z_matrix():
    row = lax.broadcasted_iota(jnp.int32, (512, 256), 0) & 255
    column = lax.broadcasted_iota(jnp.int32, (512, 256), 1)
    distance = jnp.abs(row - column)
    result = jnp.zeros((512, 256), jnp.float32)
    for reach, value in enumerate(RING):
        result = jnp.where(distance == reach + 1, value, result)
    return result.astype(jnp.bfloat16)


def hat(fine, coarse, lower, limit, fraction):
    higher = jnp.minimum(lower + 1, limit)
    first = jnp.where(coarse == lower, 1.0 - fraction, 0.0)
    second = jnp.where(coarse == higher, fraction, 0.0)
    return first + second


def list_kernel(base_ref, cells_ref, own_ref, ext_ref, count_ref):
    base_x = base_ref[0] - (HALO - 4)
    base_y = base_ref[1] - (HALO - 4)
    span = EXT - 8

    def body(receiver, carry):
        own, ext = carry
        x = cells_ref[receiver] - base_x
        y = cells_ref[1024 + receiver] - base_y
        z = cells_ref[2048 + receiver]
        packed = receiver | (z << 10) | (y << 18) | (x << 25)
        in_ext = (x >= 0) & (x < span) & (y >= 0) & (y < span)
        in_own = (x >= 12) & (x < 52) & (y >= 12) & (y < 52)
        own_ref[own] = packed
        ext_ref[ext] = packed
        return own + in_own.astype(jnp.int32), ext + in_ext.astype(jnp.int32)

    own, ext = lax.fori_loop(0, 1024, body, (0, 0), unroll=8)
    count_ref[0] = own
    count_ref[1] = ext


def unpack(packed):
    receiver = packed & 1023
    z = (packed >> 10) & 255
    y = (packed >> 18) & 127
    x = packed >> 25
    return receiver, x + 4, y + 4, z


def model_kernel(base_ref, model_ref, courant_ref, inverse_ref, plane_ref):
    row = lax.broadcasted_iota(jnp.int32, (64, 256), 0)
    column = lax.broadcasted_iota(jnp.int32, (64, 256), 1)
    weight_z = hat(column, row, column // 4, 63, (column & 3).astype(jnp.float32) * 0.25)
    deep = jnp.dot(
        model_ref[...].reshape(480, 64), weight_z, precision=EXACT,
        preferred_element_type=jnp.float32,
    ).reshape(20, 24, 256)
    fine = lax.broadcasted_iota(jnp.int32, (EXT, 24), 0)
    coarse = lax.broadcasted_iota(jnp.int32, (EXT, 24), 1)
    limit_y = 159 - (base_ref[1] // 4 - 3)
    weight_y = hat(fine, coarse, fine // 4 - 1, limit_y, (fine & 3).astype(jnp.float32) * 0.25)
    place = fine + (base_ref[1] - HALO)
    weight_y = jnp.where((place >= 0) & (place < 640), weight_y, 0.0)
    for a in range(2, 19):
        plane = jnp.dot(weight_y, deep[a], precision=EXACT, preferred_element_type=jnp.float32)
        plane_ref[a, 0] = plane[:, :LANES]
        plane_ref[a, 1] = plane[:, LANES:]
    limit_x = 79 - (base_ref[0] // 4 - 5)
    factor = 0.01 / SCALE

    def group(index, carry):
        a = index + 1
        higher = jnp.minimum(a + 1, limit_x)
        start = base_ref[0] - HALO + 4 * index
        inside = ((start >= 0) & (start < 320)).astype(jnp.float32) * factor
        for half in range(2):
            for tile in range(EXT // 8):
                rows = pl.ds(8 * tile, 8)
                low = plane_ref[a, half, rows, :]
                high = plane_ref[higher, half, rows, :]
                for step in range(4):
                    speed = low * (1.0 - 0.25 * step) + high * (0.25 * step)
                    courant_ref[4 * index + step, half, rows, :] = speed * speed * inside
        return carry

    lax.fori_loop(1, 17, group, 0)

    def invert(index, carry):
        a = index + 5
        higher = jnp.minimum(a + 1, limit_x)
        for half in range(2):
            for tile in range(OWN // 8):
                rows = pl.ds(HALO + 8 * tile, 8)
                low = plane_ref[a, half, rows, :]
                high = plane_ref[higher, half, rows, :]
                for step in range(4):
                    speed = low * (1.0 - 0.25 * step) + high * (0.25 * step)
                    inverse_ref[4 * index + step, half, pl.ds(8 * tile, 8), :] = 2.0 / speed
        return carry

    lax.fori_loop(0, 10, invert, 0)


def copies(now, before, pieces, ext_now, ext_before):
    x_low, x_high, y_low, y_high, c_low, c_high = pieces
    result = []
    mid = pl.ds(HALO, OWN)
    for half in range(2):
        lanes = pl.ds(half * LANES, LANES)

        def add(source, planes, rows, target, to_planes, to_rows):
            result.append(
                (source.at[planes, rows, lanes], target.at[to_planes, half, to_rows, :])
            )

        every = pl.ds(0, OWN)
        add(now, every, every, ext_now, mid, mid)
        add(x_low, pl.ds(0, 16), every, ext_now, pl.ds(0, 16), mid)
        add(x_high, pl.ds(0, 16), every, ext_now, pl.ds(56, 16), mid)
        add(y_low, every, pl.ds(0, 16), ext_now, mid, pl.ds(0, 16))
        add(y_high, every, pl.ds(0, 16), ext_now, mid, pl.ds(56, 16))
        add(before, every, every, ext_before, mid, mid)
        add(x_low, pl.ds(16, 12), every, ext_before, pl.ds(4, 12), mid)
        add(x_high, pl.ds(16, 12), every, ext_before, pl.ds(56, 12), mid)
        add(y_low, pl.ds(40, 40), pl.ds(0, 16), ext_before, mid, pl.ds(0, 16))
        add(y_high, pl.ds(40, 40), pl.ds(0, 16), ext_before, mid, pl.ds(56, 16))
        for piece, near, far in ((c_low, 8, 0), (c_high, 56, 64)):
            for side, first in ((0, 12), (24, 56)):
                rows = pl.ds(0, 8)
                second = 4 if side == 0 else 60
                third = 8 if side == 0 else 56
                add(piece, pl.ds(side, 4), rows, ext_now, pl.ds(first, 4), pl.ds(far, 8))
                add(piece, pl.ds(side + 4, 4), rows, ext_now, pl.ds(first, 4), pl.ds(near, 8))
                add(piece, pl.ds(side + 8, 8), rows, ext_now, pl.ds(second, 8), pl.ds(near, 8))
                add(piece, pl.ds(side + 16, 8), rows, ext_before, pl.ds(third, 8), pl.ds(near, 8))
    return result


def start_all(pairs, sem):
    started = [pltpu.make_async_copy(a, b, sem) for a, b in pairs]
    for copy in started:
        copy.start()
    return started


def wait_all(started):
    for copy in started:
        copy.wait()


def stencil_pass(source, matrix_ref, step, emit):
    first = 4 * step
    span = EXT - 8 * step
    tiles = span // 8

    def group(index, carry):
        x = first + 4 * index
        whole = [
            source[pl.ds(x, 4), half, pl.ds(first, span), :].reshape(4 * span, LANES)
            for half in range(2)
        ]
        whole = jnp.concatenate(whole, axis=1)
        upper = whole.astype(jnp.bfloat16)
        lower = (whole - upper.astype(jnp.float32)).astype(jnp.bfloat16)
        along_z = jnp.dot(
            jnp.concatenate([upper, lower], axis=1), matrix_ref[...],
            preferred_element_type=jnp.float32,
        )
        for tile in range(tiles):
            for half in range(2):
                row = first + 8 * tile
                window = [source[x - 4 + j, half, pl.ds(row, 8), :] for j in range(12)]
                for g in range(4):
                    start = g * span + 8 * tile
                    total = along_z[start : start + 8, half * LANES : (half + 1) * LANES]
                    total = total + CENTRE * window[4 + g]
                    for reach in range(1, 5):
                        pair_x = window[4 + g + reach] + window[4 + g - reach]
                        pair_y = (
                            source[x + g, half, pl.ds(row + reach, 8), :]
                            + source[x + g, half, pl.ds(row - reach, 8), :]
                        )
                        total = total + RING[reach - 1] * (pair_x + pair_y)
                    emit(x, g, half, row, window[4 + g], total)
        return carry

    lax.fori_loop(0, span // 4, group, 0)


def own_plane(x, g):
    inside = (x >= HALO) & (x < HALO + OWN)
    return jnp.where(inside, x - HALO, OWN) + g


def forward_kernel(
    base_ref, source_ref, wavelet_ref, own_ref, count_ref, receivers_ref, observed_ref, matrix_ref,
    now, before, x_low, x_high, y_low, y_high, c_low, c_high, courant_in,
    accel_out, residual_ref,
    field_a, field_b, field_c, field_d, courant, accel, sems,
):
    loads = start_all(
        copies(now, before, (x_low, x_high, y_low, y_high, c_low, c_high), field_b, field_a)
        + [(courant_in, courant)],
        sems.at[0],
    )
    wait_all(loads)
    lane = lax.broadcasted_iota(jnp.int32, (1, LANES), 1)
    fields = [field_a, field_b, field_a, field_b, field_c, field_d]
    stores = []
    for step in range(1, ITERS + 1):
        older, newer, target = fields[step - 1], fields[step], fields[step + 1]

        def emit(x, g, half, row, centre, total):
            rows = pl.ds(row, 8)
            change = courant[x + g, half, rows, :] * total
            if HALO - 8 < row < HALO + OWN:
                accel[step - 1, own_plane(x, g), half, pl.ds(row - 12, 8), :] = change
            target[x + g, half, rows, :] = (
                centre + centre - older[x + g, half, rows, :] + change
            )

        if step == ITERS:
            def emit(x, g, half, row, centre, total):
                rows = pl.ds(row, 8)
                change = courant[x + g, half, rows, :] * total
                accel[step - 1, x + g - HALO, half, pl.ds(row - 12, 8), :] = change
                target[x + g, half, rows, :] = (
                    centre + centre - older[x + g, half, rows, :] + change
                )

        stencil_pass(newer, matrix_ref, step, emit)
        for source in range(4):
            x = source_ref[source] - (base_ref[0] - HALO)
            y = source_ref[4 + source] - (base_ref[1] - HALO)
            z = source_ref[8 + source]
            amount = wavelet_ref[4 * (step - 1) + source]

            @pl.when((x >= 0) & (x < EXT) & (y >= 0) & (y < EXT))
            def _():
                half = z // LANES
                added = jnp.where(lane == (z & (LANES - 1)), amount, 0.0)
                target[x, half, pl.ds(y, 1), :] += added

                @pl.when((x >= 16) & (x < 56) & (y >= 16) & (y < 56))
                def _():
                    accel[step - 1, x - 16, half, pl.ds(y - 12, 1), :] += added

        stores += start_all([(accel.at[step - 1], accel_out.at[step - 1])], sems.at[1])
    number = count_ref[0]
    place = (
        lax.broadcasted_iota(jnp.int32, (8, LANES), 0) * LANES
        + lax.broadcasted_iota(jnp.int32, (8, LANES), 1)
    )
    samples = fields[2:]

    def sample(index, carry):
        carry = list(carry)
        for j in range(4):
            entry = 4 * index + j
            valid = entry < number
            packed = jnp.where(valid, own_ref[jnp.minimum(entry, 1023)], 0)
            receiver, x, y, z = unpack(packed)
            half = z // LANES
            at_lane = lane == jnp.where(valid, z & (LANES - 1), -1)
            at_place = place == jnp.where(valid, receiver, -1)
            for step in range(ITERS):
                values = jnp.where(at_lane, samples[step][x, half, pl.ds(y, 1), :], 0.0)
                value = jnp.sum(values, axis=1, keepdims=True)
                carry[step] = jnp.where(at_place, value, carry[step])
        return tuple(carry)

    zero = jnp.zeros((8, LANES), jnp.float32)
    sampled = lax.fori_loop(0, (number + 3) // 4, sample, (zero,) * ITERS)
    local_x = receivers_ref[0] - base_ref[0]
    local_y = receivers_ref[1] - base_ref[1]
    mine = (local_x >= 0) & (local_x < OWN) & (local_y >= 0) & (local_y < OWN)
    for step in range(ITERS):
        residual_ref[step] = jnp.where(mine, sampled[step] - observed_ref[step], 0.0)
    wait_all(stores)


def adjoint_kernel(
    base_ref, ext_ref, count_ref, residual_ref, matrix_ref,
    now, after, x_low, x_high, y_low, y_high, c_low, c_high, courant_in, accel_in, inverse_in,
    out_ref,
    field_a, field_b, field_c, field_d, scaled_a, scaled_b, courant, accel, inverse, coarse, sems,
):
    loads = start_all(
        copies(now, after, (x_low, x_high, y_low, y_high, c_low, c_high), field_b, field_a)
        + [(courant_in, courant)],
        sems.at[0],
    )
    later = start_all([(accel_in, accel), (inverse_in, inverse)], sems.at[1])
    wait_all(loads)

    def scale(x, carry):
        for half in range(2):
            for tile in range(EXT // 8):
                rows = pl.ds(8 * tile, 8)
                scaled_a[x, half, rows, :] = field_b[x, half, rows, :] * courant[x, half, rows, :]
        return carry

    lax.fori_loop(0, EXT, scale, 0)
    lane = lax.broadcasted_iota(jnp.int32, (1, LANES), 1)
    fields = [field_a, field_b, field_a, field_b, field_c, field_d]
    number = count_ref[1]
    for step in range(1, ITERS + 1):
        older, newer, target = fields[step - 1], fields[step], fields[step + 1]
        source, scaled = (scaled_a, scaled_b) if step % 2 else (scaled_b, scaled_a)

        def emit(x, g, half, row, centre, total):
            rows = pl.ds(row, 8)
            middle = newer[x + g, half, rows, :]
            value = middle + middle - older[x + g, half, rows, :] + total
            target[x + g, half, rows, :] = value
            if step < ITERS:
                scaled[x + g, half, rows, :] = value * courant[x + g, half, rows, :]

        stencil_pass(source, matrix_ref, step, emit)

        def inject(entry, carry):
            receiver, x, y, z = unpack(ext_ref[entry])
            half = z // LANES
            amount = residual_ref[(ITERS - step) * 1024 + receiver]
            added = jnp.where(lane == (z & (LANES - 1)), amount, 0.0)
            target[x, half, pl.ds(y, 1), :] += added
            if step < ITERS:
                scaled[x, half, pl.ds(y, 1), :] += added * courant[x, half, pl.ds(y, 1), :]
            return carry

        lax.fori_loop(0, number, inject, 0)
    wait_all(later)
    coarse[...] = jnp.zeros(coarse.shape, jnp.float32)
    limit_x = 79 - base_ref[0] // 4

    def image(a, carry):
        higher = jnp.minimum(a + 1, limit_x)
        for half in range(2):
            for tile in range(OWN // 8):
                rows = pl.ds(8 * tile, 8)
                low, high = None, None
                for g in range(4):
                    x = 4 * a + g
                    total = None
                    for step in range(1, ITERS + 1):
                        term = (
                            fields[step + 1][x + HALO, half, pl.ds(HALO + 8 * tile, 8), :]
                            * accel[ITERS - step, x, half, pl.ds(4 + 8 * tile, 8), :]
                        )
                        total = term if total is None else total + term
                    total = total * inverse[x, half, rows, :]
                    weight = 0.25 * g
                    low = total if low is None else low + (1.0 - weight) * total
                    if g:
                        part = weight * total
                        high = part if high is None else high + part
                coarse[a, half, rows, :] += low
                coarse[higher, half, rows, :] += high
        return carry

    lax.fori_loop(0, 10, image, 0)
    row = lax.broadcasted_iota(jnp.int32, (16, OWN), 0)
    fine = lax.broadcasted_iota(jnp.int32, (16, OWN), 1)
    limit_y = 159 - base_ref[1] // 4
    weight_y = hat(fine, row, fine // 4, limit_y, (fine & 3).astype(jnp.float32) * 0.25)
    fine = lax.broadcasted_iota(jnp.int32, (256, 64), 0)
    column = lax.broadcasted_iota(jnp.int32, (256, 64), 1)
    weight_z = hat(fine, column, fine // 4, 63, (fine & 3).astype(jnp.float32) * 0.25)
    parts = []
    for a in range(11):
        plane = jnp.concatenate([coarse[a, 0], coarse[a, 1]], axis=1)
        parts.append(
            jnp.dot(weight_y, plane, precision=EXACT, preferred_element_type=jnp.float32)
        )
    stacked = jnp.concatenate(parts, axis=0)
    result = jnp.dot(stacked, weight_z, precision=EXACT, preferred_element_type=jnp.float32)
    out_ref[...] = (result * 0.125).reshape(11, 16, 64)


def shifts(axis, block_up, block_down):
    count = lax.axis_size(axis)
    up = [(i, i + 1) for i in range(count - 1)]
    down = [(i + 1, i) for i in range(count - 1)]
    return lax.ppermute(block_up, axis, up), lax.ppermute(block_down, axis, down)


def exchange_x(now, before):
    return shifts(
        "gx",
        jnp.concatenate([now[24:], before[28:]], axis=0),
        jnp.concatenate([now[:16], before[:12]], axis=0),
    )


def exchange_y(now, before):
    return shifts(
        "gy",
        jnp.concatenate([now[:, 24:], before[:, 24:]], axis=0),
        jnp.concatenate([now[:, :16], before[:, :16]], axis=0),
    )


def exchange_corners(x_low, x_high):
    up = [
        x_low[12:16, 24:32], x_low[12:16, 32:40], x_low[4:12, 32:40], x_low[20:28, 32:40],
        x_high[0:4, 24:32], x_high[0:4, 32:40], x_high[4:12, 32:40], x_high[16:24, 32:40],
    ]
    down = [
        x_low[12:16, 8:16], x_low[12:16, 0:8], x_low[4:12, 0:8], x_low[20:28, 0:8],
        x_high[0:4, 8:16], x_high[0:4, 0:8], x_high[4:12, 0:8], x_high[16:24, 0:8],
    ]
    return shifts("gy", jnp.concatenate(up, axis=0), jnp.concatenate(down, axis=0))


def exchange(now, before):
    x_low, x_high = exchange_x(now, before)
    y_low, y_high = exchange_y(now, before)
    c_low, c_high = exchange_corners(x_low, x_high)
    return (x_low, x_high, y_low, y_high, c_low, c_high)


def spec(space):
    return pl.BlockSpec(memory_space=space)


def per_device(
    velocity, forward_now, forward_before, adjoint_now, adjoint_after,
    source_cells, receiver_cells, wavelet, observed,
):
    index_x = lax.axis_index("gx")
    index_y = lax.axis_index("gy")
    base = jnp.stack([index_x * OWN, index_y * OWN]).astype(jnp.int32)
    everywhere = ("gx", "gy")

    padded = jnp.pad(velocity, ((0, 0), (3, 4), (0, 0)))
    windows = jnp.stack([padded[:, 10 * j : 10 * j + 17].reshape(-1) for j in range(16)])
    windows = jnp.broadcast_to(windows[None], (8, 16, 680)).reshape(128, 680)
    arrived = lax.all_to_all(windows, everywhere, 0, 0, tiled=True)
    arrived = jnp.pad(arrived.reshape(8, 16, 680), ((0, 0), (1, 1), (0, 0)))
    arrived = lax.dynamic_slice_in_dim(arrived, 2 * index_x, 4, axis=1)
    arrived = arrived.reshape(8, 20, 17, 8).transpose(1, 2, 0, 3).reshape(20, 17, 64)
    model = jnp.pad(arrived, ((0, 0), (0, 7), (0, 0)))

    forward_pieces = exchange(forward_now, forward_before)
    adjoint_pieces = exchange(adjoint_now, adjoint_after)

    own_list, ext_list, counts = pl.pallas_call(
        list_kernel,
        out_shape=(
            jax.ShapeDtypeStruct((1024,), jnp.int32),
            jax.ShapeDtypeStruct((1024,), jnp.int32),
            jax.ShapeDtypeStruct((2,), jnp.int32),
        ),
        in_specs=[spec(SMEM)] * 2,
        out_specs=(spec(SMEM),) * 3,
        cost_estimate=pl.CostEstimate(flops=10_000_000, bytes_accessed=20_000_000, transcendentals=0),
    )(base, receiver_cells.reshape(-1))

    courant, inverse = pl.pallas_call(
        model_kernel,
        out_shape=(
            jax.ShapeDtypeStruct((EXT, 2, EXT, LANES), jnp.float32),
            jax.ShapeDtypeStruct((OWN, 2, OWN, LANES), jnp.float32),
        ),
        in_specs=[spec(SMEM), spec(VMEM)],
        out_specs=(spec(VMEM), spec(VMEM)),
        scratch_shapes=[VMEM((20, 2, EXT, LANES), jnp.float32)],
        compiler_params=params(32),
        cost_estimate=pl.CostEstimate(flops=10_000_000, bytes_accessed=10_000_000, transcendentals=0),
    )(base, model)

    field = VMEM((EXT, 2, EXT, LANES), jnp.float32)
    accel_shape = (ITERS, ACC_PLANES, 2, ACC_ROWS, LANES)
    matrix = z_matrix()
    accel, residual = pl.pallas_call(
        forward_kernel,
        out_shape=(
            jax.ShapeDtypeStruct(accel_shape, jnp.float32),
            jax.ShapeDtypeStruct((ITERS, 8, LANES), jnp.float32),
        ),
        in_specs=[spec(SMEM)] * 5 + [spec(VMEM)] * 3 + [spec(pl.ANY)] * 9,
        out_specs=(spec(pl.ANY), spec(VMEM)),
        scratch_shapes=[field] * 5 + [VMEM(accel_shape, jnp.float32), pltpu.SemaphoreType.DMA((2,))],
        compiler_params=params(48),
        cost_estimate=pl.CostEstimate(flops=100_000_000, bytes_accessed=30_000_000, transcendentals=0),
    )(
        base, source_cells.reshape(-1), wavelet.reshape(-1), own_list, counts,
        receiver_cells.reshape(3, 8, LANES), observed.reshape(ITERS, 8, LANES), matrix,
        forward_now, forward_before, *forward_pieces, courant,
    )

    low, high = shifts("gx", residual, residual)
    residual = residual + low + high
    low, high = shifts("gy", residual, residual)
    residual = (residual + low + high).reshape(-1)

    part = pl.pallas_call(
        adjoint_kernel,
        out_shape=jax.ShapeDtypeStruct((11, 16, 64), jnp.float32),
        in_specs=[spec(SMEM)] * 4 + [spec(VMEM)] + [spec(pl.ANY)] * 11,
        out_specs=spec(VMEM),
        scratch_shapes=[field] * 7
        + [
            VMEM(accel_shape, jnp.float32),
            VMEM((OWN, 2, OWN, LANES), jnp.float32),
            VMEM((11, 2, OWN, LANES), jnp.float32),
            pltpu.SemaphoreType.DMA((2,)),
        ],
        compiler_params=params(58),
        cost_estimate=pl.CostEstimate(flops=100_000_000, bytes_accessed=30_000_000, transcendentals=0),
    )(
        base, ext_list, counts, residual, matrix,
        adjoint_now, adjoint_after, *adjoint_pieces, courant, accel, inverse,
    )

    spread = lax.dynamic_update_slice(
        jnp.zeros((85, 11, 64), jnp.float32), part[:, :11], (10 * index_x, 0, 0)
    )[:80]
    spread = spread.reshape(16, 5, 11, 8, 8).transpose(3, 0, 1, 2, 4).reshape(128, 440)
    returned = lax.all_to_all(spread, everywhere, 0, 0, tiled=True)
    summed = returned.reshape(8, 16, 5, 11, 8).sum(axis=0)
    main = summed[:, :, :10]
    over = jnp.pad(summed[:-1, :, 10:], ((1, 0), (0, 0), (0, 9), (0, 0)))
    return (main + over).transpose(1, 0, 2, 3).reshape(5, 160, 8)


def solution(mesh):
    return jax.shard_map(
        per_device,
        mesh=mesh,
        in_specs=(
            P("gy", None, "gx"),
            P("gx", "gy", None),
            P("gx", "gy", None),
            P("gx", "gy", None),
            P("gx", "gy", None),
            P(),
            P(),
            P(),
            P(),
        ),
        out_specs=P("gy", None, "gx"),
        check_vma=False,
    )
```

time: 824 us -> 244 us (0.30); the launches traced: 810 us -> 243 us
  other arithmetic: 310 us -> 12.6 us
  local copies, waits for them, and re-layouts: 227 us -> 31.8 us
  Pallas kernels: 0 us -> 76.2 us
  waiting for transfers between devices: 99.1 us -> 31.1 us
  starting transfers between devices: 120 us -> 54.7 us
  matrix products: 14.6 us -> 0 us
  between operations: 14.9 us -> 0.7 us
  blocking collectives: 25.7 us -> 35.4 us
    gather x6 -> x0, local copies, waits for them, and re-layouts: 152 us -> none  [the longest x4 149 us: per_device(): sampled = field_after.reshape(-1)[receiver_flat]]
    mul x13 -> x0, other arithmetic: 101 us -> none  [the longest x4 87 us: per_device(): accel = courant * stencil(field_now)]
    add x8 -> x1, other arithmetic: 94.3 us -> 0.01 us  [per_device(): residual = residual + low + high]
    pallas_call x0 -> x4, Pallas kernels: none -> 76.2 us  [the longest x1 31.2 us: per_device(): pl.pallas_call(adjoint_kernel, out_shape=jax.ShapeDtypeStruct((11, 16, 64...]
    ppermute x32 -> x16, starting transfers between devices: 107 us -> 43.4 us  [the longest x8 29.8 us: shifts(): lax.ppermute(block_up, axis, up)]
    concatenate x24 -> x8, other arithmetic: 67.2 us -> 10.4 us  [the longest x2 3.71 us: exchange_y(): jnp.concatenate([now[:, 24:], before[:, 24:]], axis=0)]
    scatter-add x10 -> x0, other arithmetic: 46.4 us -> none  [the longest x4 29.9 us: per_device(): change = change.reshape(-1).at[receiver_flat].add(residual_list[section])...]
    all_to_all x0 -> x1, blocking collectives: none -> 35.4 us  [per_device(): returned = lax.all_to_all(spread, everywhere, 0, 0, tiled=True)]
  transfers between devices with their start and end apart: 35 -> 17, of which waited for: 20 -> 5; matrix products, arithmetic and copies ran while one was open for 26% -> 11% of each run, Pallas kernels for 0% -> 19%
where the time goes in v1:
time: 244 us; the launch traced here: 243 us
  Pallas kernels  76.2 us (31%)
  starting transfers between devices  54.7 us (22%)
  blocking collectives  35.4 us (15%)
  local copies, waits for them, and re-layouts  31.8 us (13%)
  waiting for transfers between devices  31.1 us (13%)
  other arithmetic  12.6 us (5%)
    all_to_all x1, blocking collectives, per_device(): returned = lax.all_to_all(spread, everywhere, 0, 0, tiled=True)  35.4 us
    pallas_call x1, Pallas kernels, per_device(): pl.pallas_call(adjoint_kernel, out_shape=jax.ShapeDtypeStruct((11, 16, 64...  31.2 us
    ppermute x8, starting transfers between devices, shifts(): lax.ppermute(block_up, axis, up)  29.8 us
    pallas_call x1, Pallas kernels, per_device(): pl.pallas_call(forward_kernel, out_shape=(jax.ShapeDtypeStruct(accel_shap...  27.7 us
    ppermute x8, waiting for transfers between devices, shifts(): lax.ppermute(block_down, axis, down)  27.4 us
    ppermute x8, starting transfers between devices, shifts(): lax.ppermute(block_down, axis, down)  13.6 us
    pallas_call x1, Pallas kernels, per_device(): pl.pallas_call(list_kernel, out_shape=(jax.ShapeDtypeStruct((1024,), jnp....  13.3 us
    all_to_all x1, starting transfers between devices, per_device(): arrived = lax.all_to_all(windows, everywhere, 0, 0, tiled=True)  11.3 us
  transfers between devices with their start and end apart: 17, of which 5 were waited for; matrix products, arithmetic and copies ran while one was open for 11% of the time, Pallas kernels for 19%

profile of v1, /device:TPU:1, one launch (start us, length us, event | category | flops | bytes accessed | tf_op | source)
XLA Modules:
  0.0 242.5 jit_solution(10526173389528238936)
XLA Ops:
  0.0 1.4 fusion.12
  2.9 4.2 %collective-permute-start = (f32[28,40,256]{2,1,0:T(8,128)}, f32[28,40,256]{2,1,0:T(8,128)S(1)}, u32[]{:S(2)}, u32[]{:S(2)}) collective-permute-start(f32[28,40,256]{2,1,0:T(8,128)} %pad_maximum_fusion.4), channel_id=1, source_target_pairs={{0,16},{16,32},{32,48},{48,64},{64,80},{80,96},{96,112},{1,17},{17... | collective-permute-start | bytes 3440648 | tf_op jit(solution)/shard_map/ppermute | solution.py:408
  11.1 4.4 %collective-permute-start.2 = (f32[80,16,256]{2,1,0:T(8,128)}, f32[80,16,256]{2,1,0:T(8,128)}, u32[]{:S(2)}, u32[]{:S(2)}) collective-permute-start(f32[80,16,256]{2,1,0:T(8,128)} %pad_maximum_fusion), channel_id=1, source_target_pairs={{0,1},{1,2},{2,3},{3,4},{4,5},{5,6},{6,7},{7,8},{8,9},{9,10},{10,1... | collective-permute-start | bytes 3932168 | tf_op jit(solution)/shard_map/ppermute | solution.py:408
  16.7 1.9 collective-permute-start.3
  23.3 11.3 %all-to-all-start = ((f32[128,1,680]{2,1,0:T(1,128)}), f32[128,1,680]{2,1,0:T(1,128)S(1)}, u32[]{:S(2)}, u32[]{:S(2)}) async-start(f32[128,1,680]{2,1,0:T(1,128)} %copy.69), calls=%async_computation | async-start | bytes 786432 | tf_op jit(solution)/shard_map/all_to_all | solution.py:462
  34.7 1.4 fusion.8
  37.6 4.4 %collective-permute-start.10 = (f32[28,40,256]{2,1,0:T(8,128)}, f32[28,40,256]{2,1,0:T(8,128)}, u32[]{:S(2)}, u32[]{:S(2)}) collective-permute-start(f32[28,40,256]{2,1,0:T(8,128)} %pad_maximum_fusion.6), channel_id=1, source_target_pairs={{0,16},{16,32},{32,48},{48,64},{64,80},{80,96},{96,112},{1,17},{17... | collective-permute-start | bytes 3440648 | tf_op jit(solution)/shard_map/ppermute | solution.py:408
  42.0 1.5 fusion.5
  44.6 2.5 %pad_maximum_fusion.2 = f32[80,16,256]{2,1,0:T(8,128)} fusion(f32[40,16,256]{2,1,0:T(8,128)} %get-tuple-element.81, f32[40,16,256]{2,1,0:T(8,128)} %get-tuple-element.20), kind=kLoop, calls=%fused_computation.2 | loop fusion | flops 327680 | bytes 2621440 | tf_op jit(solution)/shard_map/concatenate | solution.py:422
  49.7 13.3 %shard_map.91 = (s32[1024]{0:T(1024)}, s32[1024]{0:T(1024)}, s32[2]{0:T(128)}) custom-call(s32[2]{0:T(128)} %pad_add_fusion.base_ref, s32[3072]{0:T(1024)} %reshape.47.cells_ref), custom_call_target="tpu_custom_call" | custom-call | flops 10000000 | bytes 20000000 | tf_op jit(solution)/shard_map/pallas_call | solution.py:471
  63.4 2.0 reshape.53
  65.4 2.4 copy.70
  68.1 4.0 %shard_map.92 = (f32[72,2,72,128]{3,2,1,0:T(8,128)S(1)}, f32[40,2,40,128]{3,2,1,0:T(8,128)S(1)}) custom-call(s32[2]{0:T(128)S(1)} %copy-done.3, f32[20,24,64]{2,1,0:T(8,128)S(1)} %pad.18.model_ref), custom_call_target="tpu_custom_call" | custom-call | flops 10000000 | bytes 10000000 | tf_op jit(solution)/shard_map/pallas_call | solution.py:483
  72.1 2.4 copy-done
  75.9 3.8 %collective-permute-start.12 = (f32[80,16,256]{2,1,0:T(8,128)}, f32[80,16,256]{2,1,0:T(8,128)}, u32[]{:S(2)}, u32[]{:S(2)}) collective-permute-start(f32[80,16,256]{2,1,0:T(8,128)} %pad_maximum_fusion.2), channel_id=1, source_target_pairs={{0,1},{1,2},{2,3},{3,4},{4,5},{5,6},{6,7},{7,8},{8,9},{9,10},{10,1... | collective-permute-start | bytes 3932168 | tf_op jit(solution)/shard_map/ppermute | solution.py:408
  80.5 1.9 collective-permute-start.13
  85.1 17.7 %collective-permute-done.11.x_high = f32[28,40,256]{2,1,0:T(8,128)S(1)} collective-permute-done((f32[28,40,256]{2,1,0:T(8,128)}, f32[28,40,256]{2,1,0:T(8,128)S(1)}, u32[]{:S(2)}, u32[]{:S(2)}) %collective-permute-start.11) | collective-permute-done | bytes 1146912 | tf_op jit(solution)/shard_map/ppermute | solution.py:408
  102.8 4.7 %collective-permute-start.4 = (f32[48,8,256]{2,1,0:T(8,128)S(1)}, f32[48,8,256]{2,1,0:T(8,128)S(1)}, u32[]{:S(2)}, u32[]{:S(2)}) collective-permute-start(f32[48,8,256]{2,1,0:T(8,128)S(1)} %get-tuple-element.50), channel_id=1, source_target_pairs={{0,1},{1,2},{2,3},{3,4},{4,5},{5,6},{6,7},{7,8},{8,9},{9,10},{10,1... | collective-permute-start | bytes 1179656 | tf_op jit(solution)/shard_map/ppermute | solution.py:408
  107.5 1.9 collective-permute-start.5
  109.5 2.7 %collective-permute-done.4.c_low = f32[48,8,256]{2,1,0:T(8,128)S(1)} collective-permute-done((f32[48,8,256]{2,1,0:T(8,128)S(1)}, f32[48,8,256]{2,1,0:T(8,128)S(1)}, u32[]{:S(2)}, u32[]{:S(2)}) %collective-permute-start.4) | collective-permute-done | bytes 393248 | tf_op jit(solution)/shard_map/ppermute | solution.py:408
  112.2 4.4 %collective-permute-done.5.c_high = f32[48,8,256]{2,1,0:T(8,128)S(1)} collective-permute-done((f32[48,8,256]{2,1,0:T(8,128)S(1)}, f32[48,8,256]{2,1,0:T(8,128)S(1)}, u32[]{:S(2)}, u32[]{:S(2)}) %collective-permute-start.5) | collective-permute-done | bytes 393248 | tf_op jit(solution)/shard_map/ppermute | solution.py:408
  116.6 27.7 %shard_map.93 = (f32[4,44,2,48,128]{4,3,2,1,0:T(8,128)}, f32[4,8,128]{2,1,0:T(8,128)S(1)}) custom-call(s32[2]{0:T(128)S(1)} %copy-done.3, s32[12]{0:T(128)S(1)} %reshape.48.source_ref, f32[16]{0:T(128)S(1)} %reshape.49.wavelet_ref, s32[1024]{0:T(1024)S(1)} %copy-done.4, s32[2]{0:T(128)S(1)} %copy-done.5, s32[3,8,128]{2,1,0:T(8,128)S(1)} %bitcast.33, ...), custom_call_target="tpu_custom_call" | custom-call | flops 100000000 | bytes 30000000 | tf_op jit(solution)/shard_map/pallas_call | solution.py:499
  145.6 4.0 %collective-permute-start.6 = (f32[4,8,128]{2,1,0:T(8,128)S(1)}, f32[4,8,128]{2,1,0:T(8,128)S(1)}, u32[]{:S(2)}, u32[]{:S(2)}) collective-permute-start(f32[4,8,128]{2,1,0:T(8,128)S(1)} %get-tuple-element.16), channel_id=1, source_target_pairs={{0,16},{16,32},{32,48},{48,64},{64,80},{80,96},{96,112},{1,17},{17... | collective-permute-start | bytes 49160 | tf_op jit(solution)/shard_map/ppermute | solution.py:408
  149.6 2.3 collective-permute-start.14
  151.9 2.1 collective-permute-start.15
  154.0 1.9 collective-permute-start.9
  155.9 5.3 %collective-permute-done.9 = f32[4,8,128]{2,1,0:T(8,128)S(1)} collective-permute-done((f32[4,8,128]{2,1,0:T(8,128)S(1)}, f32[4,8,128]{2,1,0:T(8,128)S(1)}, u32[]{:S(2)}, u32[]{:S(2)}) %collective-permute-start.9) | collective-permute-done | bytes 16416 | tf_op jit(solution)/shard_map/ppermute | solution.py:408
  161.2 2.1 collective-permute-start.8
  165.7 31.2 %shard_map.94 = f32[11,16,64]{2,1,0:T(8,128)} custom-call(s32[2]{0:T(128)} %pad_add_fusion.base_ref, s32[1024]{0:T(1024)} %get-tuple-element.12.ext_ref, s32[2]{0:T(128)} %get-tuple-element.13.count_ref, f32[4096]{0:T(1024)} %add_bitcast_fusion.residual_ref, bf16[512,256]{1,0:T(8,128)(2,1)} %copy-done.1, f32[40,40,256]{2,1,0:T(8,128)} %now.3, ...), custom_call_target="tpu_custom_call" | custom-call | flops 100000000 | bytes 30000000 | tf_op jit(solution)/shard_map/pallas_call | solution.py:521
  198.2 2.9 %reshape.56 = f32[16,5,11,8,8]{4,3,1,0,2:T(8,128)} reshape(f32[80,11,64]{2,0,1:T(8,128)S(1)} %slice.307) | data formatting | bytes 450560 | tf_op jit(solution)/shard_map/reshape | solution.py:543
  201.1 2.9 %copy.73 = f32[8,16,5,11,8]{1,0,4,3,2:T(8,128)S(1)} copy(f32[8,16,5,11,8]{4,0,2,1,3:T(8,128)} %bitcast.34) | data formatting | bytes 450560 | tf_op jit(solution)/shard_map/transpose | solution.py:543
  204.6 35.4 %all_to_all.18 = f32[128,1,440]{2,1,0:T(1,128)S(1)} all-to-all(f32[128,1,440]{2,1,0:T(1,128)S(1)} %copy.74), channel_id=1, replica_groups=mesh['gx'=8,'gy'=16] {'gx','gy'}, dimensions={0} | all-to-all | bytes 450560 | tf_op jit(solution)/shard_map/all_to_all | solution.py:544
  (140 shorter events, 29.9 us)
Async XLA Ops:
  2.9 6.6 %copy-start.9 = (f32[40,40,256]{2,1,0:T(8,128)S(1)}, f32[40,40,256]{2,1,0:T(8,128)}, u32[]{:S(2)}) copy-start(f32[40,40,256]{2,1,0:T(8,128)} %before.1) | copy-start | bytes 4915204
  2.9 71.6 %collective-permute-start = (f32[28,40,256]{2,1,0:T(8,128)}, f32[28,40,256]{2,1,0:T(8,128)S(1)}, u32[]{:S(2)}, u32[]{:S(2)}) collective-permute-start(f32[28,40,256]{2,1,0:T(8,128)} %pad_maximum_fusion.4), channel_id=1, source_target_pairs={{0,16},{16,32},{32,48},{48,64},{64,80},{80,96},{96,112},{1,17},{17... | collective-permute-start | bytes 3440648 | tf_op jit(solution)/shard_map/ppermute | solution.py:408
  8.3 72.3 %collective-permute-start.1 = (f32[28,40,256]{2,1,0:T(8,128)}, f32[28,40,256]{2,1,0:T(8,128)S(1)}, u32[]{:S(2)}, u32[]{:S(2)}) collective-permute-start(f32[28,40,256]{2,1,0:T(8,128)} %pad_maximum_fusion.5), channel_id=1, source_target_pairs={{16,0},{32,16},{48,32},{64,48},{80,64},{96,80},{112,96},{17,1},{33... | collective-permute-start | bytes 3440648 | tf_op jit(solution)/shard_map/ppermute | solution.py:408
  11.1 96.3 %collective-permute-start.2 = (f32[80,16,256]{2,1,0:T(8,128)}, f32[80,16,256]{2,1,0:T(8,128)}, u32[]{:S(2)}, u32[]{:S(2)}) collective-permute-start(f32[80,16,256]{2,1,0:T(8,128)} %pad_maximum_fusion), channel_id=1, source_target_pairs={{0,1},{1,2},{2,3},{3,4},{4,5},{5,6},{6,7},{7,8},{8,9},{9,10},{10,1... | collective-permute-start | bytes 3932168 | tf_op jit(solution)/shard_map/ppermute | solution.py:408
  15.5 3.1 %copy-start.11 = (f32[5,160,8]{1,2,0:T(8,128)S(1)}, f32[5,160,8]{1,2,0:T(8,128)}, u32[]{:S(2)}) copy-start(f32[5,160,8]{1,2,0:T(8,128)} %param.9) | copy-start | bytes 76804
  16.7 92.8 %collective-permute-start.3 = (f32[80,16,256]{2,1,0:T(8,128)}, f32[80,16,256]{2,1,0:T(8,128)}, u32[]{:S(2)}, u32[]{:S(2)}) collective-permute-start(f32[80,16,256]{2,1,0:T(8,128)} %pad_maximum_fusion.1), channel_id=1, source_target_pairs={{1,0},{2,1},{3,2},{4,3},{5,4},{6,5},{7,6},{8,7},{9,8},{10,9},{11,1... | collective-permute-start | bytes 3932168 | tf_op jit(solution)/shard_map/ppermute | solution.py:408
  23.3 40.0 %all-to-all-start = ((f32[128,1,680]{2,1,0:T(1,128)}), f32[128,1,680]{2,1,0:T(1,128)S(1)}, u32[]{:S(2)}, u32[]{:S(2)}) async-start(f32[128,1,680]{2,1,0:T(1,128)} %copy.69), calls=%async_computation | async-start | bytes 786432 | tf_op jit(solution)/shard_map/all_to_all | solution.py:462
  36.5 5.5 %copy-start.8 = (f32[40,40,256]{2,1,0:T(8,128)S(1)}, f32[40,40,256]{2,1,0:T(8,128)}, u32[]{:S(2)}) copy-start(f32[40,40,256]{2,1,0:T(8,128)} %after.1) | copy-start | bytes 4915204
  37.6 38.2 %collective-permute-start.10 = (f32[28,40,256]{2,1,0:T(8,128)}, f32[28,40,256]{2,1,0:T(8,128)}, u32[]{:S(2)}, u32[]{:S(2)}) collective-permute-start(f32[28,40,256]{2,1,0:T(8,128)} %pad_maximum_fusion.6), channel_id=1, source_target_pairs={{0,16},{16,32},{32,48},{48,64},{64,80},{80,96},{96,112},{1,17},{17... | collective-permute-start | bytes 3440648 | tf_op jit(solution)/shard_map/ppermute | solution.py:408
  44.6 2.5 %copy-start.10 = (f32[40,16,256]{2,1,0:T(8,128)S(1)}, f32[40,16,256]{2,1,0:T(8,128)}, u32[]{:S(2)}) copy-start(f32[40,16,256]{2,1,0:T(8,128)} %get-tuple-element.82) | copy-start | bytes 1966084
  47.1 1.8 copy-start.15
  47.1 2.4 copy-start.17
  47.1 2.5 %copy-start.18 = (f32[4,4]{1,0:T(4,128)S(1)}, f32[4,4]{1,0:T(4,128)}, u32[]{:S(2)}) copy-start(f32[4,4]{1,0:T(4,128)} %param.16) | copy-start | bytes 196
  47.1 2.6 %copy-start.16 = (f32[4,1024]{1,0:T(4,128)S(1)}, f32[4,1024]{1,0:T(4,128)}, u32[]{:S(2)}) copy-start(f32[4,1024]{1,0:T(4,128)} %param.17) | copy-start | bytes 49156
  63.3 53.3 %copy-start.1 = (bf16[512,256]{1,0:T(8,128)(2,1)}, bf16[512,256]{1,0:T(8,128)(2,1)S(1)}, u32[]{:S(2)}) copy-start(bf16[512,256]{1,0:T(8,128)(2,1)S(1)} %select_convert_fusion.matrix_ref) | copy-start | bytes 786436
  65.4 2.7 %copy-start.3 = (s32[2]{0:T(128)S(1)}, s32[2]{0:T(128)}, u32[]{:S(2)}) copy-start(s32[2]{0:T(128)} %pad_add_fusion.base_ref) | copy-start | bytes 28
  72.1 2.4 copy-start
  74.5 34.9 %copy-start.2 = (f32[40,2,40,128]{3,2,1,0:T(8,128)}, f32[40,2,40,128]{3,2,1,0:T(8,128)S(1)}, u32[]{:S(2)}) copy-start(f32[40,2,40,128]{3,2,1,0:T(8,128)S(1)} %get-tuple-element.18.inverse_in) | copy-start | bytes 4915204
  74.5 28.3 %collective-permute-start.11 = (f32[28,40,256]{2,1,0:T(8,128)}, f32[28,40,256]{2,1,0:T(8,128)S(1)}, u32[]{:S(2)}, u32[]{:S(2)}) collective-permute-start(f32[28,40,256]{2,1,0:T(8,128)} %pad_maximum_fusion.7), channel_id=1, source_target_pairs={{16,0},{32,16},{48,32},{64,48},{80,64},{96,80},{112,96},{17,1},{33... | collective-permute-start | bytes 3440648 | tf_op jit(solution)/shard_map/ppermute | solution.py:408
  75.9 89.0 %collective-permute-start.12 = (f32[80,16,256]{2,1,0:T(8,128)}, f32[80,16,256]{2,1,0:T(8,128)}, u32[]{:S(2)}, u32[]{:S(2)}) collective-permute-start(f32[80,16,256]{2,1,0:T(8,128)} %pad_maximum_fusion.2), channel_id=1, source_target_pairs={{0,1},{1,2},{2,3},{3,4},{4,5},{5,6},{6,7},{7,8},{8,9},{9,10},{10,1... | collective-permute-start | bytes 3932168 | tf_op jit(solution)/shard_map/ppermute | solution.py:408
  80.4 36.1 %copy-start.4 = (s32[1024]{0:T(1024)S(1)}, s32[1024]{0:T(1024)}, u32[]{:S(2)}) copy-start(s32[1024]{0:T(1024)} %get-tuple-element.14.own_ref) | copy-start | bytes 12292
  80.4 36.1 %copy-start.5 = (s32[2]{0:T(128)S(1)}, s32[2]{0:T(128)}, u32[]{:S(2)}) copy-start(s32[2]{0:T(128)} %get-tuple-element.13.count_ref) | copy-start | bytes 28
  80.5 84.3 %collective-permute-start.13 = (f32[80,16,256]{2,1,0:T(8,128)}, f32[80,16,256]{2,1,0:T(8,128)}, u32[]{:S(2)}, u32[]{:S(2)}) collective-permute-start(f32[80,16,256]{2,1,0:T(8,128)} %pad_maximum_fusion.3), channel_id=1, source_target_pairs={{1,0},{2,1},{3,2},{4,3},{5,4},{6,5},{7,6},{8,7},{9,8},{10,9},{11,1... | collective-permute-start | bytes 3932168 | tf_op jit(solution)/shard_map/ppermute | solution.py:408
  102.8 46.8 %copy-start.12 = (f32[28,40,256]{2,1,0:T(8,128)}, f32[28,40,256]{2,1,0:T(8,128)S(1)}, u32[]{:S(2)}) copy-start(f32[28,40,256]{2,1,0:T(8,128)S(1)} %collective-permute-done.11.x_high) | copy-start | bytes 3440644
  102.8 9.4 %collective-permute-start.4 = (f32[48,8,256]{2,1,0:T(8,128)S(1)}, f32[48,8,256]{2,1,0:T(8,128)S(1)}, u32[]{:S(2)}, u32[]{:S(2)}) collective-permute-start(f32[48,8,256]{2,1,0:T(8,128)S(1)} %get-tuple-element.50), channel_id=1, source_target_pairs={{0,1},{1,2},{2,3},{3,4},{4,5},{5,6},{6,7},{7,8},{8,9},{9,10},{10,1... | collective-permute-start | bytes 1179656 | tf_op jit(solution)/shard_map/ppermute | solution.py:408
  107.5 9.1 %collective-permute-start.5 = (f32[48,8,256]{2,1,0:T(8,128)S(1)}, f32[48,8,256]{2,1,0:T(8,128)S(1)}, u32[]{:S(2)}, u32[]{:S(2)}) collective-permute-start(f32[48,8,256]{2,1,0:T(8,128)S(1)} %get-tuple-element.49), channel_id=1, source_target_pairs={{1,0},{2,1},{3,2},{4,3},{5,4},{6,5},{7,6},{8,7},{9,8},{10,9},{11,1... | collective-permute-start | bytes 1179656 | tf_op jit(solution)/shard_map/ppermute | solution.py:408
  144.3 7.6 %collective-permute-start.7 = (f32[4,8,128]{2,1,0:T(8,128)S(1)}, f32[4,8,128]{2,1,0:T(8,128)S(1)}, u32[]{:S(2)}, u32[]{:S(2)}) collective-permute-start(f32[4,8,128]{2,1,0:T(8,128)S(1)} %get-tuple-element.16), channel_id=1, source_target_pairs={{16,0},{32,16},{48,32},{64,48},{80,64},{96,80},{112,96},{17,1},{33... | collective-permute-start | bytes 49160 | tf_op jit(solution)/shard_map/ppermute | solution.py:408
  145.6 8.4 %collective-permute-start.6 = (f32[4,8,128]{2,1,0:T(8,128)S(1)}, f32[4,8,128]{2,1,0:T(8,128)S(1)}, u32[]{:S(2)}, u32[]{:S(2)}) collective-permute-start(f32[4,8,128]{2,1,0:T(8,128)S(1)} %get-tuple-element.16), channel_id=1, source_target_pairs={{0,16},{16,32},{32,48},{48,64},{64,80},{80,96},{96,112},{1,17},{17... | collective-permute-start | bytes 49160 | tf_op jit(solution)/shard_map/ppermute | solution.py:408
  149.6 15.3 %collective-permute-start.14 = (f32[48,8,256]{2,1,0:T(8,128)S(1)}, f32[48,8,256]{2,1,0:T(8,128)S(1)}, u32[]{:S(2)}, u32[]{:S(2)}) collective-permute-start(f32[48,8,256]{2,1,0:T(8,128)S(1)} %get-tuple-element.36), channel_id=1, source_target_pairs={{0,1},{1,2},{2,3},{3,4},{4,5},{5,6},{6,7},{7,8},{8,9},{9,10},{10,1... | collective-permute-start | bytes 1179656 | tf_op jit(solution)/shard_map/ppermute | solution.py:408
  151.9 13.0 %collective-permute-start.15 = (f32[48,8,256]{2,1,0:T(8,128)S(1)}, f32[48,8,256]{2,1,0:T(8,128)S(1)}, u32[]{:S(2)}, u32[]{:S(2)}) collective-permute-start(f32[48,8,256]{2,1,0:T(8,128)S(1)} %get-tuple-element.35), channel_id=1, source_target_pairs={{1,0},{2,1},{3,2},{4,3},{5,4},{6,5},{7,6},{8,7},{9,8},{10,9},{11,1... | collective-permute-start | bytes 1179656 | tf_op jit(solution)/shard_map/ppermute | solution.py:408
  154.0 7.2 %collective-permute-start.9 = (f32[4,8,128]{2,1,0:T(8,128)S(1)}, f32[4,8,128]{2,1,0:T(8,128)S(1)}, u32[]{:S(2)}, u32[]{:S(2)}) collective-permute-start(f32[4,8,128]{2,1,0:T(8,128)S(1)} %add_add_fusion), channel_id=1, source_target_pairs={{1,0},{2,1},{3,2},{4,3},{5,4},{6,5},{7,6},{8,7},{9,8},{10,9},{11,1... | collective-permute-start | bytes 49160 | tf_op jit(solution)/shard_map/ppermute | solution.py:408
  161.2 3.1 %collective-permute-start.8 = (f32[4,8,128]{2,1,0:T(8,128)S(1)}, f32[4,8,128]{2,1,0:T(8,128)S(1)}, u32[]{:S(2)}, u32[]{:S(2)}) collective-permute-start(f32[4,8,128]{2,1,0:T(8,128)S(1)} %add_add_fusion), channel_id=1, source_target_pairs={{0,1},{1,2},{2,3},{3,4},{4,5},{5,6},{6,7},{7,8},{8,9},{9,10},{10,1... | collective-permute-start | bytes 49160 | tf_op jit(solution)/shard_map/ppermute | solution.py:408
  (4 other events, 5.1 us)

commit v2 on v0

v2 whole, which is shorter than its diff:
```python
import jax
import jax.numpy as jnp
from jax import lax
from jax.experimental import pallas as pl
from jax.experimental.pallas import tpu as pltpu
from jax.sharding import PartitionSpec as P

ITERS = 4
OWN = 40
HALO = 20
EXT = OWN + 2 * HALO
TOP = 24
ROWS = 96
WIDE = 72
LANES = 128
CENTRE = -43050.0
RING = (8064.0, -1008.0, 128.0, -9.0)
SCALE = 0.01 / 5040.0
SMEM = pltpu.SMEM
VMEM = pltpu.VMEM
HBM = pltpu.HBM
EXACT = lax.Precision.HIGHEST


def params(mib):
    return pltpu.CompilerParams(vmem_limit_bytes=mib * 1024 * 1024)


def cost(flops, size):
    return pl.CostEstimate(flops=flops, bytes_accessed=size, transcendentals=0)


def spec(space):
    return pl.BlockSpec(memory_space=space)


def z_matrix():
    row = lax.broadcasted_iota(jnp.int32, (512, 256), 0) & 255
    column = lax.broadcasted_iota(jnp.int32, (512, 256), 1)
    distance = jnp.abs(row - column)
    result = jnp.zeros((512, 256), jnp.float32)
    for reach, value in enumerate(RING):
        result = jnp.where(distance == reach + 1, value, result)
    return result.astype(jnp.bfloat16)


def y_matrix(rows, window):
    row = lax.broadcasted_iota(jnp.int32, (rows, 2 * window), 0)
    column = lax.broadcasted_iota(jnp.int32, (rows, 2 * window), 1) % window
    distance = jnp.abs(column - 8 - row)
    result = jnp.zeros((rows, 2 * window), jnp.float32)
    for reach, value in enumerate(RING):
        result = jnp.where(distance == reach + 1, value, result)
    return result.astype(jnp.bfloat16)


def hat(fine, coarse, lower, limit, fraction):
    higher = jnp.minimum(lower + 1, limit)
    first = jnp.where(coarse == lower, 1.0 - fraction, 0.0)
    second = jnp.where(coarse == higher, fraction, 0.0)
    return first + second


def quarter(fine):
    return (fine & 3).astype(jnp.float32) * 0.25


def start_all(pairs, sem):
    started = [pltpu.make_async_copy(a, b, sem) for a, b in pairs]
    for copy in started:
        copy.start()
    return started


def wait_all(started):
    for copy in started:
        copy.wait()


def list_kernel(code_ref, own_ref, count_ref):
    def body(receiver, own):
        code = code_ref[receiver]
        own_ref[own] = code
        return own + lax.shift_right_logical(code, 31)

    count_ref[0] = lax.fori_loop(0, 1024, body, 0, unroll=16)


def receiver_codes(cells, base):
    x = cells[0] - base[0]
    y = cells[1] - base[1]
    own = (x >= 0) & (x < OWN) & (y >= 0) & (y < OWN)
    code = jnp.arange(1024, dtype=jnp.int32) | (cells[2] << 10)
    code = code | ((y & 63) << 18) | ((x & 63) << 24)
    return code | (own.astype(jnp.int32) << 31)


def unpack(code):
    receiver = code & 1023
    z = (code >> 10) & 255
    y = (code >> 18) & 63
    x = (code >> 24) & 63
    return receiver, x + HALO, y + TOP, z // LANES, z & (LANES - 1)


def model_pack_kernel(velocity_ref, out_ref):
    lane = lax.broadcasted_iota(jnp.int32, (8, LANES), 1)
    blocks = [velocity_ref[a] for a in range(5)]
    for j in range(16):
        tile = jnp.zeros((8, LANES), jnp.float32)
        for a in range(5):
            moved = pltpu.roll(blocks[a], (24 * a - 10 * j) % 256, 1)[:, :LANES]
            tile = jnp.where((lane >= 24 * a) & (lane < 24 * a + 24), moved, tile)
        for i in range(8):
            out_ref[i, j] = tile


def model_kernel(base_ref, model_ref, plane_out, plane_ref, sem):
    row = lax.broadcasted_iota(jnp.int32, (64, 256), 0)
    column = lax.broadcasted_iota(jnp.int32, (64, 256), 1)
    weight_z = hat(column, row, column // 4, 63, quarter(column))
    fine = lax.broadcasted_iota(jnp.int32, (ROWS, 24), 0)
    coarse = lax.broadcasted_iota(jnp.int32, (ROWS, 24), 1)
    limit_y = 159 - (base_ref[1] // 4 - 4)
    weight_y = hat(fine, coarse, fine // 4 - 2, limit_y, quarter(fine))
    place = fine + (base_ref[1] - TOP)
    weight_y = jnp.where((place >= 0) & (place < 640), weight_y, 0.0)
    first = 2 * (base_ref[0] // OWN) - 1
    for r in range(4):
        owner = jnp.clip(first + r, 0, 15)
        block = jnp.concatenate([model_ref[i, owner] for i in range(8)], axis=0)
        deep = jnp.dot(block.T, weight_z, precision=EXACT, preferred_element_type=jnp.float32)
        for a in range(5):
            plane = jnp.dot(
                weight_y, deep[24 * a : 24 * a + 24], precision=EXACT,
                preferred_element_type=jnp.float32,
            )
            plane_ref[5 * r + a, 0] = plane[:, :LANES]
            plane_ref[5 * r + a, 1] = plane[:, LANES:]
    wait_all(start_all([(plane_ref, plane_out)], sem))


def fill_courant(base_ref, plane_ref, courant_ref):
    limit_x = 79 - (base_ref[0] // 4 - 5)

    def group(a, carry):
        higher = jnp.minimum(a + 1, limit_x)
        start = base_ref[0] - HALO + 4 * a
        inside = ((start >= 0) & (start < 320)).astype(jnp.float32) * SCALE
        for half in range(2):
            for tile in range(1, 10):
                rows = pl.ds(8 * tile, 8)
                low = plane_ref[a, half, rows, :]
                high = plane_ref[higher, half, rows, :]
                for step in range(4):
                    speed = low * (1.0 - 0.25 * step) + high * (0.25 * step)
                    courant_ref[4 * a + step, half, rows, :] = speed * speed * inside
        return carry

    lax.fori_loop(1, 19, group, 0)


def clear(ref, planes, tiles):
    def body(x, carry):
        for half in range(2):
            for tile in tiles:
                ref[x, half, pl.ds(8 * tile, 8), :] = jnp.zeros((8, LANES), jnp.float32)
        return carry

    lax.fori_loop(planes[0], planes[1], body, 0)


def clear_edges(ref):
    outer = (0, 1, 2, 8, 9, 10, 11)
    clear(ref, (0, HALO), outer)
    clear(ref, (HALO, HALO + OWN), (0, 10, 11))
    clear(ref, (HALO + OWN, EXT), outer)


def copies(now, before, pieces, ext_now, ext_before):
    x_low, x_high, y_low, y_high, c_low, c_high = pieces
    result = []
    for half in range(2):
        lanes = pl.ds(half * LANES, LANES)

        def add(source, plane, count, row, rows, target, to_plane, to_row):
            result.append((
                source.at[pl.ds(plane, count), pl.ds(row, rows), lanes],
                target.at[pl.ds(to_plane, count), half, pl.ds(to_row, rows), :],
            ))

        add(now, 0, OWN, 0, OWN, ext_now, HALO, TOP)
        add(before, 0, OWN, 0, OWN, ext_before, HALO, TOP)
        for source, first, second in ((x_low, 0, 4), (x_high, 60, 60)):
            add(source, 0, 20, 0, OWN, ext_now, first, TOP)
            add(source, 20, 16, 0, OWN, ext_before, second, TOP)
        for source, first, second in ((y_low, 0, 8), (y_high, 64, 64)):
            add(source, 0, OWN, 0, 24, ext_now, HALO, first)
            add(source, 0, OWN, 24, 16, ext_before, HALO, second)
        for piece, near, far in ((c_low, 16, 8), (c_high, 64, 72)):
            for side, places in ((0, (4, 12, 8, 16)), (40, (60, 60, 60, 60))):
                add(piece, side, 16, 0, 8, ext_now, places[0], near)
                add(piece, side + 16, 8, 0, 8, ext_now, places[1], far)
                add(piece, side + 24, 12, 0, 8, ext_before, places[2], near)
                add(piece, side + 36, 4, 0, 8, ext_before, places[3], far)
    return result


def stencil_pass(source, z_ref, y_refs, along, step, emit):
    first = 4 * step
    top = 4 + 4 * step
    span = EXT - 8 * step
    tiles = span // 8
    y_ref, window_rows = ((y_refs[0], 96), (y_refs[1], 80), (y_refs[1], 80), (y_refs[2], 64))[
        step - 1
    ]

    def multiply(x):
        parts = []
        for g in range(4):
            plane = jnp.concatenate(
                [source[x + g, half, pl.ds(top - 8, window_rows), :] for half in range(2)], axis=1
            )
            upper = plane.astype(jnp.bfloat16)
            lower = (plane - upper.astype(jnp.float32)).astype(jnp.bfloat16)
            parts.append((upper, lower))
        stacked = jnp.concatenate(
            [jnp.concatenate([part[side] for part in parts], axis=0) for side in range(2)], axis=1
        )
        along_z = jnp.dot(stacked, z_ref[...], preferred_element_type=jnp.float32)
        for g in range(4):
            along_y = jnp.dot(
                y_ref[...], jnp.concatenate(parts[g], axis=0), preferred_element_type=jnp.float32
            )
            for tile in range(tiles):
                start = g * window_rows + 8 + 8 * tile
                total = along_z[start : start + 8] + along_y[8 * tile : 8 * tile + 8]
                for half in range(2):
                    along[g, half, pl.ds(8 * tile, 8), :] = total[
                        :, half * LANES : (half + 1) * LANES
                    ]

    multiply(first)

    def group(index, carry):
        x = first + 4 * index
        for tile in range(tiles):
            for half in range(2):
                row = top + 8 * tile
                window = [source[x - 4 + j, half, pl.ds(row, 8), :] for j in range(12)]
                for g in range(4):
                    total = along[g, half, pl.ds(8 * tile, 8), :] + CENTRE * window[4 + g]
                    for reach in range(1, 5):
                        pair = window[4 + g + reach] + window[4 + g - reach]
                        total = total + RING[reach - 1] * pair
                    emit(x + g, half, row, window[4 + g], total)
        multiply(x + 4)
        return carry

    lax.fori_loop(0, span // 4, group, 0)


def propagate_kernel(
    base_ref, source_ref, wavelet_ref, own_ref, count_ref, observed_ref,
    z_ref, y_ref_a, y_ref_b, y_ref_c,
    now, before, adjoint_now, adjoint_after, *refs,
):
    pieces, refs = refs[:6], refs[6:]
    (
        plane_in, out_ref,
        field_a, field_b, field_c, stage, courant, term_a, term_b, term_c, term_d,
        planes, along, picked, sems,
    ) = refs
    terms = (term_a, term_b, term_c, term_d)
    matrices = (y_ref_a, y_ref_b, y_ref_c)
    first = start_all([(plane_in, planes)], sems.at[0])
    clear_edges(field_a)
    clear_edges(field_b)
    loads = start_all(copies(now, before, pieces, field_b, field_a), sems.at[1])
    clear(field_c, (0, EXT), range(12))
    own = pl.ds(HALO, OWN)
    later = []
    for half in range(2):
        lanes = pl.ds(half * LANES, LANES)
        later += [
            (adjoint_now.at[:, :, lanes], field_c.at[own, half, pl.ds(TOP, OWN), :]),
            (adjoint_after.at[:, :, lanes], stage.at[:, half]),
        ]
    later = start_all(later, sems.at[2])
    clear(term_b, (0, 64), (0, 8))
    clear(term_d, (0, 48), (1, 7))
    wait_all(first)
    fill_courant(base_ref, planes, courant)
    wait_all(loads)
    lane = lax.broadcasted_iota(jnp.int32, (1, LANES), 1)
    number = count_ref[0]

    for step in range(1, ITERS + 1):
        target, newer = (field_a, field_b) if step % 2 else (field_b, field_a)
        term = terms[step - 1]
        origin = 4 * step
        span = EXT - 8 * step

        def emit(x, half, row, centre, total):
            rows = pl.ds(row, 8)
            term[x - origin, half, pl.ds(row - 8, 8), :] = total
            target[x, half, rows, :] = (
                centre + centre - target[x, half, rows, :] + courant[x, half, rows, :] * total
            )

        stencil_pass(newer, z_ref, matrices, along, step, emit)
        for source in range(4):
            x = source_ref[source] - (base_ref[0] - HALO)
            row = source_ref[4 + source] - (base_ref[1] - TOP)
            z = source_ref[8 + source]
            inside_x = (x >= origin) & (x < origin + span)
            inside_y = (row >= origin + 4) & (row < origin + 4 + span)

            @pl.when(inside_x & inside_y)
            def _():
                half = z // LANES
                added = jnp.where(
                    lane == (z & (LANES - 1)), wavelet_ref[4 * (step - 1) + source], 0.0
                )
                target[x, half, pl.ds(row, 1), :] += added
                term[x - origin, half, pl.ds(row - 8, 1), :] += (
                    added / courant[x, half, pl.ds(row, 1), :]
                )

        def sample(index, carry):
            for j in range(4):
                entry = 4 * index + j
                valid = entry < number
                code = jnp.where(valid, own_ref[jnp.minimum(entry, 1023)], 0)
                receiver, x, row, half, z = unpack(code)
                at_lane = lane == jnp.where(valid, z, -1)
                line = target[x, half, pl.ds(row, 1), :]
                seen = observed_ref[1024 * (step - 1) + receiver]
                picked[step - 1, pl.ds(entry, 1), :] = jnp.where(at_lane, line - seen, 0.0)
            return carry

        lax.fori_loop(0, (number + 3) // 4, sample, 0)

    clear(field_a, (0, EXT), range(12))
    clear(field_b, (0, EXT), range(12))
    wait_all(later)

    def scale(index, carry):
        x = index + HALO
        for half in range(2):
            for tile in range(5):
                rows = pl.ds(TOP + 8 * tile, 8)
                factor = courant[x, half, rows, :]
                field_c[x, half, rows, :] = field_c[x, half, rows, :] * factor
                field_a[x, half, rows, :] = stage[index, half, pl.ds(8 * tile, 8), :] * factor
        return carry

    lax.fori_loop(0, OWN, scale, 0)
    chain = ((field_c, field_a, field_a), (field_a, field_c, field_c), (field_c, field_a, field_b))
    for step in range(ITERS, 1, -1):
        newer, older, target = chain[ITERS - step]

        def emit(x, half, row, centre, total):
            rows = pl.ds(row, 8)
            target[x, half, rows, :] = (
                centre + centre - older[x, half, rows, :] + courant[x, half, rows, :] * total
            )

        stencil_pass(newer, z_ref, matrices, along, step, emit)

        def inject(entry, carry):
            _, x, row, half, _ = unpack(own_ref[entry])
            rows = pl.ds(row, 1)
            target[x, half, rows, :] += (
                courant[x, half, rows, :] * picked[step - 1, pl.ds(entry, 1), :]
            )
            return carry

        lax.fori_loop(0, number, inject, 0)

    def prepare(entry, carry):
        _, x, row, half, _ = unpack(own_ref[entry])
        rows = pl.ds(row, 1)
        picked[0, pl.ds(entry, 1), :] = (
            picked[0, pl.ds(entry, 1), :]
            * courant[x, half, rows, :]
            * term_a[x - 4, half, pl.ds(row - 8, 1), :]
        )
        return carry

    lax.fori_loop(0, number, prepare, 0)

    def emit(x, half, row, centre, total):
        rows, place = pl.ds(row, 8), pl.ds(row - 8, 8)
        value = centre + centre - field_c[x, half, rows, :] + courant[x, half, rows, :] * total
        term_a[x - 4, half, place, :] = value * term_a[x - 4, half, place, :]

    stencil_pass(field_b, z_ref, matrices, along, 1, emit)

    def finish(entry, carry):
        _, x, row, half, _ = unpack(own_ref[entry])
        term_a[x - 4, half, pl.ds(row - 8, 1), :] += picked[0, pl.ds(entry, 1), :]
        return carry

    lax.fori_loop(0, number, finish, 0)

    coarse = planes
    clear(coarse, (0, 20), range(9))
    limit_x = 79 - (base_ref[0] // 4 - 4)

    def image(a, carry):
        higher = jnp.clip(limit_x, 0, a + 1)
        for half in range(2):
            for tile in range(9):
                rows, place = pl.ds(8 + 8 * tile, 8), pl.ds(8 * tile, 8)
                low, high = None, None
                for g in range(4):
                    x = 4 + 4 * a + g
                    total = term_a[x - 4, half, place, :] + (
                        field_b[x, half, rows, :]
                        * term_b[jnp.clip(x - 8, 0, 63), half, place, :]
                    )
                    if 0 < tile < 8:
                        total = total + (
                            field_c[x, half, rows, :]
                            * term_c[jnp.clip(x - 12, 0, 55), half, place, :]
                        )
                        total = total + (
                            field_a[x, half, rows, :]
                            * term_d[jnp.clip(x - 16, 0, 47), half, place, :]
                        )
                    total = total * lax.rsqrt(jnp.maximum(courant[x, half, rows, :], 1e-9))
                    weight = 0.25 * g
                    low = total if low is None else low + (1.0 - weight) * total
                    if g:
                        part = weight * total
                        high = part if high is None else high + part
                coarse[a, half, place, :] += low
                coarse[higher, half, place, :] += high
        return carry

    lax.fori_loop(0, 18, image, 0)
    row = lax.broadcasted_iota(jnp.int32, (24, WIDE), 0)
    fine = lax.broadcasted_iota(jnp.int32, (24, WIDE), 1)
    limit_y = 159 - (base_ref[1] // 4 - 4)
    weight_y = hat(fine, row, fine // 4, limit_y, quarter(fine))
    column = lax.broadcasted_iota(jnp.int32, (64, 256), 0)
    fine = lax.broadcasted_iota(jnp.int32, (64, 256), 1)
    weight_z = hat(fine, column, fine // 4, 63, quarter(fine))
    parts = [jnp.zeros((24, 256), jnp.float32)]
    for a in range(19):
        plane = jnp.concatenate(
            [coarse[a, half, pl.ds(0, WIDE), :] for half in range(2)], axis=1
        )
        parts.append(
            jnp.dot(weight_y, plane, precision=EXACT, preferred_element_type=jnp.float32)
        )
    parts.append(jnp.zeros((32, 256), jnp.float32))
    result = (0.125 * 2.0 * SCALE**0.5) * lax.dot_general(
        weight_z, jnp.concatenate(parts, axis=0), (((1,), (1,)), ((), ())),
        precision=EXACT, preferred_element_type=jnp.float32,
    )
    out_ref[...] = jnp.zeros(out_ref.shape, jnp.float32)
    index = base_ref[0] // OWN
    for piece in range(4):
        owner = 2 * index - 1 + piece

        @pl.when((owner >= 0) & (owner < 16))
        def _():
            moved = pltpu.roll(result, (512 - 120 * piece) % 512, 1) if piece else result
            for i in range(8):
                out_ref[i, owner] = moved[8 * i : 8 * i + 8, :LANES]


def gather_kernel(base_ref, parts_ref, out_ref):
    wide = lax.broadcasted_iota(jnp.int32, (8, 256), 1)
    index = base_ref[1] // OWN
    one = index // 2
    other = jnp.where(index % 2 == 0, one - 1, one + 1)
    valid = (other >= 0) & (other < 8)
    other = jnp.clip(other, 0, 7)
    sums = [jnp.zeros((8, 256), jnp.float32) for _ in range(5)]
    for j in range(16):
        tile = parts_ref[one, j] + jnp.where(valid, parts_ref[other, j], 0.0)
        tile = jnp.concatenate([tile, jnp.zeros((8, LANES), jnp.float32)], axis=1)
        inside = (wide >= 10 * j - 4) & (wide < 10 * j + 15)
        for r in range(5):
            moved = pltpu.roll(tile, (10 * j - 4 - 24 * r) % 256, 1)
            sums[r] = sums[r] + jnp.where(inside, moved, 0.0)
    for r in range(5):
        out_ref[r] = sums[r]


def face_kernel(now, before, *refs):
    outs, stages, sem = refs[:4], refs[4:8], refs[8]
    pairs = []
    for side, (first, second, strip_first) in enumerate(((20, 24, 16), (0, 0, 0))):
        face, strip = stages[side], stages[2 + side]
        pairs += [
            (now.at[pl.ds(first, 20)], face.at[pl.ds(0, 20)]),
            (before.at[pl.ds(second, 16)], face.at[pl.ds(20, 16)]),
            (now.at[:, pl.ds(strip_first, 24)], strip.at[:, pl.ds(0, 24)]),
            (before.at[:, pl.ds(second, 16)], strip.at[:, pl.ds(24, 16)]),
        ]
    wait_all(start_all(pairs, sem))
    wait_all(start_all(list(zip(stages, outs)), sem))


def corner_kernel(x_low, x_high, up, down, stage_up, stage_down, sem):
    pairs = []
    for target, near, far in ((stage_up, 32, 24), (stage_down, 0, 8)):
        for piece, start, places in ((x_low, 0, (4, 12, 24, 32)), (x_high, 40, (0, 0, 20, 20))):
            place = start
            for plane, row, count in zip(places, (near, far, near, far), (16, 8, 12, 4)):
                pairs.append((
                    piece.at[pl.ds(plane, count), pl.ds(row, 8)],
                    target.at[pl.ds(place, count)],
                ))
                place += count
    wait_all(start_all(pairs, sem))
    wait_all(start_all([(stage_up, up), (stage_down, down)], sem))


def gate_kernel(*refs):
    pass


def gate(arrays, tokens):
    return pl.pallas_call(
        gate_kernel,
        out_shape=tuple(jax.ShapeDtypeStruct(a.shape, a.dtype) for a in arrays),
        in_specs=[spec(HBM)] * len(arrays) + [spec(pl.ANY)] * len(tokens),
        out_specs=(spec(HBM),) * len(arrays),
        input_output_aliases={i: i for i in range(len(arrays))},
        cost_estimate=cost(1000, 1000),
    )(*arrays, *tokens)


def shifts(axis, block_up, block_down):
    count = lax.axis_size(axis)
    up = [(i, i + 1) for i in range(count - 1)]
    down = [(i + 1, i) for i in range(count - 1)]
    return lax.ppermute(block_up, axis, up), lax.ppermute(block_down, axis, down)


def staged(kernel, shapes, operands, size):
    shapes = tuple(jax.ShapeDtypeStruct(shape, jnp.float32) for shape in shapes)
    return pl.pallas_call(
        kernel,
        out_shape=shapes,
        in_specs=[spec(HBM)] * len(operands),
        out_specs=(spec(HBM),) * len(shapes),
        scratch_shapes=[VMEM(shape.shape, shape.dtype) for shape in shapes]
        + [pltpu.SemaphoreType.DMA],
        cost_estimate=cost(1000, size),
    )(*operands)


def per_device(
    velocity, forward_now, forward_before, adjoint_now, adjoint_after,
    source_cells, receiver_cells, wavelet, observed,
):
    index_x = lax.axis_index("gx")
    index_y = lax.axis_index("gy")
    base = jnp.stack([index_x * OWN, index_y * OWN]).astype(jnp.int32)
    everywhere = ("gx", "gy")
    buffer = jax.ShapeDtypeStruct((8, 16, 8, LANES), jnp.float32)

    turned = jnp.pad(velocity.transpose(0, 2, 1), ((0, 0), (0, 0), (4, 92)))
    windows = pl.pallas_call(
        model_pack_kernel,
        out_shape=buffer,
        in_specs=[spec(VMEM)],
        out_specs=spec(VMEM),
        cost_estimate=cost(100_000, 600_000),
    )(turned)
    model = lax.all_to_all(windows.reshape(128, 8, LANES), everywhere, 0, 0, tiled=True)
    model = model.reshape(8, 16, 8, LANES)

    own_list, counts = pl.pallas_call(
        list_kernel,
        out_shape=(
            jax.ShapeDtypeStruct((1024,), jnp.int32),
            jax.ShapeDtypeStruct((1,), jnp.int32),
        ),
        in_specs=[spec(SMEM)],
        out_specs=(spec(SMEM),) * 2,
        cost_estimate=cost(10_000_000, 20_000_000),
    )(receiver_codes(receiver_cells, base))

    faces = staged(
        face_kernel, ((36, OWN, 256),) * 2 + ((OWN, 40, 256),) * 2,
        (forward_now, forward_before), 9_000_000,
    )
    x_up, x_down, y_up, y_down = gate(faces, (windows,))
    x_low, x_high = shifts("gx", x_up, x_down)
    y_low, y_high = shifts("gy", y_up, y_down)

    plane_shape = (20, 2, ROWS, LANES)
    planes = pl.pallas_call(
        model_kernel,
        out_shape=jax.ShapeDtypeStruct(plane_shape, jnp.float32),
        in_specs=[spec(SMEM), spec(VMEM)],
        out_specs=spec(HBM),
        scratch_shapes=[VMEM(plane_shape, jnp.float32), pltpu.SemaphoreType.DMA],
        compiler_params=params(32),
        cost_estimate=cost(10_000_000, 10_000_000),
    )(base, model)

    corners = staged(corner_kernel, ((80, 8, 256),) * 2, (x_low, x_high), 2_000_000)
    c_low, c_high = shifts("gy", *corners)

    field = VMEM((EXT, 2, ROWS, LANES), jnp.float32)
    parts = pl.pallas_call(
        propagate_kernel,
        out_shape=buffer,
        in_specs=[spec(SMEM)] * 6 + [spec(VMEM)] * 4 + [spec(HBM)] * 11,
        out_specs=spec(VMEM),
        scratch_shapes=[
            field, field, field,
            VMEM((OWN, 2, OWN, LANES), jnp.float32),
            field,
            *(VMEM((EXT - 8 * s, 2, WIDE, LANES), jnp.float32) for s in range(1, 5)),
            VMEM(plane_shape, jnp.float32),
            VMEM((4, 2, WIDE, LANES), jnp.float32),
            VMEM((ITERS, 1024, LANES), jnp.float32),
            pltpu.SemaphoreType.DMA((3,)),
        ],
        compiler_params=params(60),
        cost_estimate=cost(200_000_000, 30_000_000),
    )(
        base, source_cells.reshape(-1), wavelet.reshape(-1), own_list, counts,
        observed.reshape(-1), z_matrix(), y_matrix(80, 96), y_matrix(64, 80), y_matrix(48, 64),
        forward_now, forward_before, adjoint_now, adjoint_after,
        x_low, x_high, y_low, y_high, c_low, c_high, planes,
    )

    parts = lax.all_to_all(parts.reshape(128, 8, LANES), everywhere, 0, 0, tiled=True)
    grid = pl.pallas_call(
        gather_kernel,
        out_shape=jax.ShapeDtypeStruct((5, 8, 256), jnp.float32),
        in_specs=[spec(SMEM), spec(VMEM)],
        out_specs=spec(VMEM),
        cost_estimate=cost(100_000, 600_000),
    )(base, parts.reshape(8, 16, 8, LANES))
    return grid[:, :, :160].transpose(0, 2, 1)


def solution(mesh):
    return jax.shard_map(
        per_device,
        mesh=mesh,
        in_specs=(
            P("gy", None, "gx"),
            P("gx", "gy", None),
            P("gx", "gy", None),
            P("gx", "gy", None),
            P("gx", "gy", None),
            P(),
            P(),
            P(),
            P(),
        ),
        out_specs=P("gy", None, "gx"),
        check_vma=False,
    )
```

time: 824 us -> 174 us (0.21); the launches traced: 810 us -> 173 us
  other arithmetic: 310 us -> 3.66 us
  local copies, waits for them, and re-layouts: 227 us -> 8.08 us
  starting transfers between devices: 120 us -> 32.4 us
  Pallas kernels: 0 us -> 80 us
  waiting for transfers between devices: 99.1 us -> 25.4 us
  between operations: 14.9 us -> 0.24 us
  matrix products: 14.6 us -> 0 us
    gather x6 -> x0, local copies, waits for them, and re-layouts: 152 us -> none  [the longest x4 149 us: per_device(): sampled = field_after.reshape(-1)[receiver_flat]]
    mul x13 -> x0, other arithmetic: 101 us -> none  [the longest x4 87 us: per_device(): accel = courant * stencil(field_now)]
    add x8 -> x0, other arithmetic: 94.3 us -> none  [the longest x4 81.6 us: laplacian(): result_sum = result_sum + COEFFS[reach] * pairs]
    ppermute x32 -> x6, starting transfers between devices: 107 us -> 21.1 us  [the longest x3 16 us: shifts(): lax.ppermute(block_up, axis, up)]
    pallas_call x0 -> x8, Pallas kernels: none -> 80 us  [the longest x1 60.9 us: per_device(): pl.pallas_call(propagate_kernel, out_shape=buffer, in_specs=[spec(SMEM)]...]
    concatenate x24 -> x0, other arithmetic: 67.2 us -> none  [padded_2(): block = jnp.concatenate([low, block, high], axis=dim)]
    scatter-add x10 -> x0, other arithmetic: 46.4 us -> none  [the longest x4 29.9 us: per_device(): change = change.reshape(-1).at[receiver_flat].add(residual_list[section])...]
    all_gather x1 -> x0, waiting for transfers between devices: 35.2 us -> none  [per_device(): whole_model = lax.all_gather(deep_model, 'gy', axis=0, tiled=True)]
  transfers between devices with their start and end apart: 35 -> 7, of which waited for: 20 -> 3; matrix products, arithmetic and copies ran while one was open for 26% -> 3% of each run, Pallas kernels for 0% -> 6%
where the time goes in v2:
time: 174 us; the launch traced here: 173 us
  Pallas kernels  80 us (46%)
  starting transfers between devices  32.4 us (19%)
  waiting for transfers between devices  25.4 us (15%)
  blocking collectives  23.3 us (13%)
  local copies, waits for them, and re-layouts  8.08 us (5%)
  other arithmetic  3.66 us (2%)
    pallas_call x1, Pallas kernels, per_device(): pl.pallas_call(propagate_kernel, out_shape=buffer, in_specs=[spec(SMEM)]...  60.9 us
    all_to_all x1, blocking collectives, per_device(): lax.all_to_all(parts.reshape(128, 8, LANES), everywhere, 0, 0, tiled=True)  23.3 us
    ppermute x3, starting transfers between devices, shifts(): lax.ppermute(block_up, axis, up)  16 us
    all_to_all x1, waiting for transfers between devices, per_device(): lax.all_to_all(windows.reshape(128, 8, LANES), everywhere, 0, 0, tiled=True)  13.8 us
    all_to_all x1, starting transfers between devices, per_device(): lax.all_to_all(windows.reshape(128, 8, LANES), everywhere, 0, 0, tiled=True)  11.3 us
    pallas_call x2, Pallas kernels, staged(): pl.pallas_call(kernel, out_shape=shapes, in_specs=[spec(HBM)] * len(opera...  8.18 us
    ppermute x3, waiting for transfers between devices, shifts(): lax.ppermute(block_up, axis, up)  6.15 us
    ppermute x3, waiting for transfers between devices, shifts(): lax.ppermute(block_down, axis, down)  5.43 us
  transfers between devices with their start and end apart: 7, of which 3 were waited for; matrix products, arithmetic and copies ran while one was open for 3% of the time, Pallas kernels for 6%

profile of v2, /device:TPU:1, one launch (start us, length us, event | category | flops | bytes accessed | tf_op | source)
XLA Modules:
  0.0 173.1 jit_solution(5938529824635225303)
XLA Ops:
  0.0 1.5 pad.4.velocity_ref
  1.5 1.8 %shard_map.93.refs_4_ = f32[8,16,8,128]{3,2,1,0:T(8,128)} custom-call(f32[5,8,256]{2,1,0:T(8,128)} %pad.4.velocity_ref), custom_call_target="tpu_custom_call" | custom-call | flops 100000 | bytes 600000 | tf_op jit(solution)/shard_map/pallas_call | solution.py:570
  3.3 5.7 %shard_map.92 = (f32[36,40,256]{2,1,0:T(8,128)}, f32[36,40,256]{2,1,0:T(8,128)}, f32[40,40,256]{2,1,0:T(8,128)}, f32[40,40,256]{2,1,0:T(8,128)}) custom-call(f32[40,40,256]{2,1,0:T(8,128)} %now.3, f32[40,40,256]{2,1,0:T(8,128)} %before.3), custom_call_target="tpu_custom_call" | custom-call | flops 1000 | bytes 9000000 | tf_op jit(solution)/shard_map/pallas_call | solution.py:548
  9.0 4.1 %collective-permute-start = (f32[36,40,256]{2,1,0:T(8,128)}, f32[36,40,256]{2,1,0:T(8,128)S(1)}, u32[]{:S(2)}, u32[]{:S(2)}) collective-permute-start(f32[36,40,256]{2,1,0:T(8,128)} %get-tuple-element.23), channel_id=1, source_target_pairs={{0,16},{16,32},{32,48},{48,64},{64,80},{80,96},{96,112},{1,17},{17... | collective-permute-start | bytes 4423688 | tf_op jit(solution)/shard_map/ppermute | solution.py:543
  13.1 1.3 collective-permute-start.1
  14.4 4.4 %collective-permute-start.2 = (f32[40,40,256]{2,1,0:T(8,128)}, f32[40,40,256]{2,1,0:T(8,128)}, u32[]{:S(2)}, u32[]{:S(2)}) collective-permute-start(f32[40,40,256]{2,1,0:T(8,128)} %get-tuple-element.25), channel_id=1, source_target_pairs={{0,1},{1,2},{2,3},{3,4},{4,5},{5,6},{6,7},{7,8},{8,9},{9,10},{10,1... | collective-permute-start | bytes 4915208 | tf_op jit(solution)/shard_map/ppermute | solution.py:543
  18.8 1.9 %collective-permute-start.3 = (f32[40,40,256]{2,1,0:T(8,128)}, f32[40,40,256]{2,1,0:T(8,128)}, u32[]{:S(2)}, u32[]{:S(2)}) collective-permute-start(f32[40,40,256]{2,1,0:T(8,128)} %get-tuple-element.26), channel_id=1, source_target_pairs={{1,0},{2,1},{3,2},{4,3},{5,4},{6,5},{7,6},{8,7},{9,8},{10,9},{11,1... | collective-permute-start | bytes 4915208 | tf_op jit(solution)/shard_map/ppermute | solution.py:543
  20.8 11.3 %all-to-all-start = ((f32[128,8,128]{2,1,0:T(8,128)}), f32[128,8,128]{2,1,0:T(8,128)S(1)}, u32[]{:S(2)}, u32[]{:S(2)}) async-start(f32[128,8,128]{2,1,0:T(8,128)} %bitcast.18), calls=%async_computation | async-start | bytes 1048576 | tf_op jit(solution)/shard_map/all_to_all | solution.py:577
  32.1 0.6 copy.16
  32.7 0.7 reshape.45.source_ref
  33.4 0.7 reshape.46.wavelet_ref
  34.1 0.6 or_or_fusion.code_ref
  34.7 3.2 %shard_map.91 = (s32[1024]{0:T(1024)}, s32[1]{0:T(128)}) custom-call(s32[1024]{0:T(1024)} %or_or_fusion.code_ref), custom_call_target="tpu_custom_call" | custom-call | flops 10000000 | bytes 20000000 | tf_op jit(solution)/shard_map/pallas_call | solution.py:580
  38.0 0.6 select_convert_fusion.3.y_ref_c
  38.6 0.6 select_convert_fusion.2.y_ref_b
  39.3 6.1 %collective-permute-done.x_low.refs_0_ = f32[36,40,256]{2,1,0:T(8,128)S(1)} collective-permute-done((f32[36,40,256]{2,1,0:T(8,128)}, f32[36,40,256]{2,1,0:T(8,128)S(1)}, u32[]{:S(2)}, u32[]{:S(2)}) %collective-permute-start) | collective-permute-done | bytes 1474592 | tf_op jit(solution)/shard_map/ppermute | solution.py:543
  45.4 5.4 %collective-permute-done.1.x_high.refs_1_ = f32[36,40,256]{2,1,0:T(8,128)S(1)} collective-permute-done((f32[36,40,256]{2,1,0:T(8,128)}, f32[36,40,256]{2,1,0:T(8,128)S(1)}, u32[]{:S(2)}, u32[]{:S(2)}) %collective-permute-start.1) | collective-permute-done | bytes 1474592 | tf_op jit(solution)/shard_map/ppermute | solution.py:543
  50.9 1.1 copy-done.3
  52.0 2.5 %shard_map.95 = (f32[80,8,256]{2,1,0:T(8,128)}, f32[80,8,256]{2,1,0:T(8,128)}) custom-call(f32[36,40,256]{2,1,0:T(8,128)} %copy-done.2, f32[36,40,256]{2,1,0:T(8,128)} %copy-done.3), custom_call_target="tpu_custom_call" | custom-call | flops 1000 | bytes 2000000 | tf_op jit(solution)/shard_map/pallas_call | solution.py:548
  54.5 7.4 %collective-permute-start.4 = (f32[80,8,256]{2,1,0:T(8,128)}, f32[80,8,256]{2,1,0:T(8,128)S(1)}, u32[]{:S(2)}, u32[]{:S(2)}) collective-permute-start(f32[80,8,256]{2,1,0:T(8,128)} %get-tuple-element.27), channel_id=1, source_target_pairs={{0,1},{1,2},{2,3},{3,4},{4,5},{5,6},{6,7},{7,8},{8,9},{9,10},{10,1... | collective-permute-start | bytes 1966088 | tf_op jit(solution)/shard_map/ppermute | solution.py:543
  62.0 1.9 %collective-permute-start.5 = (f32[80,8,256]{2,1,0:T(8,128)}, f32[80,8,256]{2,1,0:T(8,128)}, u32[]{:S(2)}, u32[]{:S(2)}) collective-permute-start(f32[80,8,256]{2,1,0:T(8,128)} %get-tuple-element.28), channel_id=1, source_target_pairs={{1,0},{2,1},{3,2},{4,3},{5,4},{6,5},{7,6},{8,7},{9,8},{10,9},{11,1... | collective-permute-start | bytes 1966088 | tf_op jit(solution)/shard_map/ppermute | solution.py:543
  63.9 0.1 pad_add_fusion.base_ref
  64.0 0.7 select_convert_fusion.1.y_ref_a
  64.6 1.0 select_convert_fusion.z_ref
  65.6 13.8 %all-to-all-done = f32[128,8,128]{2,1,0:T(8,128)S(1)} async-done(((f32[128,8,128]{2,1,0:T(8,128)}), f32[128,8,128]{2,1,0:T(8,128)S(1)}, u32[]{:S(2)}, u32[]{:S(2)}) %all-to-all-start) | async-done | bytes 524320 | tf_op jit(solution)/shard_map/all_to_all | solution.py:577
  79.5 4.0 %shard_map.96.refs_6_ = f32[20,2,96,128]{3,2,1,0:T(8,128)S(1)} custom-call(s32[2]{0:T(128)S(1)} %pad_add_fusion.base_ref, f32[8,16,8,128]{3,2,1,0:T(8,128)S(1)} %bitcast.17), custom_call_target="tpu_custom_call" | custom-call | flops 10000000 | bytes 10000000 | tf_op jit(solution)/shard_map/pallas_call | solution.py:600
  83.5 1.3 copy-done
  84.8 0.8 copy-done.4
  85.6 60.9 %shard_map.97 = f32[8,16,8,128]{3,2,1,0:T(8,128)} custom-call(s32[2]{0:T(128)} %copy-done.1, s32[12]{0:T(128)} %reshape.45.source_ref, f32[16]{0:T(128)} %reshape.46.wavelet_ref, s32[1024]{0:T(1024)} %get-tuple-element.17.own_ref, s32[1]{0:T(128)} %get-tuple-element.18.count_ref, f32[4096]{0:T(1024)} %bitcast.21, bf16[512,256]{1,0:T(8,128)(2,1)} %select_convert_fusion.z_ref, ...), custom_call_target="tpu_custom_call" | custom-call | flops 200000000 | bytes 30000000 | tf_op jit(solution)/shard_map/pallas_call | solution.py:614
  146.5 23.3 %all_to_all.10 = f32[128,8,128]{2,1,0:T(8,128)} all-to-all(f32[128,8,128]{2,1,0:T(8,128)} %bitcast.19), channel_id=1, replica_groups=mesh['gx'=8,'gy'=16] {'gx','gy'}, dimensions={0} | all-to-all | bytes 1048576 | tf_op jit(solution)/shard_map/all_to_all | solution.py:638
  169.8 1.9 %shard_map.98 = f32[5,8,256]{2,1,0:T(8,128)} custom-call(s32[2]{0:T(128)} %copy-done.1, f32[8,16,8,128]{3,2,1,0:T(8,128)} %bitcast.20), custom_call_target="tpu_custom_call" | custom-call | flops 100000 | bytes 600000 | tf_op jit(solution)/shard_map/pallas_call | solution.py:639
  171.7 1.4 slice_bitcast_fusion
  (28 shorter events, 0.1 us)
Async XLA Ops:
  9.0 23.2 %copy-start.5 = (f32[4,1024]{1,0:T(4,128)S(1)}, f32[4,1024]{1,0:T(4,128)}, u32[]{:S(2)}) copy-start(f32[4,1024]{1,0:T(4,128)} %param.17) | copy-start | bytes 49156
  9.0 23.8 %copy-start.7 = (s32[3,4]{1,0:T(4,128)S(1)}, s32[3,4]{1,0:T(4,128)}, u32[]{:S(2)}) copy-start(s32[3,4]{1,0:T(4,128)} %param.14) | copy-start | bytes 148
  9.0 24.4 %copy-start.8 = (f32[4,4]{1,0:T(4,128)S(1)}, f32[4,4]{1,0:T(4,128)}, u32[]{:S(2)}) copy-start(f32[4,4]{1,0:T(4,128)} %param.16) | copy-start | bytes 196
  9.0 25.1 %copy-start.6 = (s32[3,1024]{1,0:T(4,128)S(1)}, s32[3,1024]{1,0:T(4,128)}, u32[]{:S(2)}) copy-start(s32[3,1024]{1,0:T(4,128)} %param.15) | copy-start | bytes 36868
  9.0 36.4 %collective-permute-start = (f32[36,40,256]{2,1,0:T(8,128)}, f32[36,40,256]{2,1,0:T(8,128)S(1)}, u32[]{:S(2)}, u32[]{:S(2)}) collective-permute-start(f32[36,40,256]{2,1,0:T(8,128)} %get-tuple-element.23), channel_id=1, source_target_pairs={{0,16},{16,32},{32,48},{48,64},{64,80},{80,96},{96,112},{1,17},{17... | collective-permute-start | bytes 4423688 | tf_op jit(solution)/shard_map/ppermute | solution.py:543
  13.1 37.7 %collective-permute-start.1 = (f32[36,40,256]{2,1,0:T(8,128)}, f32[36,40,256]{2,1,0:T(8,128)S(1)}, u32[]{:S(2)}, u32[]{:S(2)}) collective-permute-start(f32[36,40,256]{2,1,0:T(8,128)} %get-tuple-element.24), channel_id=1, source_target_pairs={{16,0},{32,16},{48,32},{64,48},{80,64},{96,80},{112,96},{17,1},{33... | collective-permute-start | bytes 4423688 | tf_op jit(solution)/shard_map/ppermute | solution.py:543
  14.4 70.3 %collective-permute-start.2 = (f32[40,40,256]{2,1,0:T(8,128)}, f32[40,40,256]{2,1,0:T(8,128)}, u32[]{:S(2)}, u32[]{:S(2)}) collective-permute-start(f32[40,40,256]{2,1,0:T(8,128)} %get-tuple-element.25), channel_id=1, source_target_pairs={{0,1},{1,2},{2,3},{3,4},{4,5},{5,6},{6,7},{7,8},{8,9},{9,10},{10,1... | collective-permute-start | bytes 4915208 | tf_op jit(solution)/shard_map/ppermute | solution.py:543
  18.8 65.9 %collective-permute-start.3 = (f32[40,40,256]{2,1,0:T(8,128)}, f32[40,40,256]{2,1,0:T(8,128)}, u32[]{:S(2)}, u32[]{:S(2)}) collective-permute-start(f32[40,40,256]{2,1,0:T(8,128)} %get-tuple-element.26), channel_id=1, source_target_pairs={{1,0},{2,1},{3,2},{4,3},{5,4},{6,5},{7,6},{8,7},{9,8},{10,9},{11,1... | collective-permute-start | bytes 4915208 | tf_op jit(solution)/shard_map/ppermute | solution.py:543
  20.8 58.7 %all-to-all-start = ((f32[128,8,128]{2,1,0:T(8,128)}), f32[128,8,128]{2,1,0:T(8,128)S(1)}, u32[]{:S(2)}, u32[]{:S(2)}) async-start(f32[128,8,128]{2,1,0:T(8,128)} %bitcast.18), calls=%async_computation | async-start | bytes 1048576 | tf_op jit(solution)/shard_map/all_to_all | solution.py:577
  45.4 5.4 %copy-start.2 = (f32[36,40,256]{2,1,0:T(8,128)}, f32[36,40,256]{2,1,0:T(8,128)S(1)}, u32[]{:S(2)}) copy-start(f32[36,40,256]{2,1,0:T(8,128)S(1)} %collective-permute-done.x_low.refs_0_) | copy-start | bytes 4423684
  50.9 1.1 copy-start.3
  54.5 30.3 %collective-permute-start.4 = (f32[80,8,256]{2,1,0:T(8,128)}, f32[80,8,256]{2,1,0:T(8,128)S(1)}, u32[]{:S(2)}, u32[]{:S(2)}) collective-permute-start(f32[80,8,256]{2,1,0:T(8,128)} %get-tuple-element.27), channel_id=1, source_target_pairs={{0,1},{1,2},{2,3},{3,4},{4,5},{5,6},{6,7},{7,8},{8,9},{9,10},{10,1... | collective-permute-start | bytes 1966088 | tf_op jit(solution)/shard_map/ppermute | solution.py:543
  62.0 22.8 %collective-permute-start.5 = (f32[80,8,256]{2,1,0:T(8,128)}, f32[80,8,256]{2,1,0:T(8,128)}, u32[]{:S(2)}, u32[]{:S(2)}) collective-permute-start(f32[80,8,256]{2,1,0:T(8,128)} %get-tuple-element.28), channel_id=1, source_target_pairs={{1,0},{2,1},{3,2},{4,3},{5,4},{6,5},{7,6},{8,7},{9,8},{10,9},{11,1... | collective-permute-start | bytes 1966088 | tf_op jit(solution)/shard_map/ppermute | solution.py:543
  64.0 20.8 %copy-start.1 = (s32[2]{0:T(128)}, s32[2]{0:T(128)S(1)}, u32[]{:S(2)}) copy-start(s32[2]{0:T(128)S(1)} %pad_add_fusion.base_ref) | copy-start | bytes 28
  83.5 1.3 copy-start
  84.8 0.9 copy-start.4

commit v3 on v2

--- a/solution.py
+++ b/solution.py
@@ -8,6 +8,7 @@
 ITERS = 4
 OWN = 40
 HALO = 20
+SPLIT = 40
 EXT = OWN + 2 * HALO
 TOP = 24
 ROWS = 96
@@ -35,10 +36,10 @@
 
 
 def z_matrix():
-    row = lax.broadcasted_iota(jnp.int32, (512, 256), 0) & 255
-    column = lax.broadcasted_iota(jnp.int32, (512, 256), 1)
+    row = lax.broadcasted_iota(jnp.int32, (256, 256), 0)
+    column = lax.broadcasted_iota(jnp.int32, (256, 256), 1)
     distance = jnp.abs(row - column)
-    result = jnp.zeros((512, 256), jnp.float32)
+    result = jnp.zeros((256, 256), jnp.float32)
     for reach, value in enumerate(RING):
         result = jnp.where(distance == reach + 1, value, result)
     return result.astype(jnp.bfloat16)
@@ -179,85 +180,91 @@
 
 def copies(now, before, pieces, ext_now, ext_before):
     x_low, x_high, y_low, y_high, c_low, c_high = pieces
-    result = []
+    early, late = [], []
     for half in range(2):
         lanes = pl.ds(half * LANES, LANES)
 
         def add(source, plane, count, row, rows, target, to_plane, to_row):
-            result.append((
+            (early if to_plane < SPLIT else late).append((
                 source.at[pl.ds(plane, count), pl.ds(row, rows), lanes],
                 target.at[pl.ds(to_plane, count), half, pl.ds(to_row, rows), :],
             ))
 
-        add(now, 0, OWN, 0, OWN, ext_now, HALO, TOP)
-        add(before, 0, OWN, 0, OWN, ext_before, HALO, TOP)
+        for plane in (0, SPLIT - HALO):
+            place = plane + HALO
+            add(now, plane, 20, 0, OWN, ext_now, place, TOP)
+            add(before, plane, 20, 0, OWN, ext_before, place, TOP)
+            for source, first, second in ((y_low, 0, 8), (y_high, 64, 64)):
+                add(source, plane, 20, 0, 24, ext_now, place, first)
+                add(source, plane, 20, 24, 16, ext_before, place, second)
         for source, first, second in ((x_low, 0, 4), (x_high, 60, 60)):
             add(source, 0, 20, 0, OWN, ext_now, first, TOP)
             add(source, 20, 16, 0, OWN, ext_before, second, TOP)
-        for source, first, second in ((y_low, 0, 8), (y_high, 64, 64)):
-            add(source, 0, OWN, 0, 24, ext_now, HALO, first)
-            add(source, 0, OWN, 24, 16, ext_before, HALO, second)
         for piece, near, far in ((c_low, 16, 8), (c_high, 64, 72)):
             for side, places in ((0, (4, 12, 8, 16)), (40, (60, 60, 60, 60))):
                 add(piece, side, 16, 0, 8, ext_now, places[0], near)
                 add(piece, side + 16, 8, 0, 8, ext_now, places[1], far)
                 add(piece, side + 24, 12, 0, 8, ext_before, places[2], near)
                 add(piece, side + 36, 4, 0, 8, ext_before, places[3], far)
-    return result
-
-
-def stencil_pass(source, z_ref, y_refs, along, step, emit):
+    return early, late
+
+
+def stencil_pass(source, z_ref, y_refs, step, emit, wait_late=None):
     first = 4 * step
     top = 4 + 4 * step
     span = EXT - 8 * step
     tiles = span // 8
+    keep = -(-(8 + span) // 16) * 16
     y_ref, window_rows = ((y_refs[0], 96), (y_refs[1], 80), (y_refs[1], 80), (y_refs[2], 64))[
         step - 1
     ]
 
     def multiply(x):
         parts = []
-        for g in range(4):
+        kept = {}
+        for g in range(8):
             plane = jnp.concatenate(
                 [source[x + g, half, pl.ds(top - 8, window_rows), :] for half in range(2)], axis=1
             )
             upper = plane.astype(jnp.bfloat16)
             lower = (plane - upper.astype(jnp.float32)).astype(jnp.bfloat16)
             parts.append((upper, lower))
-        stacked = jnp.concatenate(
-            [jnp.concatenate([part[side] for part in parts], axis=0) for side in range(2)], axis=1
-        )
-        along_z = jnp.dot(stacked, z_ref[...], preferred_element_type=jnp.float32)
-        for g in range(4):
+        along_z = []
+        for pair in (parts[:2], parts[2:4], parts[4:6], parts[6:]):
+            stacked = jnp.concatenate(
+                [part[side][:keep] for side in range(2) for part in pair], axis=0
+            )
+            both = jnp.dot(stacked, z_ref[...], preferred_element_type=jnp.float32)
+            along_z.append(both[: 2 * keep] + both[2 * keep :])
+        for g in range(8):
             along_y = jnp.dot(
                 y_ref[...], jnp.concatenate(parts[g], axis=0), preferred_element_type=jnp.float32
             )
             for tile in range(tiles):
-                start = g * window_rows + 8 + 8 * tile
-                total = along_z[start : start + 8] + along_y[8 * tile : 8 * tile + 8]
+                start = (g % 2) * keep + 8 + 8 * tile
+                total = along_z[g // 2][start : start + 8] + along_y[8 * tile : 8 * tile + 8]
                 for half in range(2):
-                    along[g, half, pl.ds(8 * tile, 8), :] = total[
-                        :, half * LANES : (half + 1) * LANES
-                    ]
-
-    multiply(first)
+                    kept[g, tile, half] = total[:, half * LANES : (half + 1) * LANES]
+        return kept
 
     def group(index, carry):
-        x = first + 4 * index
+        if wait_late is not None:
+            pl.when(index == (SPLIT - 16) // 8)(wait_late)
+        x = first + 8 * index
+        kept = multiply(x)
         for tile in range(tiles):
             for half in range(2):
                 row = top + 8 * tile
-                window = [source[x - 4 + j, half, pl.ds(row, 8), :] for j in range(12)]
-                for g in range(4):
-                    total = along[g, half, pl.ds(8 * tile, 8), :] + CENTRE * window[4 + g]
+                for g in range(8):
+                    window = [source[x + g - 4 + j, half, pl.ds(row, 8), :] for j in range(9)]
+                    total = CENTRE * window[4]
                     for reach in range(1, 5):
-                        pair = window[4 + g + reach] + window[4 + g - reach]
-                        total = total + RING[reach - 1] * pair
-                    emit(x + g, half, row, window[4 + g], total)
-        multiply(x + 4)
+                        total = total + RING[reach - 1] * (window[4 + reach] + window[4 - reach])
+                    total = total + kept[g, tile, half]
+                    emit(x + g, half, row, window[4], total)
         return carry
 
-    lax.fori_loop(0, span // 4, group, 0)
+    lax.fori_loop(0, span // 8, group, 0)
 
 
 def propagate_kernel(
@@ -269,14 +276,16 @@
     (
         plane_in, out_ref,
         field_a, field_b, field_c, stage, courant, term_a, term_b, term_c, term_d,
-        planes, along, picked, sems,
+        planes, picked, sems,
     ) = refs
     terms = (term_a, term_b, term_c, term_d)
     matrices = (y_ref_a, y_ref_b, y_ref_c)
     first = start_all([(plane_in, planes)], sems.at[0])
     clear_edges(field_a)
     clear_edges(field_b)
-    loads = start_all(copies(now, before, pieces, field_b, field_a), sems.at[1])
+    early, late = copies(now, before, pieces, field_b, field_a)
+    early = start_all(early, sems.at[1])
+    late = start_all(late, sems.at[2])
     clear(field_c, (0, EXT), range(12))
     own = pl.ds(HALO, OWN)
     later = []
@@ -286,12 +295,12 @@
             (adjoint_now.at[:, :, lanes], field_c.at[own, half, pl.ds(TOP, OWN), :]),
             (adjoint_after.at[:, :, lanes], stage.at[:, half]),
         ]
-    later = start_all(later, sems.at[2])
+    later = start_all(later, sems.at[3])
     clear(term_b, (0, 64), (0, 8))
     clear(term_d, (0, 48), (1, 7))
     wait_all(first)
     fill_courant(base_ref, planes, courant)
-    wait_all(loads)
+    wait_all(early)
     lane = lax.broadcasted_iota(jnp.int32, (1, LANES), 1)
     number = count_ref[0]
 
@@ -308,7 +317,10 @@
                 centre + centre - target[x, half, rows, :] + courant[x, half, rows, :] * total
             )
 
-        stencil_pass(newer, z_ref, matrices, along, step, emit)
+        stencil_pass(
+            newer, z_ref, matrices, step, emit,
+            (lambda: wait_all(late)) if step == 1 else None,
+        )
         for source in range(4):
             x = source_ref[source] - (base_ref[0] - HALO)
             row = source_ref[4 + source] - (base_ref[1] - TOP)
@@ -341,8 +353,10 @@
 
         lax.fori_loop(0, (number + 3) // 4, sample, 0)
 
-    clear(field_a, (0, EXT), range(12))
-    clear(field_b, (0, EXT), range(12))
+    clear(field_a, (4, EXT - 4), range(1, 11))
+    clear(field_b, (0, 8), range(12))
+    clear(field_b, (8, EXT - 8), (0, 1, 9, 10, 11))
+    clear(field_b, (EXT - 8, EXT), range(12))
     wait_all(later)
 
     def scale(index, carry):
@@ -366,7 +380,7 @@
                 centre + centre - older[x, half, rows, :] + courant[x, half, rows, :] * total
             )
 
-        stencil_pass(newer, z_ref, matrices, along, step, emit)
+        stencil_pass(newer, z_ref, matrices, step, emit)
 
         def inject(entry, carry):
             _, x, row, half, _ = unpack(own_ref[entry])
@@ -395,7 +409,7 @@
         value = centre + centre - field_c[x, half, rows, :] + courant[x, half, rows, :] * total
         term_a[x - 4, half, place, :] = value * term_a[x - 4, half, place, :]
 
-    stencil_pass(field_b, z_ref, matrices, along, 1, emit)
+    stencil_pass(field_b, z_ref, matrices, 1, emit)
 
     def finish(entry, carry):
         _, x, row, half, _ = unpack(own_ref[entry])
@@ -614,7 +628,7 @@
     parts = pl.pallas_call(
         propagate_kernel,
         out_shape=buffer,
-        in_specs=[spec(SMEM)] * 6 + [spec(VMEM)] * 4 + [spec(HBM)] * 11,
+        in_specs=[spec(SMEM)] * 6 + [spec(VMEM)] * 4 + [spec(HBM)] * 8 + [spec(pl.ANY)] * 3,
         out_specs=spec(VMEM),
         scratch_shapes=[
             field, field, field,
@@ -622,9 +636,8 @@
             field,
             *(VMEM((EXT - 8 * s, 2, WIDE, LANES), jnp.float32) for s in range(1, 5)),
             VMEM(plane_shape, jnp.float32),
-            VMEM((4, 2, WIDE, LANES), jnp.float32),
             VMEM((ITERS, 1024, LANES), jnp.float32),
-            pltpu.SemaphoreType.DMA((3,)),
+            pltpu.SemaphoreType.DMA((4,)),
         ],
         compiler_params=params(60),
         cost_estimate=cost(200_000_000, 30_000_000),

time: 174 us -> 163 us (0.937)
  Pallas kernels: 80 us -> 69.5 us
    pallas_call x1, Pallas kernels: 60.9 us -> 50.5 us  [per_device(): pl.pallas_call(propagate_kernel, out_shape=buffer, in_specs=[spec(SMEM)]...]
    unnamed x19 -> x21, local copies, waits for them, and re-layouts: 3.87 us -> 4.1 us
where the time goes in v3:
time: 163 us
  Pallas kernels  69.5 us (43%)
  starting transfers between devices  32.4 us (20%)
  waiting for transfers between devices  25.8 us (16%)
  blocking collectives  23.1 us (14%)
  local copies, waits for them, and re-layouts  8.24 us (5%)
  other arithmetic  3.38 us (2%)
    pallas_call x1, Pallas kernels, per_device(): pl.pallas_call(propagate_kernel, out_shape=buffer, in_specs=[spec(SMEM)]...  50.5 us
    all_to_all x1, blocking collectives, per_device(): lax.all_to_all(parts.reshape(128, 8, LANES), everywhere, 0, 0, tiled=True)  23.1 us
    ppermute x3, starting transfers between devices, shifts(): lax.ppermute(block_up, axis, up)  16 us
    all_to_all x1, waiting for transfers between devices, per_device(): lax.all_to_all(windows.reshape(128, 8, LANES), everywhere, 0, 0, tiled=True)  14.2 us
    all_to_all x1, starting transfers between devices, per_device(): lax.all_to_all(windows.reshape(128, 8, LANES), everywhere, 0, 0, tiled=True)  11.3 us
    pallas_call x2, Pallas kernels, staged(): pl.pallas_call(kernel, out_shape=shapes, in_specs=[spec(HBM)] * len(opera...  8.11 us
    ppermute x3, waiting for transfers between devices, shifts(): lax.ppermute(block_up, axis, up)  6.16 us
    ppermute x3, waiting for transfers between devices, shifts(): lax.ppermute(block_down, axis, down)  5.43 us
  transfers between devices with their start and end apart: 7, of which 3 were waited for; matrix products, arithmetic and copies ran while one was open for 3% of the time, Pallas kernels for 6%

profile of v3, /device:TPU:1, one launch (start us, length us, event | category | flops | bytes accessed | tf_op | source)
XLA Modules:
  0.0 162.7 jit_solution(12665684037079351386)
XLA Ops:
  0.0 1.5 pad.4.velocity_ref
  1.5 1.8 %shard_map.93.refs_4_ = f32[8,16,8,128]{3,2,1,0:T(8,128)} custom-call(f32[5,8,256]{2,1,0:T(8,128)} %pad.4.velocity_ref), custom_call_target="tpu_custom_call" | custom-call | flops 100000 | bytes 600000 | tf_op jit(solution)/shard_map/pallas_call | solution.py:584
  3.3 5.6 %shard_map.92 = (f32[36,40,256]{2,1,0:T(8,128)}, f32[36,40,256]{2,1,0:T(8,128)}, f32[40,40,256]{2,1,0:T(8,128)}, f32[40,40,256]{2,1,0:T(8,128)}) custom-call(f32[40,40,256]{2,1,0:T(8,128)} %now.3, f32[40,40,256]{2,1,0:T(8,128)} %before.3), custom_call_target="tpu_custom_call" | custom-call | flops 1000 | bytes 9000000 | tf_op jit(solution)/shard_map/pallas_call | solution.py:562
  9.0 4.1 %collective-permute-start = (f32[36,40,256]{2,1,0:T(8,128)}, f32[36,40,256]{2,1,0:T(8,128)S(1)}, u32[]{:S(2)}, u32[]{:S(2)}) collective-permute-start(f32[36,40,256]{2,1,0:T(8,128)} %get-tuple-element.23), channel_id=1, source_target_pairs={{0,16},{16,32},{32,48},{48,64},{64,80},{80,96},{96,112},{1,17},{17... | collective-permute-start | bytes 4423688 | tf_op jit(solution)/shard_map/ppermute | solution.py:557
  13.1 1.3 collective-permute-start.1
  14.4 4.4 %collective-permute-start.2 = (f32[40,40,256]{2,1,0:T(8,128)}, f32[40,40,256]{2,1,0:T(8,128)}, u32[]{:S(2)}, u32[]{:S(2)}) collective-permute-start(f32[40,40,256]{2,1,0:T(8,128)} %get-tuple-element.25), channel_id=1, source_target_pairs={{0,1},{1,2},{2,3},{3,4},{4,5},{5,6},{6,7},{7,8},{8,9},{9,10},{10,1... | collective-permute-start | bytes 4915208 | tf_op jit(solution)/shard_map/ppermute | solution.py:557
  18.8 1.9 %collective-permute-start.3 = (f32[40,40,256]{2,1,0:T(8,128)}, f32[40,40,256]{2,1,0:T(8,128)}, u32[]{:S(2)}, u32[]{:S(2)}) collective-permute-start(f32[40,40,256]{2,1,0:T(8,128)} %get-tuple-element.26), channel_id=1, source_target_pairs={{1,0},{2,1},{3,2},{4,3},{5,4},{6,5},{7,6},{8,7},{9,8},{10,9},{11,1... | collective-permute-start | bytes 4915208 | tf_op jit(solution)/shard_map/ppermute | solution.py:557
  20.8 11.3 %all-to-all-start = ((f32[128,8,128]{2,1,0:T(8,128)}), f32[128,8,128]{2,1,0:T(8,128)S(1)}, u32[]{:S(2)}, u32[]{:S(2)}) async-start(f32[128,8,128]{2,1,0:T(8,128)} %bitcast.18), calls=%async_computation | async-start | bytes 1048576 | tf_op jit(solution)/shard_map/all_to_all | solution.py:591
  32.1 0.6 or_or_fusion.code_ref
  32.7 0.6 copy.16
  33.4 0.6 reshape.45.source_ref
  34.0 0.7 reshape.46.wavelet_ref
  34.6 3.2 %shard_map.91 = (s32[1024]{0:T(1024)}, s32[1]{0:T(128)}) custom-call(s32[1024]{0:T(1024)} %or_or_fusion.code_ref), custom_call_target="tpu_custom_call" | custom-call | flops 10000000 | bytes 20000000 | tf_op jit(solution)/shard_map/pallas_call | solution.py:594
  37.9 0.7 select_convert_fusion.z_ref
  38.6 0.6 select_convert_fusion.3.y_ref_c
  39.3 6.2 %collective-permute-done.x_low.refs_0_ = f32[36,40,256]{2,1,0:T(8,128)S(1)} collective-permute-done((f32[36,40,256]{2,1,0:T(8,128)}, f32[36,40,256]{2,1,0:T(8,128)S(1)}, u32[]{:S(2)}, u32[]{:S(2)}) %collective-permute-start) | collective-permute-done | bytes 1474592 | tf_op jit(solution)/shard_map/ppermute | solution.py:557
  45.4 5.4 %collective-permute-done.1.x_high.refs_1_ = f32[36,40,256]{2,1,0:T(8,128)S(1)} collective-permute-done((f32[36,40,256]{2,1,0:T(8,128)}, f32[36,40,256]{2,1,0:T(8,128)S(1)}, u32[]{:S(2)}, u32[]{:S(2)}) %collective-permute-start.1) | collective-permute-done | bytes 1474592 | tf_op jit(solution)/shard_map/ppermute | solution.py:557
  50.8 1.1 copy-done.3
  52.0 2.5 %shard_map.95 = (f32[80,8,256]{2,1,0:T(8,128)}, f32[80,8,256]{2,1,0:T(8,128)}) custom-call(f32[36,40,256]{2,1,0:T(8,128)} %copy-done.2, f32[36,40,256]{2,1,0:T(8,128)} %copy-done.3), custom_call_target="tpu_custom_call" | custom-call | flops 1000 | bytes 2000000 | tf_op jit(solution)/shard_map/pallas_call | solution.py:562
  54.4 7.4 %collective-permute-start.4 = (f32[80,8,256]{2,1,0:T(8,128)}, f32[80,8,256]{2,1,0:T(8,128)S(1)}, u32[]{:S(2)}, u32[]{:S(2)}) collective-permute-start(f32[80,8,256]{2,1,0:T(8,128)} %get-tuple-element.27), channel_id=1, source_target_pairs={{0,1},{1,2},{2,3},{3,4},{4,5},{5,6},{6,7},{7,8},{8,9},{9,10},{10,1... | collective-permute-start | bytes 1966088 | tf_op jit(solution)/shard_map/ppermute | solution.py:557
  61.9 1.9 %collective-permute-start.5 = (f32[80,8,256]{2,1,0:T(8,128)}, f32[80,8,256]{2,1,0:T(8,128)S(1)}, u32[]{:S(2)}, u32[]{:S(2)}) collective-permute-start(f32[80,8,256]{2,1,0:T(8,128)} %get-tuple-element.28), channel_id=1, source_target_pairs={{1,0},{2,1},{3,2},{4,3},{5,4},{6,5},{7,6},{8,7},{9,8},{10,9},{11,1... | collective-permute-start | bytes 1966088 | tf_op jit(solution)/shard_map/ppermute | solution.py:557
  63.9 0.6 select_convert_fusion.2.y_ref_b
  64.6 0.7 select_convert_fusion.1.y_ref_a
  65.2 14.2 %all-to-all-done = f32[128,8,128]{2,1,0:T(8,128)S(1)} async-done(((f32[128,8,128]{2,1,0:T(8,128)}), f32[128,8,128]{2,1,0:T(8,128)S(1)}, u32[]{:S(2)}, u32[]{:S(2)}) %all-to-all-start) | async-done | bytes 524320 | tf_op jit(solution)/shard_map/all_to_all | solution.py:591
  79.5 4.0 %shard_map.96.refs_6_ = f32[20,2,96,128]{3,2,1,0:T(8,128)S(1)} custom-call(s32[2]{0:T(128)S(1)} %pad_add_fusion.base_ref, f32[8,16,8,128]{3,2,1,0:T(8,128)S(1)} %bitcast.17), custom_call_target="tpu_custom_call" | custom-call | flops 10000000 | bytes 10000000 | tf_op jit(solution)/shard_map/pallas_call | solution.py:614
  83.5 1.3 copy-done
  84.8 0.8 copy-done.4
  85.6 0.2 copy-done.5
  85.9 50.5 %shard_map.97 = f32[8,16,8,128]{3,2,1,0:T(8,128)} custom-call(s32[2]{0:T(128)} %copy-done.1, s32[12]{0:T(128)} %reshape.45.source_ref, f32[16]{0:T(128)} %reshape.46.wavelet_ref, s32[1024]{0:T(1024)} %get-tuple-element.17.own_ref, s32[1]{0:T(128)} %get-tuple-element.18.count_ref, f32[4096]{0:T(1024)} %bitcast.21, bf16[256,256]{1,0:T(8,128)(2,1)} %select_convert_fusion.z_ref, ...), custom_call_target="tpu_custom_call" | custom-call | flops 200000000 | bytes 30000000 | tf_op jit(solution)/shard_map/pallas_call | solution.py:628
  136.3 23.1 %all_to_all.10 = f32[128,8,128]{2,1,0:T(8,128)} all-to-all(f32[128,8,128]{2,1,0:T(8,128)} %bitcast.19), channel_id=1, replica_groups=mesh['gx'=8,'gy'=16] {'gx','gy'}, dimensions={0} | all-to-all | bytes 1048576 | tf_op jit(solution)/shard_map/all_to_all | solution.py:651
  159.4 1.9 %shard_map.98 = f32[5,8,256]{2,1,0:T(8,128)} custom-call(s32[2]{0:T(128)} %copy-done.1, f32[8,16,8,128]{3,2,1,0:T(8,128)} %bitcast.20), custom_call_target="tpu_custom_call" | custom-call | flops 100000 | bytes 600000 | tf_op jit(solution)/shard_map/pallas_call | solution.py:652
  161.3 1.4 slice_bitcast_fusion
  (29 shorter events, 0.2 us)
Async XLA Ops:
  8.9 23.2 %copy-start.7 = (s32[3,1024]{1,0:T(4,128)S(1)}, s32[3,1024]{1,0:T(4,128)}, u32[]{:S(2)}) copy-start(s32[3,1024]{1,0:T(4,128)} %param.15) | copy-start | bytes 36868
  9.0 23.8 %copy-start.6 = (f32[4,1024]{1,0:T(4,128)S(1)}, f32[4,1024]{1,0:T(4,128)}, u32[]{:S(2)}) copy-start(f32[4,1024]{1,0:T(4,128)} %param.17) | copy-start | bytes 49156
  9.0 24.4 %copy-start.8 = (s32[3,4]{1,0:T(4,128)S(1)}, s32[3,4]{1,0:T(4,128)}, u32[]{:S(2)}) copy-start(s32[3,4]{1,0:T(4,128)} %param.14) | copy-start | bytes 148
  9.0 25.0 %copy-start.9 = (f32[4,4]{1,0:T(4,128)S(1)}, f32[4,4]{1,0:T(4,128)}, u32[]{:S(2)}) copy-start(f32[4,4]{1,0:T(4,128)} %param.16) | copy-start | bytes 196
  9.0 36.4 %collective-permute-start = (f32[36,40,256]{2,1,0:T(8,128)}, f32[36,40,256]{2,1,0:T(8,128)S(1)}, u32[]{:S(2)}, u32[]{:S(2)}) collective-permute-start(f32[36,40,256]{2,1,0:T(8,128)} %get-tuple-element.23), channel_id=1, source_target_pairs={{0,16},{16,32},{32,48},{48,64},{64,80},{80,96},{96,112},{1,17},{17... | collective-permute-start | bytes 4423688 | tf_op jit(solution)/shard_map/ppermute | solution.py:557
  13.1 37.7 %collective-permute-start.1 = (f32[36,40,256]{2,1,0:T(8,128)}, f32[36,40,256]{2,1,0:T(8,128)S(1)}, u32[]{:S(2)}, u32[]{:S(2)}) collective-permute-start(f32[36,40,256]{2,1,0:T(8,128)} %get-tuple-element.24), channel_id=1, source_target_pairs={{16,0},{32,16},{48,32},{64,48},{80,64},{96,80},{112,96},{17,1},{33... | collective-permute-start | bytes 4423688 | tf_op jit(solution)/shard_map/ppermute | solution.py:557
  14.4 70.3 %collective-permute-start.2 = (f32[40,40,256]{2,1,0:T(8,128)}, f32[40,40,256]{2,1,0:T(8,128)}, u32[]{:S(2)}, u32[]{:S(2)}) collective-permute-start(f32[40,40,256]{2,1,0:T(8,128)} %get-tuple-element.25), channel_id=1, source_target_pairs={{0,1},{1,2},{2,3},{3,4},{4,5},{5,6},{6,7},{7,8},{8,9},{9,10},{10,1... | collective-permute-start | bytes 4915208 | tf_op jit(solution)/shard_map/ppermute | solution.py:557
  18.8 65.9 %collective-permute-start.3 = (f32[40,40,256]{2,1,0:T(8,128)}, f32[40,40,256]{2,1,0:T(8,128)}, u32[]{:S(2)}, u32[]{:S(2)}) collective-permute-start(f32[40,40,256]{2,1,0:T(8,128)} %get-tuple-element.26), channel_id=1, source_target_pairs={{1,0},{2,1},{3,2},{4,3},{5,4},{6,5},{7,6},{8,7},{9,8},{10,9},{11,1... | collective-permute-start | bytes 4915208 | tf_op jit(solution)/shard_map/ppermute | solution.py:557
  20.8 58.7 %all-to-all-start = ((f32[128,8,128]{2,1,0:T(8,128)}), f32[128,8,128]{2,1,0:T(8,128)S(1)}, u32[]{:S(2)}, u32[]{:S(2)}) async-start(f32[128,8,128]{2,1,0:T(8,128)} %bitcast.18), calls=%async_computation | async-start | bytes 1048576 | tf_op jit(solution)/shard_map/all_to_all | solution.py:591
  45.4 5.4 %copy-start.2 = (f32[36,40,256]{2,1,0:T(8,128)}, f32[36,40,256]{2,1,0:T(8,128)S(1)}, u32[]{:S(2)}) copy-start(f32[36,40,256]{2,1,0:T(8,128)S(1)} %collective-permute-done.x_low.refs_0_) | copy-start | bytes 4423684
  50.8 1.1 copy-start.3
  54.4 30.3 %collective-permute-start.4 = (f32[80,8,256]{2,1,0:T(8,128)}, f32[80,8,256]{2,1,0:T(8,128)S(1)}, u32[]{:S(2)}, u32[]{:S(2)}) collective-permute-start(f32[80,8,256]{2,1,0:T(8,128)} %get-tuple-element.27), channel_id=1, source_target_pairs={{0,1},{1,2},{2,3},{3,4},{4,5},{5,6},{6,7},{7,8},{8,9},{9,10},{10,1... | collective-permute-start | bytes 1966088 | tf_op jit(solution)/shard_map/ppermute | solution.py:557
  61.9 22.9 %collective-permute-start.5 = (f32[80,8,256]{2,1,0:T(8,128)}, f32[80,8,256]{2,1,0:T(8,128)S(1)}, u32[]{:S(2)}, u32[]{:S(2)}) collective-permute-start(f32[80,8,256]{2,1,0:T(8,128)} %get-tuple-element.28), channel_id=1, source_target_pairs={{1,0},{2,1},{3,2},{4,3},{5,4},{6,5},{7,6},{8,7},{9,8},{10,9},{11,1... | collective-permute-start | bytes 1966088 | tf_op jit(solution)/shard_map/ppermute | solution.py:557
  63.9 20.9 %copy-start.1 = (s32[2]{0:T(128)}, s32[2]{0:T(128)S(1)}, u32[]{:S(2)}) copy-start(s32[2]{0:T(128)S(1)} %pad_add_fusion.base_ref) | copy-start | bytes 28
  83.5 1.3 copy-start
  84.8 0.8 copy-start.4
  84.8 1.1 copy-start.5

commit v4 on v3

--- a/solution.py
+++ b/solution.py
@@ -20,7 +20,6 @@
 SMEM = pltpu.SMEM
 VMEM = pltpu.VMEM
 HBM = pltpu.HBM
-EXACT = lax.Precision.HIGHEST
 
 
 def params(mib):
@@ -60,6 +59,19 @@
     first = jnp.where(coarse == lower, 1.0 - fraction, 0.0)
     second = jnp.where(coarse == higher, fraction, 0.0)
     return first + second
+
+
+def thirds(data):
+    upper = data.astype(jnp.bfloat16)
+    rest = data - upper.astype(jnp.float32)
+    middle = rest.astype(jnp.bfloat16)
+    return upper, middle, (rest - middle.astype(jnp.float32)).astype(jnp.bfloat16)
+
+
+def exact_dot(weight, data):
+    return sum(
+        jnp.dot(weight, part, preferred_element_type=jnp.float32) for part in thirds(data)
+    )
 
 
 def quarter(fine):
@@ -119,23 +131,22 @@
 def model_kernel(base_ref, model_ref, plane_out, plane_ref, sem):
     row = lax.broadcasted_iota(jnp.int32, (64, 256), 0)
     column = lax.broadcasted_iota(jnp.int32, (64, 256), 1)
-    weight_z = hat(column, row, column // 4, 63, quarter(column))
+    weight_z = hat(column, row, column // 4, 63, quarter(column)).astype(jnp.bfloat16)
     fine = lax.broadcasted_iota(jnp.int32, (ROWS, 24), 0)
     coarse = lax.broadcasted_iota(jnp.int32, (ROWS, 24), 1)
     limit_y = 159 - (base_ref[1] // 4 - 4)
     weight_y = hat(fine, coarse, fine // 4 - 2, limit_y, quarter(fine))
     place = fine + (base_ref[1] - TOP)
-    weight_y = jnp.where((place >= 0) & (place < 640), weight_y, 0.0)
+    weight_y = jnp.where((place >= 0) & (place < 640), weight_y, 0.0).astype(jnp.bfloat16)
     first = 2 * (base_ref[0] // OWN) - 1
     for r in range(4):
         owner = jnp.clip(first + r, 0, 15)
         block = jnp.concatenate([model_ref[i, owner] for i in range(8)], axis=0)
-        deep = jnp.dot(block.T, weight_z, precision=EXACT, preferred_element_type=jnp.float32)
+        stacked = jnp.concatenate(thirds(block.T), axis=0)
+        deep = jnp.dot(stacked, weight_z, preferred_element_type=jnp.float32)
+        deep = deep[:LANES] + deep[LANES : 2 * LANES] + deep[2 * LANES :]
         for a in range(5):
-            plane = jnp.dot(
-                weight_y, deep[24 * a : 24 * a + 24], precision=EXACT,
-                preferred_element_type=jnp.float32,
-            )
+            plane = exact_dot(weight_y, deep[24 * a : 24 * a + 24])
             plane_ref[5 * r + a, 0] = plane[:, :LANES]
             plane_ref[5 * r + a, 1] = plane[:, LANES:]
     wait_all(start_all([(plane_ref, plane_out)], sem))
@@ -457,22 +468,22 @@
     row = lax.broadcasted_iota(jnp.int32, (24, WIDE), 0)
     fine = lax.broadcasted_iota(jnp.int32, (24, WIDE), 1)
     limit_y = 159 - (base_ref[1] // 4 - 4)
-    weight_y = hat(fine, row, fine // 4, limit_y, quarter(fine))
+    weight_y = hat(fine, row, fine // 4, limit_y, quarter(fine)).astype(jnp.bfloat16)
     column = lax.broadcasted_iota(jnp.int32, (64, 256), 0)
     fine = lax.broadcasted_iota(jnp.int32, (64, 256), 1)
-    weight_z = hat(fine, column, fine // 4, 63, quarter(fine))
+    weight_z = hat(fine, column, fine // 4, 63, quarter(fine)).astype(jnp.bfloat16)
     parts = [jnp.zeros((24, 256), jnp.float32)]
     for a in range(19):
         plane = jnp.concatenate(
             [coarse[a, half, pl.ds(0, WIDE), :] for half in range(2)], axis=1
         )
-        parts.append(
-            jnp.dot(weight_y, plane, precision=EXACT, preferred_element_type=jnp.float32)
+        parts.append(exact_dot(weight_y, plane))
+    parts.append(jnp.zeros((32, 256), jnp.float32))
+    result = (0.125 * 2.0 * SCALE**0.5) * sum(
+        lax.dot_general(
+            weight_z, part, (((1,), (1,)), ((), ())), preferred_element_type=jnp.float32
         )
-    parts.append(jnp.zeros((32, 256), jnp.float32))
-    result = (0.125 * 2.0 * SCALE**0.5) * lax.dot_general(
-        weight_z, jnp.concatenate(parts, axis=0), (((1,), (1,)), ((), ())),
-        precision=EXACT, preferred_element_type=jnp.float32,
+        for part in thirds(jnp.concatenate(parts, axis=0))
     )
     out_ref[...] = jnp.zeros(out_ref.shape, jnp.float32)
     index = base_ref[0] // OWN

time: 163 us -> 162 us (level)
  transfers between devices with their start and end apart: 7 -> 7, of which waited for: 3 -> 3; matrix products, arithmetic and copies ran while one was open for 3% -> 3% of each run, Pallas kernels for 6% -> 5%
where the time goes in v4:
time: 162 us; the launch traced here: 161 us
  Pallas kernels  68.1 us (42%)
  starting transfers between devices  32.4 us (20%)
  waiting for transfers between devices  25.8 us (16%)
  blocking collectives  23.1 us (14%)
  local copies, waits for them, and re-layouts  8.24 us (5%)
  other arithmetic  3.38 us (2%)
    pallas_call x1, Pallas kernels, per_device(): pl.pallas_call(propagate_kernel, out_shape=buffer, in_specs=[spec(SMEM)]...  50.2 us
    all_to_all x1, blocking collectives, per_device(): lax.all_to_all(parts.reshape(128, 8, LANES), everywhere, 0, 0, tiled=True)  23.1 us
    ppermute x3, starting transfers between devices, shifts(): lax.ppermute(block_up, axis, up)  16 us
    all_to_all x1, waiting for transfers between devices, per_device(): lax.all_to_all(windows.reshape(128, 8, LANES), everywhere, 0, 0, tiled=True)  14.2 us
    all_to_all x1, starting transfers between devices, per_device(): lax.all_to_all(windows.reshape(128, 8, LANES), everywhere, 0, 0, tiled=True)  11.3 us
    pallas_call x2, Pallas kernels, staged(): pl.pallas_call(kernel, out_shape=shapes, in_specs=[spec(HBM)] * len(opera...  8.11 us
    ppermute x3, waiting for transfers between devices, shifts(): lax.ppermute(block_up, axis, up)  6.16 us
    ppermute x3, waiting for transfers between devices, shifts(): lax.ppermute(block_down, axis, down)  5.43 us
  transfers between devices with their start and end apart: 7, of which 3 were waited for; matrix products, arithmetic and copies ran while one was open for 3% of the time, Pallas kernels for 5%

profile of v4, /device:TPU:1, one launch (start us, length us, event | category | flops | bytes accessed | tf_op | source)
XLA Modules:
  0.0 161.2 jit_solution(7494291747875526848)
XLA Ops:
  0.0 1.5 pad.4.velocity_ref
  1.5 1.8 %shard_map.93.refs_4_ = f32[8,16,8,128]{3,2,1,0:T(8,128)} custom-call(f32[5,8,256]{2,1,0:T(8,128)} %pad.4.velocity_ref), custom_call_target="tpu_custom_call" | custom-call | flops 100000 | bytes 600000 | tf_op jit(solution)/shard_map/pallas_call | solution.py:595
  3.3 5.6 %shard_map.92 = (f32[36,40,256]{2,1,0:T(8,128)}, f32[36,40,256]{2,1,0:T(8,128)}, f32[40,40,256]{2,1,0:T(8,128)}, f32[40,40,256]{2,1,0:T(8,128)}) custom-call(f32[40,40,256]{2,1,0:T(8,128)} %now.3, f32[40,40,256]{2,1,0:T(8,128)} %before.3), custom_call_target="tpu_custom_call" | custom-call | flops 1000 | bytes 9000000 | tf_op jit(solution)/shard_map/pallas_call | solution.py:573
  9.0 4.1 %collective-permute-start = (f32[36,40,256]{2,1,0:T(8,128)}, f32[36,40,256]{2,1,0:T(8,128)S(1)}, u32[]{:S(2)}, u32[]{:S(2)}) collective-permute-start(f32[36,40,256]{2,1,0:T(8,128)} %get-tuple-element.23), channel_id=1, source_target_pairs={{0,16},{16,32},{32,48},{48,64},{64,80},{80,96},{96,112},{1,17},{17... | collective-permute-start | bytes 4423688 | tf_op jit(solution)/shard_map/ppermute | solution.py:568
  13.1 1.3 collective-permute-start.1
  14.4 4.4 %collective-permute-start.2 = (f32[40,40,256]{2,1,0:T(8,128)}, f32[40,40,256]{2,1,0:T(8,128)}, u32[]{:S(2)}, u32[]{:S(2)}) collective-permute-start(f32[40,40,256]{2,1,0:T(8,128)} %get-tuple-element.25), channel_id=1, source_target_pairs={{0,1},{1,2},{2,3},{3,4},{4,5},{5,6},{6,7},{7,8},{8,9},{9,10},{10,1... | collective-permute-start | bytes 4915208 | tf_op jit(solution)/shard_map/ppermute | solution.py:568
  18.8 1.9 %collective-permute-start.3 = (f32[40,40,256]{2,1,0:T(8,128)}, f32[40,40,256]{2,1,0:T(8,128)}, u32[]{:S(2)}, u32[]{:S(2)}) collective-permute-start(f32[40,40,256]{2,1,0:T(8,128)} %get-tuple-element.26), channel_id=1, source_target_pairs={{1,0},{2,1},{3,2},{4,3},{5,4},{6,5},{7,6},{8,7},{9,8},{10,9},{11,1... | collective-permute-start | bytes 4915208 | tf_op jit(solution)/shard_map/ppermute | solution.py:568
  20.8 11.3 %all-to-all-start = ((f32[128,8,128]{2,1,0:T(8,128)}), f32[128,8,128]{2,1,0:T(8,128)S(1)}, u32[]{:S(2)}, u32[]{:S(2)}) async-start(f32[128,8,128]{2,1,0:T(8,128)} %bitcast.18), calls=%async_computation | async-start | bytes 1048576 | tf_op jit(solution)/shard_map/all_to_all | solution.py:602
  32.1 0.6 or_or_fusion.code_ref
  32.7 0.6 copy.16
  33.4 0.6 reshape.45.source_ref
  34.0 0.7 reshape.46.wavelet_ref
  34.6 3.2 %shard_map.91 = (s32[1024]{0:T(1024)}, s32[1]{0:T(128)}) custom-call(s32[1024]{0:T(1024)} %or_or_fusion.code_ref), custom_call_target="tpu_custom_call" | custom-call | flops 10000000 | bytes 20000000 | tf_op jit(solution)/shard_map/pallas_call | solution.py:605
  37.9 0.7 select_convert_fusion.z_ref
  38.6 0.6 select_convert_fusion.3.y_ref_c
  39.3 6.2 %collective-permute-done.x_low.refs_0_ = f32[36,40,256]{2,1,0:T(8,128)S(1)} collective-permute-done((f32[36,40,256]{2,1,0:T(8,128)}, f32[36,40,256]{2,1,0:T(8,128)S(1)}, u32[]{:S(2)}, u32[]{:S(2)}) %collective-permute-start) | collective-permute-done | bytes 1474592 | tf_op jit(solution)/shard_map/ppermute | solution.py:568
  45.4 5.4 %collective-permute-done.1.x_high.refs_1_ = f32[36,40,256]{2,1,0:T(8,128)S(1)} collective-permute-done((f32[36,40,256]{2,1,0:T(8,128)}, f32[36,40,256]{2,1,0:T(8,128)S(1)}, u32[]{:S(2)}, u32[]{:S(2)}) %collective-permute-start.1) | collective-permute-done | bytes 1474592 | tf_op jit(solution)/shard_map/ppermute | solution.py:568
  50.8 1.1 copy-done.3
  52.0 2.5 %shard_map.95 = (f32[80,8,256]{2,1,0:T(8,128)}, f32[80,8,256]{2,1,0:T(8,128)}) custom-call(f32[36,40,256]{2,1,0:T(8,128)} %copy-done.2, f32[36,40,256]{2,1,0:T(8,128)} %copy-done.3), custom_call_target="tpu_custom_call" | custom-call | flops 1000 | bytes 2000000 | tf_op jit(solution)/shard_map/pallas_call | solution.py:573
  54.4 7.4 %collective-permute-start.4 = (f32[80,8,256]{2,1,0:T(8,128)}, f32[80,8,256]{2,1,0:T(8,128)S(1)}, u32[]{:S(2)}, u32[]{:S(2)}) collective-permute-start(f32[80,8,256]{2,1,0:T(8,128)} %get-tuple-element.27), channel_id=1, source_target_pairs={{0,1},{1,2},{2,3},{3,4},{4,5},{5,6},{6,7},{7,8},{8,9},{9,10},{10,1... | collective-permute-start | bytes 1966088 | tf_op jit(solution)/shard_map/ppermute | solution.py:568
  61.9 1.9 %collective-permute-start.5 = (f32[80,8,256]{2,1,0:T(8,128)}, f32[80,8,256]{2,1,0:T(8,128)S(1)}, u32[]{:S(2)}, u32[]{:S(2)}) collective-permute-start(f32[80,8,256]{2,1,0:T(8,128)} %get-tuple-element.28), channel_id=1, source_target_pairs={{1,0},{2,1},{3,2},{4,3},{5,4},{6,5},{7,6},{8,7},{9,8},{10,9},{11,1... | collective-permute-start | bytes 1966088 | tf_op jit(solution)/shard_map/ppermute | solution.py:568
  63.9 0.6 select_convert_fusion.2.y_ref_b
  64.6 0.7 select_convert_fusion.1.y_ref_a
  65.2 14.2 %all-to-all-done = f32[128,8,128]{2,1,0:T(8,128)S(1)} async-done(((f32[128,8,128]{2,1,0:T(8,128)}), f32[128,8,128]{2,1,0:T(8,128)S(1)}, u32[]{:S(2)}, u32[]{:S(2)}) %all-to-all-start) | async-done | bytes 524320 | tf_op jit(solution)/shard_map/all_to_all | solution.py:602
  79.5 2.7 %shard_map.96.refs_6_ = f32[20,2,96,128]{3,2,1,0:T(8,128)S(1)} custom-call(s32[2]{0:T(128)S(1)} %pad_add_fusion.base_ref, f32[8,16,8,128]{3,2,1,0:T(8,128)S(1)} %bitcast.17), custom_call_target="tpu_custom_call" | custom-call | flops 10000000 | bytes 10000000 | tf_op jit(solution)/shard_map/pallas_call | solution.py:625
  82.2 1.3 copy-done
  83.6 0.8 copy-done.4
  84.4 0.2 copy-done.5
  84.6 50.2 %shard_map.97 = f32[8,16,8,128]{3,2,1,0:T(8,128)} custom-call(s32[2]{0:T(128)} %copy-done.1, s32[12]{0:T(128)} %reshape.45.source_ref, f32[16]{0:T(128)} %reshape.46.wavelet_ref, s32[1024]{0:T(1024)} %get-tuple-element.17.own_ref, s32[1]{0:T(128)} %get-tuple-element.18.count_ref, f32[4096]{0:T(1024)} %bitcast.21, bf16[256,256]{1,0:T(8,128)(2,1)} %select_convert_fusion.z_ref, ...), custom_call_target="tpu_custom_call" | custom-call | flops 200000000 | bytes 30000000 | tf_op jit(solution)/shard_map/pallas_call | solution.py:639
  134.9 23.1 %all_to_all.10 = f32[128,8,128]{2,1,0:T(8,128)} all-to-all(f32[128,8,128]{2,1,0:T(8,128)} %bitcast.19), channel_id=1, replica_groups=mesh['gx'=8,'gy'=16] {'gx','gy'}, dimensions={0} | all-to-all | bytes 1048576 | tf_op jit(solution)/shard_map/all_to_all | solution.py:662
  157.9 1.9 %shard_map.98 = f32[5,8,256]{2,1,0:T(8,128)} custom-call(s32[2]{0:T(128)} %copy-done.1, f32[8,16,8,128]{3,2,1,0:T(8,128)} %bitcast.20), custom_call_target="tpu_custom_call" | custom-call | flops 100000 | bytes 600000 | tf_op jit(solution)/shard_map/pallas_call | solution.py:663
  159.8 1.4 slice_bitcast_fusion
  (29 shorter events, 0.2 us)
Async XLA Ops:
  8.9 23.2 %copy-start.7 = (s32[3,1024]{1,0:T(4,128)S(1)}, s32[3,1024]{1,0:T(4,128)}, u32[]{:S(2)}) copy-start(s32[3,1024]{1,0:T(4,128)} %param.15) | copy-start | bytes 36868
  9.0 23.8 %copy-start.6 = (f32[4,1024]{1,0:T(4,128)S(1)}, f32[4,1024]{1,0:T(4,128)}, u32[]{:S(2)}) copy-start(f32[4,1024]{1,0:T(4,128)} %param.17) | copy-start | bytes 49156
  9.0 24.4 %copy-start.8 = (s32[3,4]{1,0:T(4,128)S(1)}, s32[3,4]{1,0:T(4,128)}, u32[]{:S(2)}) copy-start(s32[3,4]{1,0:T(4,128)} %param.14) | copy-start | bytes 148
  9.0 25.0 %copy-start.9 = (f32[4,4]{1,0:T(4,128)S(1)}, f32[4,4]{1,0:T(4,128)}, u32[]{:S(2)}) copy-start(f32[4,4]{1,0:T(4,128)} %param.16) | copy-start | bytes 196
  9.0 36.4 %collective-permute-start = (f32[36,40,256]{2,1,0:T(8,128)}, f32[36,40,256]{2,1,0:T(8,128)S(1)}, u32[]{:S(2)}, u32[]{:S(2)}) collective-permute-start(f32[36,40,256]{2,1,0:T(8,128)} %get-tuple-element.23), channel_id=1, source_target_pairs={{0,16},{16,32},{32,48},{48,64},{64,80},{80,96},{96,112},{1,17},{17... | collective-permute-start | bytes 4423688 | tf_op jit(solution)/shard_map/ppermute | solution.py:568
  13.1 37.7 %collective-permute-start.1 = (f32[36,40,256]{2,1,0:T(8,128)}, f32[36,40,256]{2,1,0:T(8,128)S(1)}, u32[]{:S(2)}, u32[]{:S(2)}) collective-permute-start(f32[36,40,256]{2,1,0:T(8,128)} %get-tuple-element.24), channel_id=1, source_target_pairs={{16,0},{32,16},{48,32},{64,48},{80,64},{96,80},{112,96},{17,1},{33... | collective-permute-start | bytes 4423688 | tf_op jit(solution)/shard_map/ppermute | solution.py:568
  14.4 69.1 %collective-permute-start.2 = (f32[40,40,256]{2,1,0:T(8,128)}, f32[40,40,256]{2,1,0:T(8,128)}, u32[]{:S(2)}, u32[]{:S(2)}) collective-permute-start(f32[40,40,256]{2,1,0:T(8,128)} %get-tuple-element.25), channel_id=1, source_target_pairs={{0,1},{1,2},{2,3},{3,4},{4,5},{5,6},{6,7},{7,8},{8,9},{9,10},{10,1... | collective-permute-start | bytes 4915208 | tf_op jit(solution)/shard_map/ppermute | solution.py:568
  18.8 64.7 %collective-permute-start.3 = (f32[40,40,256]{2,1,0:T(8,128)}, f32[40,40,256]{2,1,0:T(8,128)}, u32[]{:S(2)}, u32[]{:S(2)}) collective-permute-start(f32[40,40,256]{2,1,0:T(8,128)} %get-tuple-element.26), channel_id=1, source_target_pairs={{1,0},{2,1},{3,2},{4,3},{5,4},{6,5},{7,6},{8,7},{9,8},{10,9},{11,1... | collective-permute-start | bytes 4915208 | tf_op jit(solution)/shard_map/ppermute | solution.py:568
  20.8 58.7 %all-to-all-start = ((f32[128,8,128]{2,1,0:T(8,128)}), f32[128,8,128]{2,1,0:T(8,128)S(1)}, u32[]{:S(2)}, u32[]{:S(2)}) async-start(f32[128,8,128]{2,1,0:T(8,128)} %bitcast.18), calls=%async_computation | async-start | bytes 1048576 | tf_op jit(solution)/shard_map/all_to_all | solution.py:602
  45.4 5.4 %copy-start.2 = (f32[36,40,256]{2,1,0:T(8,128)}, f32[36,40,256]{2,1,0:T(8,128)S(1)}, u32[]{:S(2)}) copy-start(f32[36,40,256]{2,1,0:T(8,128)S(1)} %collective-permute-done.x_low.refs_0_) | copy-start | bytes 4423684
  50.8 1.1 copy-start.3
  54.4 29.1 %collective-permute-start.4 = (f32[80,8,256]{2,1,0:T(8,128)}, f32[80,8,256]{2,1,0:T(8,128)S(1)}, u32[]{:S(2)}, u32[]{:S(2)}) collective-permute-start(f32[80,8,256]{2,1,0:T(8,128)} %get-tuple-element.27), channel_id=1, source_target_pairs={{0,1},{1,2},{2,3},{3,4},{4,5},{5,6},{6,7},{7,8},{8,9},{9,10},{10,1... | collective-permute-start | bytes 1966088 | tf_op jit(solution)/shard_map/ppermute | solution.py:568
  61.9 21.6 %collective-permute-start.5 = (f32[80,8,256]{2,1,0:T(8,128)}, f32[80,8,256]{2,1,0:T(8,128)S(1)}, u32[]{:S(2)}, u32[]{:S(2)}) collective-permute-start(f32[80,8,256]{2,1,0:T(8,128)} %get-tuple-element.28), channel_id=1, source_target_pairs={{1,0},{2,1},{3,2},{4,3},{5,4},{6,5},{7,6},{8,7},{9,8},{10,9},{11,1... | collective-permute-start | bytes 1966088 | tf_op jit(solution)/shard_map/ppermute | solution.py:568
  63.9 19.6 %copy-start.1 = (s32[2]{0:T(128)}, s32[2]{0:T(128)S(1)}, u32[]{:S(2)}) copy-start(s32[2]{0:T(128)S(1)} %pad_add_fusion.base_ref) | copy-start | bytes 28
  82.2 1.3 copy-start
  83.5 0.8 copy-start.4
  83.6 1.1 copy-start.5

commit v5 on v4

--- a/solution.py
+++ b/solution.py
@@ -116,13 +116,15 @@
     return receiver, x + HALO, y + TOP, z // LANES, z & (LANES - 1)
 
 
-def model_pack_kernel(velocity_ref, out_ref):
+def model_pack_kernel(velocity_ref, out_ref, wide_ref):
+    wide_ref[...] = jnp.zeros(wide_ref.shape, jnp.float32)
+    wide_ref[:, :, pl.ds(0, 160)] = velocity_ref[...]
     lane = lax.broadcasted_iota(jnp.int32, (8, LANES), 1)
-    blocks = [velocity_ref[a] for a in range(5)]
+    blocks = [wide_ref[a] for a in range(5)]
     for j in range(16):
         tile = jnp.zeros((8, LANES), jnp.float32)
         for a in range(5):
-            moved = pltpu.roll(blocks[a], (24 * a - 10 * j) % 256, 1)[:, :LANES]
+            moved = pltpu.roll(blocks[a], (24 * a - 10 * j + 4) % 256, 1)[:, :LANES]
             tile = jnp.where((lane >= 24 * a) & (lane < 24 * a + 24), moved, tile)
         for i in range(8):
             out_ref[i, j] = tile
@@ -513,7 +515,7 @@
             moved = pltpu.roll(tile, (10 * j - 4 - 24 * r) % 256, 1)
             sums[r] = sums[r] + jnp.where(inside, moved, 0.0)
     for r in range(5):
-        out_ref[r] = sums[r]
+        out_ref[r] = sums[r][:, :160]
 
 
 def face_kernel(now, before, *refs):
@@ -591,12 +593,13 @@
     everywhere = ("gx", "gy")
     buffer = jax.ShapeDtypeStruct((8, 16, 8, LANES), jnp.float32)
 
-    turned = jnp.pad(velocity.transpose(0, 2, 1), ((0, 0), (0, 0), (4, 92)))
+    turned = velocity.transpose(0, 2, 1)
     windows = pl.pallas_call(
         model_pack_kernel,
         out_shape=buffer,
         in_specs=[spec(VMEM)],
         out_specs=spec(VMEM),
+        scratch_shapes=[VMEM((5, 8, 256), jnp.float32)],
         cost_estimate=cost(100_000, 600_000),
     )(turned)
     model = lax.all_to_all(windows.reshape(128, 8, LANES), everywhere, 0, 0, tiled=True)
@@ -662,12 +665,12 @@
     parts = lax.all_to_all(parts.reshape(128, 8, LANES), everywhere, 0, 0, tiled=True)
     grid = pl.pallas_call(
         gather_kernel,
-        out_shape=jax.ShapeDtypeStruct((5, 8, 256), jnp.float32),
+        out_shape=jax.ShapeDtypeStruct((5, 8, 160), jnp.float32),
         in_specs=[spec(SMEM), spec(VMEM)],
         out_specs=spec(VMEM),
         cost_estimate=cost(100_000, 600_000),
     )(base, parts.reshape(8, 16, 8, LANES))
-    return grid[:, :, :160].transpose(0, 2, 1)
+    return grid.transpose(0, 2, 1)
 
 
 def solution(mesh):

time: 162 us -> 159 us (0.981)
  local copies, waits for them, and re-layouts: 8.24 us -> 5.36 us
where the time goes in v5:
time: 159 us
  Pallas kernels  68.2 us (43%)
  starting transfers between devices  32.4 us (20%)
  waiting for transfers between devices  25.8 us (16%)
  blocking collectives  23.6 us (15%)
  local copies, waits for them, and re-layouts  5.36 us (3%)
  other arithmetic  3.38 us (2%)
    pallas_call x1, Pallas kernels, per_device(): pl.pallas_call(propagate_kernel, out_shape=buffer, in_specs=[spec(SMEM)]...  50.4 us
    all_to_all x1, blocking collectives, per_device(): lax.all_to_all(parts.reshape(128, 8, LANES), everywhere, 0, 0, tiled=True)  23.6 us
    ppermute x3, starting transfers between devices, shifts(): lax.ppermute(block_up, axis, up)  16 us
    all_to_all x1, waiting for transfers between devices, per_device(): lax.all_to_all(windows.reshape(128, 8, LANES), everywhere, 0, 0, tiled=True)  14.2 us
    all_to_all x1, starting transfers between devices, per_device(): lax.all_to_all(windows.reshape(128, 8, LANES), everywhere, 0, 0, tiled=True)  11.3 us
    pallas_call x2, Pallas kernels, staged(): pl.pallas_call(kernel, out_shape=shapes, in_specs=[spec(HBM)] * len(opera...  8.11 us
    ppermute x3, waiting for transfers between devices, shifts(): lax.ppermute(block_up, axis, up)  6.16 us
    ppermute x3, waiting for transfers between devices, shifts(): lax.ppermute(block_down, axis, down)  5.43 us
  transfers between devices with their start and end apart: 7, of which 3 were waited for; matrix products, arithmetic and copies ran while one was open for 3% of the time, Pallas kernels for 5%

profile of v5, /device:TPU:1, one launch (start us, length us, event | category | flops | bytes accessed | tf_op | source)
XLA Modules:
  0.0 159.1 jit_solution(17852012569425025919)
XLA Ops:
  0.0 1.8 %shard_map.93.refs_4_ = f32[8,16,8,128]{3,2,1,0:T(8,128)} custom-call(f32[5,8,160]{2,1,0:T(8,128)} %bitcast.21), custom_call_target="tpu_custom_call" | custom-call | flops 100000 | bytes 600000 | tf_op jit(solution)/shard_map/pallas_call | solution.py:597
  1.8 5.6 %shard_map.92 = (f32[36,40,256]{2,1,0:T(8,128)}, f32[36,40,256]{2,1,0:T(8,128)}, f32[40,40,256]{2,1,0:T(8,128)}, f32[40,40,256]{2,1,0:T(8,128)}) custom-call(f32[40,40,256]{2,1,0:T(8,128)} %now.3, f32[40,40,256]{2,1,0:T(8,128)} %before.3), custom_call_target="tpu_custom_call" | custom-call | flops 1000 | bytes 9000000 | tf_op jit(solution)/shard_map/pallas_call | solution.py:575
  7.5 0.0 copy-start.8
  7.5 4.1 %collective-permute-start = (f32[36,40,256]{2,1,0:T(8,128)}, f32[36,40,256]{2,1,0:T(8,128)S(1)}, u32[]{:S(2)}, u32[]{:S(2)}) collective-permute-start(f32[36,40,256]{2,1,0:T(8,128)} %get-tuple-element.23), channel_id=1, source_target_pairs={{0,16},{16,32},{32,48},{48,64},{64,80},{80,96},{96,112},{1,17},{17... | collective-permute-start | bytes 4423688 | tf_op jit(solution)/shard_map/ppermute | solution.py:570
  11.7 1.3 collective-permute-start.1
  13.0 4.4 %collective-permute-start.2 = (f32[40,40,256]{2,1,0:T(8,128)}, f32[40,40,256]{2,1,0:T(8,128)}, u32[]{:S(2)}, u32[]{:S(2)}) collective-permute-start(f32[40,40,256]{2,1,0:T(8,128)} %get-tuple-element.25), channel_id=1, source_target_pairs={{0,1},{1,2},{2,3},{3,4},{4,5},{5,6},{6,7},{7,8},{8,9},{9,10},{10,1... | collective-permute-start | bytes 4915208 | tf_op jit(solution)/shard_map/ppermute | solution.py:570
  17.4 1.9 %collective-permute-start.3 = (f32[40,40,256]{2,1,0:T(8,128)}, f32[40,40,256]{2,1,0:T(8,128)}, u32[]{:S(2)}, u32[]{:S(2)}) collective-permute-start(f32[40,40,256]{2,1,0:T(8,128)} %get-tuple-element.26), channel_id=1, source_target_pairs={{1,0},{2,1},{3,2},{4,3},{5,4},{6,5},{7,6},{8,7},{9,8},{10,9},{11,1... | collective-permute-start | bytes 4915208 | tf_op jit(solution)/shard_map/ppermute | solution.py:570
  19.3 11.3 %all-to-all-start = ((f32[128,8,128]{2,1,0:T(8,128)}), f32[128,8,128]{2,1,0:T(8,128)S(1)}, u32[]{:S(2)}, u32[]{:S(2)}) async-start(f32[128,8,128]{2,1,0:T(8,128)} %bitcast.17), calls=%async_computation | async-start | bytes 1048576 | tf_op jit(solution)/shard_map/all_to_all | solution.py:605
  30.7 0.6 or_or_fusion.code_ref
  31.3 0.6 copy.16
  31.9 0.6 reshape.45.source_ref
  32.5 0.7 reshape.46.wavelet_ref
  33.2 3.2 %shard_map.91 = (s32[1024]{0:T(1024)}, s32[1]{0:T(128)}) custom-call(s32[1024]{0:T(1024)} %or_or_fusion.code_ref), custom_call_target="tpu_custom_call" | custom-call | flops 10000000 | bytes 20000000 | tf_op jit(solution)/shard_map/pallas_call | solution.py:608
  36.5 0.7 select_convert_fusion.z_ref
  37.2 0.6 select_convert_fusion.3.y_ref_c
  37.8 6.2 %collective-permute-done.x_low.refs_0_ = f32[36,40,256]{2,1,0:T(8,128)S(1)} collective-permute-done((f32[36,40,256]{2,1,0:T(8,128)}, f32[36,40,256]{2,1,0:T(8,128)S(1)}, u32[]{:S(2)}, u32[]{:S(2)}) %collective-permute-start) | collective-permute-done | bytes 1474592 | tf_op jit(solution)/shard_map/ppermute | solution.py:570
  43.9 5.4 %collective-permute-done.1.x_high.refs_1_ = f32[36,40,256]{2,1,0:T(8,128)S(1)} collective-permute-done((f32[36,40,256]{2,1,0:T(8,128)}, f32[36,40,256]{2,1,0:T(8,128)S(1)}, u32[]{:S(2)}, u32[]{:S(2)}) %collective-permute-start.1) | collective-permute-done | bytes 1474592 | tf_op jit(solution)/shard_map/ppermute | solution.py:570
  49.4 1.1 copy-done.3
  50.5 2.5 %shard_map.95 = (f32[80,8,256]{2,1,0:T(8,128)}, f32[80,8,256]{2,1,0:T(8,128)}) custom-call(f32[36,40,256]{2,1,0:T(8,128)} %copy-done.2, f32[36,40,256]{2,1,0:T(8,128)} %copy-done.3), custom_call_target="tpu_custom_call" | custom-call | flops 1000 | bytes 2000000 | tf_op jit(solution)/shard_map/pallas_call | solution.py:575
  53.0 7.4 %collective-permute-start.4 = (f32[80,8,256]{2,1,0:T(8,128)}, f32[80,8,256]{2,1,0:T(8,128)S(1)}, u32[]{:S(2)}, u32[]{:S(2)}) collective-permute-start(f32[80,8,256]{2,1,0:T(8,128)} %get-tuple-element.27), channel_id=1, source_target_pairs={{0,1},{1,2},{2,3},{3,4},{4,5},{5,6},{6,7},{7,8},{8,9},{9,10},{10,1... | collective-permute-start | bytes 1966088 | tf_op jit(solution)/shard_map/ppermute | solution.py:570
  60.4 1.9 %collective-permute-start.5 = (f32[80,8,256]{2,1,0:T(8,128)}, f32[80,8,256]{2,1,0:T(8,128)S(1)}, u32[]{:S(2)}, u32[]{:S(2)}) collective-permute-start(f32[80,8,256]{2,1,0:T(8,128)} %get-tuple-element.28), channel_id=1, source_target_pairs={{1,0},{2,1},{3,2},{4,3},{5,4},{6,5},{7,6},{8,7},{9,8},{10,9},{11,1... | collective-permute-start | bytes 1966088 | tf_op jit(solution)/shard_map/ppermute | solution.py:570
  62.4 0.1 pad_add_fusion.base_ref
  62.5 0.6 select_convert_fusion.2.y_ref_b
  63.1 0.7 select_convert_fusion.1.y_ref_a
  63.8 14.2 %all-to-all-done = f32[128,8,128]{2,1,0:T(8,128)S(1)} async-done(((f32[128,8,128]{2,1,0:T(8,128)}), f32[128,8,128]{2,1,0:T(8,128)S(1)}, u32[]{:S(2)}, u32[]{:S(2)}) %all-to-all-start) | async-done | bytes 524320 | tf_op jit(solution)/shard_map/all_to_all | solution.py:605
  78.0 2.7 %shard_map.96.refs_6_ = f32[20,2,96,128]{3,2,1,0:T(8,128)S(1)} custom-call(s32[2]{0:T(128)S(1)} %pad_add_fusion.base_ref, f32[8,16,8,128]{3,2,1,0:T(8,128)S(1)} %bitcast.16), custom_call_target="tpu_custom_call" | custom-call | flops 10000000 | bytes 10000000 | tf_op jit(solution)/shard_map/pallas_call | solution.py:628
  80.8 1.3 copy-done
  82.1 0.8 copy-done.4
  82.9 0.2 copy-done.5
  83.2 50.4 %shard_map.97 = f32[8,16,8,128]{3,2,1,0:T(8,128)} custom-call(s32[2]{0:T(128)} %copy-done.1, s32[12]{0:T(128)} %reshape.45.source_ref, f32[16]{0:T(128)} %reshape.46.wavelet_ref, s32[1024]{0:T(1024)} %get-tuple-element.17.own_ref, s32[1]{0:T(128)} %get-tuple-element.18.count_ref, f32[4096]{0:T(1024)} %bitcast.20, bf16[256,256]{1,0:T(8,128)(2,1)} %select_convert_fusion.z_ref, ...), custom_call_target="tpu_custom_call" | custom-call | flops 200000000 | bytes 30000000 | tf_op jit(solution)/shard_map/pallas_call | solution.py:642
  133.5 23.6 %all_to_all.10 = f32[128,8,128]{2,1,0:T(8,128)} all-to-all(f32[128,8,128]{2,1,0:T(8,128)} %bitcast.18), channel_id=1, replica_groups=mesh['gx'=8,'gy'=16] {'gx','gy'}, dimensions={0} | all-to-all | bytes 1048576 | tf_op jit(solution)/shard_map/all_to_all | solution.py:665
  157.2 1.9 %shard_map.98 = f32[5,8,160]{2,1,0:T(8,128)} custom-call(s32[2]{0:T(128)} %copy-done.1, f32[8,16,8,128]{3,2,1,0:T(8,128)} %bitcast.19), custom_call_target="tpu_custom_call" | custom-call | flops 100000 | bytes 600000 | tf_op jit(solution)/shard_map/pallas_call | solution.py:666
  (27 shorter events, 0.1 us)
Async XLA Ops:
  7.5 23.2 %copy-start.7 = (s32[3,1024]{1,0:T(4,128)S(1)}, s32[3,1024]{1,0:T(4,128)}, u32[]{:S(2)}) copy-start(s32[3,1024]{1,0:T(4,128)} %param.15) | copy-start | bytes 36868
  7.5 23.8 %copy-start.6 = (f32[4,1024]{1,0:T(4,128)S(1)}, f32[4,1024]{1,0:T(4,128)}, u32[]{:S(2)}) copy-start(f32[4,1024]{1,0:T(4,128)} %param.17) | copy-start | bytes 49156
  7.5 24.4 %copy-start.8 = (s32[3,4]{1,0:T(4,128)S(1)}, s32[3,4]{1,0:T(4,128)}, u32[]{:S(2)}) copy-start(s32[3,4]{1,0:T(4,128)} %param.14) | copy-start | bytes 148
  7.5 25.0 %copy-start.9 = (f32[4,4]{1,0:T(4,128)S(1)}, f32[4,4]{1,0:T(4,128)}, u32[]{:S(2)}) copy-start(f32[4,4]{1,0:T(4,128)} %param.16) | copy-start | bytes 196
  7.5 36.4 %collective-permute-start = (f32[36,40,256]{2,1,0:T(8,128)}, f32[36,40,256]{2,1,0:T(8,128)S(1)}, u32[]{:S(2)}, u32[]{:S(2)}) collective-permute-start(f32[36,40,256]{2,1,0:T(8,128)} %get-tuple-element.23), channel_id=1, source_target_pairs={{0,16},{16,32},{32,48},{48,64},{64,80},{80,96},{96,112},{1,17},{17... | collective-permute-start | bytes 4423688 | tf_op jit(solution)/shard_map/ppermute | solution.py:570
  11.7 37.7 %collective-permute-start.1 = (f32[36,40,256]{2,1,0:T(8,128)}, f32[36,40,256]{2,1,0:T(8,128)S(1)}, u32[]{:S(2)}, u32[]{:S(2)}) collective-permute-start(f32[36,40,256]{2,1,0:T(8,128)} %get-tuple-element.24), channel_id=1, source_target_pairs={{16,0},{32,16},{48,32},{64,48},{80,64},{96,80},{112,96},{17,1},{33... | collective-permute-start | bytes 4423688 | tf_op jit(solution)/shard_map/ppermute | solution.py:570
  13.0 69.1 %collective-permute-start.2 = (f32[40,40,256]{2,1,0:T(8,128)}, f32[40,40,256]{2,1,0:T(8,128)}, u32[]{:S(2)}, u32[]{:S(2)}) collective-permute-start(f32[40,40,256]{2,1,0:T(8,128)} %get-tuple-element.25), channel_id=1, source_target_pairs={{0,1},{1,2},{2,3},{3,4},{4,5},{5,6},{6,7},{7,8},{8,9},{9,10},{10,1... | collective-permute-start | bytes 4915208 | tf_op jit(solution)/shard_map/ppermute | solution.py:570
  17.4 64.7 %collective-permute-start.3 = (f32[40,40,256]{2,1,0:T(8,128)}, f32[40,40,256]{2,1,0:T(8,128)}, u32[]{:S(2)}, u32[]{:S(2)}) collective-permute-start(f32[40,40,256]{2,1,0:T(8,128)} %get-tuple-element.26), channel_id=1, source_target_pairs={{1,0},{2,1},{3,2},{4,3},{5,4},{6,5},{7,6},{8,7},{9,8},{10,9},{11,1... | collective-permute-start | bytes 4915208 | tf_op jit(solution)/shard_map/ppermute | solution.py:570
  19.3 58.7 %all-to-all-start = ((f32[128,8,128]{2,1,0:T(8,128)}), f32[128,8,128]{2,1,0:T(8,128)S(1)}, u32[]{:S(2)}, u32[]{:S(2)}) async-start(f32[128,8,128]{2,1,0:T(8,128)} %bitcast.17), calls=%async_computation | async-start | bytes 1048576 | tf_op jit(solution)/shard_map/all_to_all | solution.py:605
  43.9 5.4 %copy-start.2 = (f32[36,40,256]{2,1,0:T(8,128)}, f32[36,40,256]{2,1,0:T(8,128)S(1)}, u32[]{:S(2)}) copy-start(f32[36,40,256]{2,1,0:T(8,128)S(1)} %collective-permute-done.x_low.refs_0_) | copy-start | bytes 4423684
  49.4 1.1 copy-start.3
  53.0 29.1 %collective-permute-start.4 = (f32[80,8,256]{2,1,0:T(8,128)}, f32[80,8,256]{2,1,0:T(8,128)S(1)}, u32[]{:S(2)}, u32[]{:S(2)}) collective-permute-start(f32[80,8,256]{2,1,0:T(8,128)} %get-tuple-element.27), channel_id=1, source_target_pairs={{0,1},{1,2},{2,3},{3,4},{4,5},{5,6},{6,7},{7,8},{8,9},{9,10},{10,1... | collective-permute-start | bytes 1966088 | tf_op jit(solution)/shard_map/ppermute | solution.py:570
  60.4 21.6 %collective-permute-start.5 = (f32[80,8,256]{2,1,0:T(8,128)}, f32[80,8,256]{2,1,0:T(8,128)S(1)}, u32[]{:S(2)}, u32[]{:S(2)}) collective-permute-start(f32[80,8,256]{2,1,0:T(8,128)} %get-tuple-element.28), channel_id=1, source_target_pairs={{1,0},{2,1},{3,2},{4,3},{5,4},{6,5},{7,6},{8,7},{9,8},{10,9},{11,1... | collective-permute-start | bytes 1966088 | tf_op jit(solution)/shard_map/ppermute | solution.py:570
  62.5 19.6 %copy-start.1 = (s32[2]{0:T(128)}, s32[2]{0:T(128)S(1)}, u32[]{:S(2)}) copy-start(s32[2]{0:T(128)S(1)} %pad_add_fusion.base_ref) | copy-start | bytes 28
  80.7 1.3 copy-start
  82.1 0.8 copy-start.4
  82.1 1.1 copy-start.5
